TPU v7x, 256 devices: a whole 4x4x8 slice. The times are simulated.
256 devices in a mesh: grp: 8 (over z_hi, core), blk: 32 (over y, x, z_lo).
Axes of the slice: x: 4, y: 4, z: 8 (z_hi: 4, z_lo: 2; z = z_hi * 2 + z_lo), core: 2. Of those that a mesh axis runs over, the one named last changes fastest.
Arguments:
- integrals: bfloat16 [2, 5120, 20480], P(None, 'blk', 'grp'), may hold values from -0.59765625 to 0.59765625
- tiles: bfloat16 [1440, 128, 128], P('grp'), may hold values from -0.1875 to 0.1875
- tile_index: int32 [1440, 2], P('grp'), may hold values from 0 to 159, as said below
- vir_energy: float32 [5120], replicated, may hold values from 0.5 to 4
- occ_energy: float32 [1000], replicated, may hold values from -3 to -0.5
- pair_index: int32 [2], replicated, may hold values from 0 to 999
Outputs:
- density: bfloat16 [5120, 20480], P('blk', 'grp')
Inputs may be any that keep to these rules, and one draw needn't show every extreme that they name: tile_index[s, 1] is 0 or 1. Where it is 1, tile_index[s, 0] is c(s) + (s % 9) - 4; where it is 0, it is c(s). Every slot with (s % 9) == 4 is listed.
All inputs are finite; a program needn't handle non-finite values.
Results may differ from a plain program's by a relative error of at most 0.0057.
Values may be sent and summed in bfloat16 or wider, within the bound.
No kernel may reach another device: no remote copies, remote signals or barrier semaphores. Data moves between devices by JAX's collectives and lax.ppermute only.
A program may use at most 128 MiB of HBM per device.

v0:
```python
import jax
import jax.numpy as jnp
from jax import lax
from jax.sharding import PartitionSpec as P

TILE = 128
HB = 4


def extended_2(shard, sides, width):
    for axis, dim in sides:
        peers, length = (lax.axis_size(axis), shard.shape[dim])
        up = [(i, (i + 1) % peers) for i in range(peers - 1)]
        down = [(j, i) for i, j in up]
        last = lax.slice_in_dim(shard, length - width, length, axis=dim)
        leading = lax.slice_in_dim(shard, 0, width, axis=dim)
        before = lax.ppermute(last, axis, up)
        after = lax.ppermute(leading, axis, down)
        shard = jnp.concatenate([before, shard, after], axis=dim)
    return shard


def fit_window(window, group_tiles, group_list):
    band_width = 2 * HB + 1
    row_count = window.shape[0]
    column_count = group_tiles.shape[0] // band_width
    blocked = window.reshape(row_count, -1, TILE)
    flags = group_list[:, 1].astype(jnp.bfloat16)
    masked = group_tiles * flags[:, None, None]
    grouped = masked.reshape(column_count, band_width, TILE, TILE)
    total = jnp.zeros((row_count, column_count, TILE), jnp.float32)
    for offset in range(band_width):
        shifted = blocked[:, offset : offset + column_count, :]
        total = total + jnp.einsum(
            "xck,ckn->xcn", shifted, grouped[:, offset], preferred_element_type=jnp.float32
        )
    return total.reshape(row_count, column_count * TILE)


def local(integrals, tiles, tile_index, vir_energy, occ_energy, pair_index):
    block_index = lax.axis_index("blk")
    vir_block = integrals.shape[1]
    extended = extended_2(integrals, (("grp", 2),), HB * TILE)
    window = extended.reshape(2 * vir_block, -1)
    fitted = fit_window(window, tiles, tile_index).astype(jnp.bfloat16)
    fitted = fitted.reshape(2, vir_block, -1)
    own_rows = fitted[0]
    partner = fitted[1]
    partner_all = lax.all_gather(partner, "blk", axis=0, tiled=True)
    partial_value = lax.dot_general(
        own_rows, partner_all, (((1,), (1,)), ((), ())), preferred_element_type=jnp.float32
    )
    own_energy = lax.dynamic_slice_in_dim(vir_energy, block_index * vir_block, vir_block)
    occ_total = occ_energy[pair_index[0]] + occ_energy[pair_index[1]]
    pair_sum = lax.psum(partial_value, "grp")
    denominator = own_energy[:, None] + vir_energy[None, :] - occ_total
    amplitudes = (pair_sum / denominator).astype(jnp.bfloat16)
    density = jnp.dot(amplitudes, partner_all, preferred_element_type=jnp.float32)
    return density.astype(jnp.bfloat16)


def solution(mesh):
    in_specs = (P(None, "blk", "grp"), P("grp", None, None), P("grp", None), P(), P(), P())
    out_specs = P("blk", "grp")
    return jax.shard_map(local, mesh=mesh, in_specs=in_specs, out_specs=out_specs, check_vma=False)
```

profile of v0, /device:TPU:1, one launch (start us, length us, event | category | flops | bytes accessed | tf_op | source)
XLA Modules:
  0.0 762.8 jit_solution(11789187877359115350)
XLA Ops:
  6.5 0.0 all-gather.2.cloned.1.call-start
  6.5 1.1 fusion.28
  7.7 5.1 collective-permute-start.1
  12.8 3.1 collective-permute-start
  15.9 0.7 fusion.26
  16.6 5.8 broadcast_multiply_fusion
  22.4 0.0 collective-permute-done.1
  22.4 0.0 collective-permute-done
  22.4 0.0 copy-done.6
  22.4 1.6 pad_maximum_fusion
  24.0 3.8 reshape_reshape.3
  27.8 6.5 fusion.27
  34.3 1.8 fusion.1
  36.1 0.0 copy-start.5
  36.1 0.0 slice-start.1
  36.1 1.8 fusion.3
  37.9 0.0 copy-start.4
  37.9 0.0 copy-done.5
  37.9 1.8 fusion.5
  39.8 0.0 copy-start.3
  39.8 0.0 slice-done
  39.8 0.0 slice-done.1
  39.8 0.0 copy-done.4
  39.8 0.6 fusion.7
  40.4 0.0 copy-start.2
  40.4 0.9 copy-done.3
  41.3 2.2 fusion.9
  43.6 0.0 copy-done.2
  43.6 2.3 fusion.11
  45.9 0.0 copy-done.1
  45.9 2.3 fusion.15
  48.2 0.0 copy-done
  48.2 2.4 fusion.13
  50.5 8.6 %fusion.20 = bf16[320,20,128]{2,0,1:T(8,128)(2,1)} fusion(bf16[320,20,128]{2,1,0:T(8,128)(2,1)} %get-tuple-element.13, f32[20,128,320]{1,2,0:T(8,128)S(1)} %fusion.1, f32[20,128,320]{1,2,0:T(8,128)S(1)} %fusion.3, f32[20,128,320]{1,2,0:T(8,128)S(1)} %fusion.5, f32[20,128,320]{1,2,0:T(8,128)S(1)} %fusion.7, f32[20,128,320]{1,2,0:T(8,128)} %fusion.9, ...), kind=kOutput, calls=%fused_computation.25 | convolution fusion | flops 217088000 | bytes 30146560 | tf_op jit(solution)/shard_map/xck,ckn->xcn/dot_general | solution.py:34
  59.1 1.5 slice_bitcast_fusion.1
  60.6 1.0 copy.72
  61.6 0.0 all-gather.2.cloned.1.call-update
  61.7 0.2 all-reduce.2.cloned.1.call-start
  61.9 565.9 %all-gather.2.cloned.1.call-done = bf16[5120,2560]{1,0:T(8,128)(2,1)} async-done(((bf16[160,2560]{1,0:T(8,128)(2,1)}), bf16[5120,2560]{1,0:T(8,128)(2,1)}) %all-gather.2.cloned.1.call-update) | async-done | bytes 26214416 | tf_op jit(solution)/shard_map/all_gather | solution.py:49
  627.8 15.2 %fusion.23 = f32[160,5120]{1,0:T(8,128)} fusion(bf16[5120,2560]{1,0:T(8,128)(2,1)} %all-gather.2.cloned.1.call-done, bf16[20,20,8,128]{3,2,1,0:T(8,128)(2,1)S(1)} %get-tuple-element.14), kind=kOutput, calls=%fused_computation.27 | convolution fusion | flops 4194304000 | bytes 30310400 | tf_op jit(solution)/shard_map/dot_general | solution.py:50
  643.0 0.0 all-reduce.2.cloned.1.call-update
  643.0 0.6 copy-done.7
  643.6 0.6 fusion.30
  648.0 1.4 fusion.29
  650.6 0.0 copy-done.8
  650.6 0.1 dynamic_slice.9
  650.7 90.5 %all-reduce.2.cloned.1.call-done = f32[160,5120]{1,0:T(8,128)} async-done(((f32[160,5120]{1,0:T(8,128)}), f32[160,5120]{1,0:T(8,128)}) %all-reduce.2.cloned.1.call-update) | async-done | bytes 3276816 | tf_op jit(solution)/shard_map/psum | solution.py:55
  741.2 14.8 %convolution_convert_fusion = bf16[160,2560]{1,0:T(8,128)(2,1)} fusion(bf16[5120,2560]{1,0:T(8,128)(2,1)} %all-gather.2.cloned.1.call-done, f32[160,5120]{1,0:T(8,128)} %all-reduce.2.cloned.1.call-done, f32[]{:T(128)} %bitcast.13, f32[5120]{0:T(1024)S(1)} %copy-done.8, f32[160]{0:T(256)S(1)} %dynamic_slice.9), kind=kOutput, calls=%fused_computation | convolution fusion | flops 4197990400 | bytes 30331524 | tf_op jit(solution)/shard_map/dot_general | solution.py:58
  (7 shorter events, 0.0 us)
Async XLA Ops:
  6.5 621.3 %all-gather.2.cloned.1.call-start = ((), (), s32[]{:S(2)}) async-start(), calls=%async_computation | async-start | bytes 27033600 | tf_op jit(solution)/shard_map/all_gather | solution.py:49
  7.7 14.7 %collective-permute-start.1 = (bf16[2,160,512]{2,1,0:T(8,128)(2,1)S(1)}, bf16[2,160,512]{2,1,0:T(8,128)(2,1)S(1)}, u32[]{:S(2)}, u32[]{:S(2)}) collective-permute-start(bf16[2,160,512]{2,1,0:T(8,128)(2,1)S(1)} %get-tuple-element.17), channel_id=1, source_target_pairs={{32,0},{64,32},{96,64},{128,96},{160,128},{192,160},{224,192},{33,... | collective-permute-start | bytes 983048 | tf_op jit(solution)/shard_map/ppermute | solution.py:18
  12.8 9.6 %collective-permute-start = (bf16[2,160,512]{2,1,0:T(8,128)(2,1)S(1)}, bf16[2,160,512]{2,1,0:T(8,128)(2,1)S(1)}, u32[]{:S(2)}, u32[]{:S(2)}) collective-permute-start(bf16[2,160,512]{2,1,0:T(8,128)(2,1)S(1)} %get-tuple-element.16), channel_id=1, source_target_pairs={{0,32},{32,64},{64,96},{96,128},{128,160},{160,192},{192,224},{1,3... | collective-permute-start | bytes 983048 | tf_op jit(solution)/shard_map/ppermute | solution.py:17
  16.6 5.8 copy-start.6
  34.3 5.5 slice-start
  36.1 1.9 copy-start.5
  36.1 3.7 slice-start.1
  37.9 1.9 copy-start.4
  39.8 1.6 copy-start.3
  40.4 3.2 copy-start.2
  43.6 2.3 copy-start.1
  45.9 2.3 copy-start
  61.7 679.5 %all-reduce.2.cloned.1.call-start = ((), (), s32[]{:S(2)}) async-start(), calls=%async_computation.1 | async-start | bytes 6553600 | tf_op jit(solution)/shard_map/psum | solution.py:55
  643.0 0.7 copy-start.7
  643.0 7.6 %copy-start.8 = (f32[5120]{0:T(1024)S(1)}, f32[5120]{0:T(1024)}, u32[]{:S(2)}) copy-start(f32[5120]{0:T(1024)} %param.9) | copy-start | bytes 61444
Sparse Core Ops, SparseCore 0:
  61.8 565.9 all-gather.1
  643.1 98.0 all-reduce.1
where the time goes:
time: 763 us
  waiting for transfers between devices  656 us (86%)
  matrix products  53.8 us (7%)
  between operations  18.6 us (2%)
  local copies, waits for them, and re-layouts  17.6 us (2%)
  starting transfers between devices  8.43 us (1%)
  other arithmetic  8.05 us (1%)
    all_gather x1, waiting for transfers between devices, local(): partner_all = lax.all_gather(partner, 'blk', axis=0, tiled=True)  566 us
    psum x1, waiting for transfers between devices, local(): pair_sum = lax.psum(partial_value, 'grp')  90.5 us
    dot_general x9, matrix products, fit_window(): jnp.einsum('xck,ckn->xcn', shifted, grouped[:, offset], preferred_element...  23.8 us
  transfers between devices with their start and end apart: 4, of which 2 were waited for; matrix products, arithmetic and copies ran while one was open for 1% of the time, Pallas kernels for 0%

commit v1 on v0

v1 whole, which is shorter than its diff:
```python
import functools

import jax
import jax.numpy as jnp
from jax import lax
from jax.experimental import pallas as pl
from jax.experimental.pallas import tpu as pltpu
from jax.sharding import PartitionSpec as P

TILE = 128
HB = 4
BAND = 2 * HB + 1
ROWS = 160
AUX = 2560
HALO = HB * TILE
bf16 = jnp.bfloat16
f32 = jnp.float32
MIB = 1 << 20


def blk_index(y, x, z):
    return ((y % 4) * 4 + x) * 2 + z


PLACES = [(y, x, z) for y in range(4) for x in range(4) for z in range(2)]
OUTER = (3, 2, 1, 0)


def send_y(v, step):
    pairs = [(blk_index(y, x, z), blk_index(y + step, x, z)) for y, x, z in PLACES]
    return lax.ppermute(v, "blk", pairs)


def send_outer(v):
    pairs = [(blk_index(y, x, z), blk_index(y, OUTER[x], z)) for y, x, z in PLACES]
    return lax.ppermute(v, "blk", pairs)


def send_inner(v):
    pairs = [(blk_index(y, x, z), blk_index(y, x ^ 1, z)) for y, x, z in PLACES]
    return lax.ppermute(v, "blk", pairs)


def send_z(v):
    pairs = [(blk_index(y, x, z), blk_index(y, x, 1 - z)) for y, x, z in PLACES]
    return lax.ppermute(v, "blk", pairs)


def send_core(v):
    return lax.ppermute(v, "grp", [(g, g ^ 1) for g in range(8)])


def send_high(v, step):
    return lax.ppermute(v, "grp", [(g, (g + 2 * step) % 8) for g in range(8)])


def params(mib, **kw):
    return pltpu.CompilerParams(vmem_limit_bytes=mib * MIB, **kw)


def cost(flops, nbytes):
    return pl.CostEstimate(flops=int(flops), bytes_accessed=int(nbytes), transcendentals=0)


def fit_kernel(index_ref, left, own, right, tiles, out_a, out_b, ext, weights):
    p = pl.program_id(0)

    @pl.when(p == 0)
    def _():
        ext[:, :HALO] = left[...]
        ext[:, HALO : HALO + AUX] = own[...]
        ext[:, HALO + AUX :] = right[...]
        weights[...] = jnp.zeros_like(weights)

    for q in range(2):
        for o in range(BAND):
            slot = q * BAND + o
            listed = index_ref[1, p * (2 * BAND) + slot] == 1
            tile = tiles[slot]
            j = q + o
            weights[j * TILE : (j + 1) * TILE, q * TILE : (q + 1) * TILE] = jnp.where(
                listed, tile, jnp.zeros_like(tile)
            )
    window = ext[:, pl.ds(pl.multiple_of(p * (2 * TILE), 2 * TILE), (BAND + 1) * TILE)]
    fitted = jnp.dot(window, weights[...], preferred_element_type=f32).astype(bf16)
    out_a[...] = fitted[:ROWS]
    out_b[...] = fitted[ROWS:]


def fit(left, own, right, tiles, index):
    whole = lambda shape: pl.BlockSpec(shape, lambda p, i: (0, 0))
    grid_spec = pltpu.PrefetchScalarGridSpec(
        num_scalar_prefetch=1,
        grid=(10,),
        in_specs=[
            whole((2 * ROWS, HALO)),
            whole((2 * ROWS, AUX)),
            whole((2 * ROWS, HALO)),
            pl.BlockSpec((2 * BAND, TILE, TILE), lambda p, i: (p, 0, 0)),
        ],
        out_specs=[pl.BlockSpec((ROWS, 2 * TILE), lambda p, i: (0, p))] * 2,
        scratch_shapes=[
            pltpu.VMEM((2 * ROWS, AUX + 2 * HALO), bf16),
            pltpu.VMEM(((BAND + 1) * TILE, 2 * TILE), bf16),
        ],
    )
    return pl.pallas_call(
        fit_kernel,
        grid_spec=grid_spec,
        out_shape=[jax.ShapeDtypeStruct((ROWS, AUX), bf16)] * 2,
        compiler_params=params(32),
        cost_estimate=cost(2.1e9, 10e6),
        name="fit",
    )(index, left, own, right, tiles)


def pair_kernel(core_ref, *refs, steps):
    a0, ax, az, d1, d2 = refs[:5]
    bs = refs[5:-5]
    keep, send, acc, acat, bcat = refs[-5:]
    k = pl.program_id(0)
    core = core_ref[0]
    first = pl.multiple_of(core * (2 * ROWS), 2 * ROWS)
    second = pl.multiple_of((1 - core) * (2 * ROWS), 2 * ROWS)
    acat[pl.ds(first, ROWS)] = a0[...]
    acat[pl.ds(first + ROWS, ROWS)] = ax[...]
    acat[pl.ds(second, ROWS)] = az[...]
    acat[pl.ds(second + ROWS, ROWS // 2)] = d1[...]
    acat[pl.ds(second + ROWS + ROWS // 2, ROWS // 2)] = d2[...]
    at = 0
    for b in bs:
        bcat[at : at + b.shape[0]] = b[...]
        at += b.shape[0]
    product = lax.dot_general(
        acat[...], bcat[...], (((1,), (1,)), ((), ())), preferred_element_type=f32
    )

    @pl.when(k == 0)
    def _():
        acc[...] = product

    @pl.when(k > 0)
    def _():
        acc[...] += product

    @pl.when(k == steps - 1)
    def _():
        keep[...] = acc[: 2 * ROWS]
        send[...] = acc[2 * ROWS :].astype(bf16)


def pair(core, a_parts, b_parts):
    width = sum(b.shape[0] for b in b_parts)
    chunk = 512
    steps = AUX // chunk
    spec = lambda rows: pl.BlockSpec((rows, chunk), lambda k, c: (0, k))
    grid_spec = pltpu.PrefetchScalarGridSpec(
        num_scalar_prefetch=1,
        grid=(steps,),
        in_specs=[spec(v.shape[0]) for v in (*a_parts, *b_parts)],
        out_specs=[pl.BlockSpec((2 * ROWS, width), lambda k, c: (0, 0))] * 2,
        scratch_shapes=[
            pltpu.VMEM((4 * ROWS, width), f32),
            pltpu.VMEM((4 * ROWS, chunk), bf16),
            pltpu.VMEM((width, chunk), bf16),
        ],
    )
    return pl.pallas_call(
        functools.partial(pair_kernel, steps=steps),
        grid_spec=grid_spec,
        out_shape=[
            jax.ShapeDtypeStruct((2 * ROWS, width), f32),
            jax.ShapeDtypeStruct((2 * ROWS, width), bf16),
        ],
        compiler_params=params(32),
        cost_estimate=cost(2 * 4 * ROWS * width * AUX, 2 * (4 * ROWS + width) * AUX),
        name="pair",
    )(core, *a_parts, *b_parts)


SHARE = ROWS // 2


def core_sum_kernel(high_ref, keep, got, own, s1, s2, s3):
    high = high_ref[0]
    for step, out in enumerate((own, s1, s2, s3)):
        at = pl.multiple_of(((high + step) % 4) * SHARE, SHARE)
        value = keep[pl.ds(at, SHARE)] + got[pl.ds(at, SHARE)].astype(f32)
        out[...] = value.astype(out.dtype)


def core_sum(high, keep, got):
    width = keep.shape[1]
    vmem = pl.BlockSpec(memory_space=pltpu.VMEM)
    return pl.pallas_call(
        core_sum_kernel,
        in_specs=[pl.BlockSpec(memory_space=pltpu.SMEM), vmem, vmem],
        out_specs=[vmem] * 4,
        out_shape=[jax.ShapeDtypeStruct((SHARE, width), f32)]
        + [jax.ShapeDtypeStruct((SHARE, width), bf16)] * 3,
        compiler_params=params(16),
        cost_estimate=cost(1e6, 3e6),
        name="core_sum",
    )(high, keep, got)


def amplitude(own, received, row_energy, column_energy, occ_total):
    total = own
    for r in received:
        total = total + r.astype(f32)
    denominator = (row_energy[:, None] + column_energy[None, :]) - occ_total
    return (total / denominator).astype(bf16)


def density_kernel(place_ref, *refs, n_b, blocks, halves):
    shares = refs[:4]
    bs = refs[4 : 4 + n_b]
    outs = refs[4 + n_b : -2]
    tcat, bcat = refs[-2:]
    core = place_ref[0]
    high = place_ref[1]

    @pl.when(pl.program_id(0) == 0)
    def _():
        for piece in range(2):
            mine, other = shares[2 * piece], shares[2 * piece + 1]
            columns = slice(piece * 4 * ROWS, (piece + 1) * 4 * ROWS)
            for k in range(4):
                at = ((high - k + 4) % 4) * SHARE
                here = pl.multiple_of(core * (2 * ROWS) + at, SHARE)
                there = pl.multiple_of((1 - core) * (2 * ROWS) + at, SHARE)
                tcat[pl.ds(here, SHARE), columns] = mine[k * SHARE : (k + 1) * SHARE]
                tcat[pl.ds(there, SHARE), columns] = other[k * SHARE : (k + 1) * SHARE]

    at = 0
    for b in bs:
        bcat[at : at + b.shape[0]] = b[...]
        at += b.shape[0]
    first, last = blocks
    value = jnp.dot(
        tcat[first * ROWS : last * ROWS], bcat[...], preferred_element_type=f32
    )
    for i, out in enumerate(outs):
        rows = ROWS // 2 if halves else ROWS
        out[...] = value[i * rows : (i + 1) * rows].astype(out.dtype)


def density(place, shares, b_parts, blocks, halves, types):
    chunk = 512
    steps = AUX // chunk
    rows = ROWS // 2 if halves else ROWS
    whole = pl.BlockSpec((2 * ROWS, 4 * ROWS), lambda k, c: (0, 0))
    grid_spec = pltpu.PrefetchScalarGridSpec(
        num_scalar_prefetch=1,
        grid=(steps,),
        in_specs=[whole] * 4
        + [pl.BlockSpec((v.shape[0], chunk), lambda k, c: (0, k)) for v in b_parts],
        out_specs=[pl.BlockSpec((rows, chunk), lambda k, c: (0, k)) for _ in types],
        scratch_shapes=[
            pltpu.VMEM((4 * ROWS, 8 * ROWS), bf16),
            pltpu.VMEM((8 * ROWS, chunk), bf16),
        ],
    )
    n = blocks[1] - blocks[0]
    return pl.pallas_call(
        functools.partial(
            density_kernel, n_b=len(b_parts), blocks=blocks, halves=halves
        ),
        grid_spec=grid_spec,
        out_shape=[jax.ShapeDtypeStruct((rows, AUX), t) for t in types],
        compiler_params=params(32),
        cost_estimate=cost(2 * n * ROWS * 8 * ROWS * AUX, 2 * 8 * ROWS * AUX),
        name="density",
    )(place, *shares, *b_parts)


def local(integrals, tiles, tile_index, vir_energy, occ_energy, pair_index):
    group = lax.axis_index("grp").astype(jnp.int32)
    me = lax.axis_index("blk").astype(jnp.int32)
    high, core = group // 2, group % 2
    y, x, z = me // 8, (me // 2) % 4, me % 2
    place = jnp.stack([core, high])

    window = integrals.reshape(2 * ROWS, AUX)
    up = [(g, g + 1) for g in range(7)]
    down = [(g + 1, g) for g in range(7)]
    left = lax.ppermute(window[:, AUX - HALO :], "grp", up)
    right = lax.ppermute(window[:, :HALO], "grp", down)
    a, b = fit(left, window, right, tiles, tile_index.T)

    bm = send_y(b, 1)
    bp = send_y(b, -1)
    bo = send_outer(b)
    ax = send_inner(a)
    az = send_z(a)
    half = ROWS // 2
    d1 = send_inner(az[:half])
    d2 = send_z(ax[half:])
    a_parts = (a, ax, az, d1, d2)
    bom = send_y(bo, 1)
    b2 = send_y(bp, -1)
    bop = send_outer(bp)
    c1 = send_outer(b2[:64])
    c2 = send_y(bom[64:112], 1)
    c3 = send_y(bop[112:], -1)
    pieces = ((b, bm, bp, bo), (bom, b2, bop, c1, c2, c3))

    ox = jnp.asarray(OUTER, jnp.int32)[x]
    index = lambda yy, xx, zz: ((yy % 4) * 4 + xx) * 2 + zz
    energy = lambda at, n: lax.dynamic_slice_in_dim(vir_energy, at, n)
    columns = (
        (index(y, x, z), index(y + 3, x, z), index(y + 1, x, z), index(y, ox, z)),
        (index(y + 3, ox, z), index(y + 2, x, z), index(y + 1, ox, z), index(y + 2, ox, z)),
    )
    row_x = jnp.where(high < 2, x, x ^ 1)
    row_z = jnp.where(core == 0, z, 1 - z)
    row_energy = energy(index(y, row_x, row_z) * ROWS + (high % 2) * half, half)
    occ_total = occ_energy[pair_index[0]] + occ_energy[pair_index[1]]

    shares = []
    for parts, places in zip(pieces, columns):
        keep, send = pair(core[None], a_parts, parts)
        own, s1, s2, s3 = core_sum(high[None], keep, send_core(send))
        received = [send_high(s1, 1), send_high(s2, 2), send_high(s3, 3)]
        column_energy = jnp.concatenate([energy(p * ROWS, ROWS) for p in places])
        mine = amplitude(own, received, row_energy, column_energy, occ_total)
        mine = jnp.concatenate([mine] + [send_high(mine, k) for k in (1, 2, 3)], axis=0)
        shares += [mine, send_core(mine)]

    b_parts = (*pieces[0], *pieces[1])
    dense = functools.partial(density, place, shares, b_parts)
    to_d1, to_d2 = dense((3, 4), True, (bf16, bf16))
    x1, x2, z1, z2 = dense((1, 3), True, (bf16, f32, f32, bf16))
    o1, o2 = dense((0, 1), True, (f32, f32))
    from_x = send_inner(to_d1)
    from_z = send_z(to_d2)
    got_x1 = send_inner(x1)
    got_z2 = send_z(z2)
    got_z1 = send_z((z1 + from_x.astype(f32)).astype(bf16))
    got_x2 = send_inner((x2 + from_z.astype(f32)).astype(bf16))
    h1 = o1 + got_x1.astype(f32) + got_z1.astype(f32)
    h2 = o2 + got_x2.astype(f32) + got_z2.astype(f32)
    return jnp.concatenate([h1, h2], axis=0).astype(bf16)


def solution(mesh):
    in_specs = (P(None, "blk", "grp"), P("grp", None, None), P("grp", None), P(), P(), P())
    return jax.shard_map(
        local, mesh=mesh, in_specs=in_specs, out_specs=P("blk", "grp"), check_vma=False
    )
```

time: 763 us -> 224 us (0.29)
  waiting for transfers between devices: 656 us -> 81.8 us
  starting transfers between devices: 8.43 us -> 68 us
  matrix products: 53.8 us -> 0 us
  Pallas kernels: 0 us -> 36.1 us
  between operations: 18.6 us -> 7.56 us
  local copies, waits for them, and re-layouts: 17.6 us -> 26.6 us
    all_gather x1 -> x0, waiting for transfers between devices: 566 us -> none  [local(): partner_all = lax.all_gather(partner, 'blk', axis=0, tiled=True)]
    psum x1 -> x0, waiting for transfers between devices: 90.5 us -> none  [local(): pair_sum = lax.psum(partial_value, 'grp')]
    ppermute x2 -> x37, waiting for transfers between devices: 0.01 us -> 81.8 us  [the longest x6 29 us: send_y(): return lax.ppermute(v, 'blk', pairs)]
    ppermute x2 -> x37, starting transfers between devices: 8.21 us -> 68 us  [the longest x12 38.8 us: send_high(): return lax.ppermute(v, 'grp', [(g, (g + 2 * step) % 8) for g in range(8)])]
    dot_general x11 -> x0, matrix products: 53.8 us -> none  [the longest x9 23.8 us: fit_window(): jnp.einsum('xck,ckn->xcn', shifted, grouped[:, offset], preferred_element...]
    pallas_call x0 -> x8, Pallas kernels: none -> 36.1 us  [the longest x3 15.2 us: density(): pl.pallas_call(functools.partial(density_kernel, n_b=len(b_parts), blocks...]
    unnamed x23 -> x50, local copies, waits for them, and re-layouts: 3.1 us -> 17.3 us
  transfers between devices with their start and end apart: 4 -> 37, of which waited for: 2 -> 16; matrix products, arithmetic and copies ran while one was open for 1% -> 4% of each run, Pallas kernels for 0% -> 12%
where the time goes in v1:
time: 224 us; the launch traced here: 222 us
  waiting for transfers between devices  81.8 us (37%)
  starting transfers between devices  68 us (30%)
  Pallas kernels  36.1 us (16%)
  local copies, waits for them, and re-layouts  26.6 us (12%)
  between operations  7.56 us (3%)
    ppermute x12, starting transfers between devices, send_high(): return lax.ppermute(v, 'grp', [(g, (g + 2 * step) % 8) for g in range(8)])  38.8 us
    ppermute x6, waiting for transfers between devices, send_y(): return lax.ppermute(v, 'blk', pairs)  29 us
    ppermute x5, waiting for transfers between devices, send_z(): return lax.ppermute(v, 'blk', pairs)  18.6 us
    ppermute x12, waiting for transfers between devices, send_high(): return lax.ppermute(v, 'grp', [(g, (g + 2 * step) % 8) for g in range(8)])  18.2 us
    unnamed x50, local copies, waits for them, and re-layouts  17.3 us
    pallas_call x3, Pallas kernels, density(): pl.pallas_call(functools.partial(density_kernel, n_b=len(b_parts), blocks...  15.2 us
    pallas_call x2, Pallas kernels, pair(): pl.pallas_call(functools.partial(pair_kernel, steps=steps), grid_spec=gri...  13.1 us
    ppermute x1, waiting for transfers between devices, local(): right = lax.ppermute(window[:, :HALO], 'grp', down)  8.76 us
  transfers between devices with their start and end apart: 37, of which 16 were waited for; matrix products, arithmetic and copies ran while one was open for 4% of the time, Pallas kernels for 12%

profile of v1, /device:TPU:1, one launch (start us, length us, event | category | flops | bytes accessed | tf_op | source)
XLA Modules:
  0.0 222.0 jit_solution(13581583539989669573)
XLA Ops:
  1.1 6.3 %collective-permute-start = (bf16[320,512]{1,0:T(8,128)(2,1)S(1)}, bf16[320,512]{1,0:T(8,128)(2,1)S(1)}, u32[]{:S(2)}, u32[]{:S(2)}) collective-permute-start(bf16[320,512]{1,0:T(8,128)(2,1)S(1)} %get-tuple-element.50), channel_id=1, source_target_pairs={{0,32},{32,64},{64,96},{96,128},{128,160},{160,192},{192,224},{1,3... | collective-permute-start | bytes 983048 | tf_op jit(solution)/shard_map/ppermute | solution.py:287
  7.4 1.9 collective-permute-start.1
  9.3 2.1 collective-permute-done.left
  11.5 8.8 %collective-permute-done.1.right = bf16[320,512]{1,0:T(8,128)(2,1)S(1)} collective-permute-done((bf16[320,512]{1,0:T(8,128)(2,1)S(1)}, bf16[320,512]{1,0:T(8,128)(2,1)S(1)}, u32[]{:S(2)}, u32[]{:S(2)}) %collective-permute-start.1) | collective-permute-done | bytes 327712 | tf_op jit(solution)/shard_map/ppermute | solution.py:288
  20.2 2.7 %copy-done.9 = bf16[180,128,128]{2,1,0:T(8,128)(2,1)S(1)} copy-done((bf16[180,128,128]{2,1,0:T(8,128)(2,1)S(1)}, bf16[180,128,128]{2,1,0:T(8,128)(2,1)}, u32[]{:S(2)}) %copy-start.9) | copy-done | bytes 5898264
  22.9 1.4 copy-done.10
  25.0 5.7 %fit.1 = (bf16[160,2560]{1,0:T(8,128)(2,1)S(1)}, bf16[160,2560]{1,0:T(8,128)(2,1)S(1)}) custom-call(s32[2,180]{1,0:T(2,128)S(1)} %bitcast.10, bf16[320,512]{1,0:T(8,128)(2,1)S(1)} %collective-permute-done.left, bf16[320,2560]{1,0:T(8,128)(2,1)S(1)} %bitcast.9, bf16[320,512]{1,0:T(8,128)(2,1)S(1)} %collective-permute-done.1.right, ...), custom_call_target="tpu_custom_call" | custom-call | flops 2100000000 | bytes 10000000 | tf_op jit(solution)/shard_map/fit/pallas_call | solution.py:107
  30.7 2.8 %collective-permute-start.7 = (bf16[160,2560]{1,0:T(8,128)(2,1)S(1)}, bf16[160,2560]{1,0:T(8,128)(2,1)S(1)}, u32[]{:S(2)}, u32[]{:S(2)}) collective-permute-start(bf16[160,2560]{1,0:T(8,128)(2,1)S(1)} %get-tuple-element.28.refs_5_.refs_4_), channel_id=1, source_target_pairs={{0,24},{1,25},{2,26},{3,27},{4,28},{5,29},{6,30},{7,31},{8,0},{9,1... | collective-permute-start | bytes 2457608 | tf_op jit(solution)/shard_map/ppermute | solution.py:31
  33.5 2.5 %collective-permute-start.8 = (bf16[160,2560]{1,0:T(8,128)(2,1)S(1)}, bf16[160,2560]{1,0:T(8,128)(2,1)S(1)}, u32[]{:S(2)}, u32[]{:S(2)}) collective-permute-start(bf16[160,2560]{1,0:T(8,128)(2,1)S(1)} %get-tuple-element.28.refs_5_.refs_4_), channel_id=1, source_target_pairs={{0,6},{1,7},{2,4},{3,5},{4,2},{5,3},{6,0},{7,1},{8,14},{9,15},{10,... | collective-permute-start | bytes 2457608 | tf_op jit(solution)/shard_map/ppermute | solution.py:36
  36.9 10.0 %collective-permute-done.7.refs_7_.refs_6_ = bf16[160,2560]{1,0:T(8,128)(2,1)S(1)} collective-permute-done((bf16[160,2560]{1,0:T(8,128)(2,1)S(1)}, bf16[160,2560]{1,0:T(8,128)(2,1)S(1)}, u32[]{:S(2)}, u32[]{:S(2)}) %collective-permute-start.7) | collective-permute-done | bytes 819232 | tf_op jit(solution)/shard_map/ppermute | solution.py:31
  46.9 3.3 %collective-permute-start.18 = (bf16[160,2560]{1,0:T(8,128)(2,1)S(1)}, bf16[160,2560]{1,0:T(8,128)(2,1)S(1)}, u32[]{:S(2)}, u32[]{:S(2)}) collective-permute-start(bf16[160,2560]{1,0:T(8,128)(2,1)S(1)} %collective-permute-done.7.refs_7_.refs_6_), channel_id=1, source_target_pairs={{0,24},{1,25},{2,26},{3,27},{4,28},{5,29},{6,30},{7,31},{8,0},{9,1... | collective-permute-start | bytes 2457608 | tf_op jit(solution)/shard_map/ppermute | solution.py:31
  50.2 2.5 %collective-permute-start.19 = (bf16[160,2560]{1,0:T(8,128)(2,1)S(1)}, bf16[160,2560]{1,0:T(8,128)(2,1)S(1)}, u32[]{:S(2)}, u32[]{:S(2)}) collective-permute-start(bf16[160,2560]{1,0:T(8,128)(2,1)S(1)} %collective-permute-done.7.refs_7_.refs_6_), channel_id=1, source_target_pairs={{0,6},{1,7},{2,4},{3,5},{4,2},{5,3},{6,0},{7,1},{8,14},{9,15},{10,... | collective-permute-start | bytes 2457608 | tf_op jit(solution)/shard_map/ppermute | solution.py:36
  55.4 5.0 %collective-permute-done.18.refs_6_.refs_9_ = bf16[160,2560]{1,0:T(8,128)(2,1)S(1)} collective-permute-done((bf16[160,2560]{1,0:T(8,128)(2,1)S(1)}, bf16[160,2560]{1,0:T(8,128)(2,1)S(1)}, u32[]{:S(2)}, u32[]{:S(2)}) %collective-permute-start.18) | collective-permute-done | bytes 819232 | tf_op jit(solution)/shard_map/ppermute | solution.py:31
  60.4 1.6 collective-permute-start.5
  62.7 2.0 collective-permute-done.19.refs_7_.refs_10_
  64.7 2.5 %collective-permute-start.20 = (bf16[64,2560]{1,0:T(8,128)(2,1)}, bf16[64,2560]{1,0:T(8,128)(2,1)}, u32[]{:S(2)}, u32[]{:S(2)}) collective-permute-start(bf16[64,2560]{1,0:T(8,128)(2,1)} %slice.40), channel_id=1, source_target_pairs={{0,6},{1,7},{2,4},{3,5},{4,2},{5,3},{6,0},{7,1},{8,14},{9,15},{10,... | collective-permute-start | bytes 983048 | tf_op jit(solution)/shard_map/ppermute | solution.py:36
  67.9 3.4 %collective-permute-done.17.refs_5_.refs_8_ = bf16[160,2560]{1,0:T(8,128)(2,1)S(1)} collective-permute-done((bf16[160,2560]{1,0:T(8,128)(2,1)S(1)}, bf16[160,2560]{1,0:T(8,128)(2,1)S(1)}, u32[]{:S(2)}, u32[]{:S(2)}) %collective-permute-start.17) | collective-permute-done | bytes 819232 | tf_op jit(solution)/shard_map/ppermute | solution.py:31
  72.0 10.7 %collective-permute-done.6.refs_6_.refs_5_ = bf16[160,2560]{1,0:T(8,128)(2,1)S(1)} collective-permute-done((bf16[160,2560]{1,0:T(8,128)(2,1)S(1)}, bf16[160,2560]{1,0:T(8,128)(2,1)S(1)}, u32[]{:S(2)}, u32[]{:S(2)}) %collective-permute-start.6) | collective-permute-done | bytes 819232 | tf_op jit(solution)/shard_map/ppermute | solution.py:31
  84.7 1.1 copy-done.4
  87.0 1.1 copy-done.16
  88.2 1.1 copy-done.19
  89.3 1.1 copy-done.22
  90.5 6.6 %pair.2 = (f32[320,640]{1,0:T(8,128)S(1)}, bf16[320,640]{1,0:T(8,128)(2,1)}) custom-call(s32[1]{0:T(128)} %bitcast.core_ref, bf16[160,2560]{1,0:T(8,128)(2,1)S(1)} %copy-done.22, bf16[160,2560]{1,0:T(8,128)(2,1)S(1)} %copy-done.19, bf16[160,2560]{1,0:T(8,128)(2,1)S(1)} %copy-done.16, bf16[80,2560]{1,0:T(8,128)(2,1)} %collective-permute-done.4.refs_3_, ...), custom_call_target="tpu_custom_call" | custom-call | flops 2097152000 | bytes 6553600 | tf_op jit(solution)/shard_map/pair/pallas_call | solution.py:168
  98.0 6.5 %pair.3 = (f32[320,640]{1,0:T(8,128)S(1)}, bf16[320,640]{1,0:T(8,128)(2,1)}) custom-call(s32[1]{0:T(128)} %bitcast.core_ref, bf16[160,2560]{1,0:T(8,128)(2,1)S(1)} %copy-done.22, bf16[160,2560]{1,0:T(8,128)(2,1)S(1)} %copy-done.19, bf16[160,2560]{1,0:T(8,128)(2,1)S(1)} %copy-done.17, bf16[80,2560]{1,0:T(8,128)(2,1)} %collective-permute-done.4.refs_3_, ...), custom_call_target="tpu_custom_call" | custom-call | flops 2097152000 | bytes 6553600 | tf_op jit(solution)/shard_map/pair/pallas_call | solution.py:168
  113.8 1.4 fusion.2
  118.8 10.5 %collective-permute-start.10 = (bf16[80,640]{1,0:T(8,128)(2,1)S(1)}, bf16[80,640]{1,0:T(8,128)(2,1)S(1)}, u32[]{:S(2)}, u32[]{:S(2)}) collective-permute-start(bf16[80,640]{1,0:T(8,128)(2,1)S(1)} %get-tuple-element.32), channel_id=1, source_target_pairs={{0,64},{32,96},{64,128},{96,160},{128,192},{160,224},{192,0},{224,... | collective-permute-start | bytes 307208 | tf_op jit(solution)/shard_map/ppermute | solution.py:54
  130.3 8.5 %collective-permute-start.11 = (bf16[80,640]{1,0:T(8,128)(2,1)S(1)}, bf16[80,640]{1,0:T(8,128)(2,1)S(1)}, u32[]{:S(2)}, u32[]{:S(2)}) collective-permute-start(bf16[80,640]{1,0:T(8,128)(2,1)S(1)} %get-tuple-element.33), channel_id=1, source_target_pairs={{0,128},{32,160},{64,192},{96,224},{128,0},{160,32},{192,64},{224,... | collective-permute-start | bytes 307208 | tf_op jit(solution)/shard_map/ppermute | solution.py:54
  138.7 3.5 %collective-permute-start.12 = (bf16[80,640]{1,0:T(8,128)(2,1)S(1)}, bf16[80,640]{1,0:T(8,128)(2,1)S(1)}, u32[]{:S(2)}, u32[]{:S(2)}) collective-permute-start(bf16[80,640]{1,0:T(8,128)(2,1)S(1)} %get-tuple-element.34), channel_id=1, source_target_pairs={{0,192},{32,224},{64,0},{96,32},{128,64},{160,96},{192,128},{224,1... | collective-permute-start | bytes 307208 | tf_op jit(solution)/shard_map/ppermute | solution.py:54
  143.5 2.1 collective-permute-start.25
  145.6 1.6 collective-permute-start.26
  147.2 2.6 %collective-permute-done.24 = bf16[80,640]{1,0:T(8,128)(2,1)S(1)} collective-permute-done((bf16[80,640]{1,0:T(8,128)(2,1)S(1)}, bf16[80,640]{1,0:T(8,128)(2,1)S(1)}, u32[]{:S(2)}, u32[]{:S(2)}) %collective-permute-start.24) | collective-permute-done | bytes 102432 | tf_op jit(solution)/shard_map/ppermute | solution.py:54
  149.8 5.0 %collective-permute-done.25 = bf16[80,640]{1,0:T(8,128)(2,1)S(1)} collective-permute-done((bf16[80,640]{1,0:T(8,128)(2,1)S(1)}, bf16[80,640]{1,0:T(8,128)(2,1)S(1)}, u32[]{:S(2)}, u32[]{:S(2)}) %collective-permute-start.25) | collective-permute-done | bytes 102432 | tf_op jit(solution)/shard_map/ppermute | solution.py:54
  154.8 1.7 collective-permute-done.26
  157.7 2.7 %collective-permute-start.28 = (bf16[80,640]{1,0:T(8,128)(2,1)S(1)}, bf16[80,640]{1,0:T(8,128)(2,1)S(1)}, u32[]{:S(2)}, u32[]{:S(2)}) collective-permute-start(bf16[80,640]{1,0:T(8,128)(2,1)S(1)} %get-tuple-element.61), channel_id=1, source_target_pairs={{0,128},{32,160},{64,192},{96,224},{128,0},{160,32},{192,64},{224,... | collective-permute-start | bytes 307208 | tf_op jit(solution)/shard_map/ppermute | solution.py:54
  160.4 3.1 %collective-permute-start.29 = (bf16[80,640]{1,0:T(8,128)(2,1)S(1)}, bf16[80,640]{1,0:T(8,128)(2,1)S(1)}, u32[]{:S(2)}, u32[]{:S(2)}) collective-permute-start(bf16[80,640]{1,0:T(8,128)(2,1)S(1)} %get-tuple-element.61), channel_id=1, source_target_pairs={{0,192},{32,224},{64,0},{96,32},{128,64},{160,96},{192,128},{224,1... | collective-permute-start | bytes 307208 | tf_op jit(solution)/shard_map/ppermute | solution.py:54
  163.5 2.2 %collective-permute-start.14 = (bf16[80,640]{1,0:T(8,128)(2,1)S(1)}, bf16[80,640]{1,0:T(8,128)(2,1)S(1)}, u32[]{:S(2)}, u32[]{:S(2)}) collective-permute-start(bf16[80,640]{1,0:T(8,128)(2,1)S(1)} %get-tuple-element.62), channel_id=1, source_target_pairs={{0,128},{32,160},{64,192},{96,224},{128,0},{160,32},{192,64},{224,... | collective-permute-start | bytes 307208 | tf_op jit(solution)/shard_map/ppermute | solution.py:54
  165.8 3.6 %collective-permute-start.15 = (bf16[80,640]{1,0:T(8,128)(2,1)S(1)}, bf16[80,640]{1,0:T(8,128)(2,1)S(1)}, u32[]{:S(2)}, u32[]{:S(2)}) collective-permute-start(bf16[80,640]{1,0:T(8,128)(2,1)S(1)} %get-tuple-element.62), channel_id=1, source_target_pairs={{0,192},{32,224},{64,0},{96,32},{128,64},{160,96},{192,128},{224,1... | collective-permute-start | bytes 307208 | tf_op jit(solution)/shard_map/ppermute | solution.py:54
  169.3 7.4 %collective-permute-done.29 = bf16[80,640]{1,0:T(8,128)(2,1)S(1)} collective-permute-done((bf16[80,640]{1,0:T(8,128)(2,1)S(1)}, bf16[80,640]{1,0:T(8,128)(2,1)S(1)}, u32[]{:S(2)}, u32[]{:S(2)}) %collective-permute-start.29) | collective-permute-done | bytes 102432 | tf_op jit(solution)/shard_map/ppermute | solution.py:54
  177.5 1.5 collective-permute-done.15
  179.7 1.3 collective-permute-done.16.refs_1_
  181.0 4.8 %density.5 = (bf16[80,2560]{1,0:T(8,128)(2,1)S(1)}, bf16[80,2560]{1,0:T(8,128)(2,1)S(1)}) custom-call(s32[2]{0:T(128)S(1)} %pad_add_fusion.place_ref, bf16[320,640]{1,0:T(8,128)(2,1)S(1)} %pad_maximum_fusion.1.refs_0_, bf16[320,640]{1,0:T(8,128)(2,1)S(1)} %collective-permute-done.16.refs_1_, bf16[320,640]{1,0:T(8,128)(2,1)S(1)} %pad_maximum_fusion.2.refs_2_, ...), custom_call_target="tpu_custom_call" | custom-call | flops 1048576000 | bytes 6553600 | tf_op jit(solution)/shard_map/density/pallas_call | solution.py:265
  186.1 5.5 %density.4 = (bf16[80,2560]{1,0:T(8,128)(2,1)S(1)}, f32[80,2560]{1,0:T(8,128)S(1)}, f32[80,2560]{1,0:T(8,128)S(1)}, bf16[80,2560]{1,0:T(8,128)(2,1)S(1)}) custom-call(s32[2]{0:T(128)S(1)} %pad_add_fusion.place_ref, bf16[320,640]{1,0:T(8,128)(2,1)S(1)} %pad_maximum_fusion.1.refs_0_, bf16[320,640]{1,0:T(8,128)(2,1)S(1)} %collective-permute-done.16.refs_1_, ...), custom_call_target="tpu_custom_call" | custom-call | flops 2097152000 | bytes 6553600 | tf_op jit(solution)/shard_map/density/pallas_call | solution.py:265
  191.6 1.5 collective-permute-start.31
  193.3 1.4 collective-permute-start.36
  194.6 4.8 %density.3 = (f32[80,2560]{1,0:T(8,128)S(1)}, f32[80,2560]{1,0:T(8,128)S(1)}) custom-call(s32[2]{0:T(128)S(1)} %pad_add_fusion.place_ref, bf16[320,640]{1,0:T(8,128)(2,1)S(1)} %pad_maximum_fusion.1.refs_0_, bf16[320,640]{1,0:T(8,128)(2,1)S(1)} %collective-permute-done.16.refs_1_, bf16[320,640]{1,0:T(8,128)(2,1)S(1)} %pad_maximum_fusion.2.refs_2_, ...), custom_call_target="tpu_custom_call" | custom-call | flops 1048576000 | bytes 6553600 | tf_op jit(solution)/shard_map/density/pallas_call | solution.py:265
  199.8 3.4 %collective-permute-done.34 = bf16[80,2560]{1,0:T(8,128)(2,1)S(1)} collective-permute-done((bf16[80,2560]{1,0:T(8,128)(2,1)S(1)}, bf16[80,2560]{1,0:T(8,128)(2,1)S(1)}, u32[]{:S(2)}, u32[]{:S(2)}) %collective-permute-start.34) | collective-permute-done | bytes 409632 | tf_op jit(solution)/shard_map/ppermute | solution.py:46
  203.8 1.8 collective-permute-done.31
  205.5 15.2 %collective-permute-done.33 = bf16[80,2560]{1,0:T(8,128)(2,1)S(1)} collective-permute-done((bf16[80,2560]{1,0:T(8,128)(2,1)S(1)}, bf16[80,2560]{1,0:T(8,128)(2,1)S(1)}, u32[]{:S(2)}, u32[]{:S(2)}) %collective-permute-start.33) | collective-permute-done | bytes 409632 | tf_op jit(solution)/shard_map/ppermute | solution.py:46
  (105 shorter events, 24.6 us)
Async XLA Ops:
  1.1 10.3 %collective-permute-start = (bf16[320,512]{1,0:T(8,128)(2,1)S(1)}, bf16[320,512]{1,0:T(8,128)(2,1)S(1)}, u32[]{:S(2)}, u32[]{:S(2)}) collective-permute-start(bf16[320,512]{1,0:T(8,128)(2,1)S(1)} %get-tuple-element.50), channel_id=1, source_target_pairs={{0,32},{32,64},{64,96},{96,128},{128,160},{160,192},{192,224},{1,3... | collective-permute-start | bytes 983048 | tf_op jit(solution)/shard_map/ppermute | solution.py:287
  7.4 12.8 %collective-permute-start.1 = (bf16[320,512]{1,0:T(8,128)(2,1)S(1)}, bf16[320,512]{1,0:T(8,128)(2,1)S(1)}, u32[]{:S(2)}, u32[]{:S(2)}) collective-permute-start(bf16[320,512]{1,0:T(8,128)(2,1)S(1)} %get-tuple-element.49), channel_id=1, source_target_pairs={{32,0},{64,32},{96,64},{128,96},{160,128},{192,160},{224,192},{33,... | collective-permute-start | bytes 983048 | tf_op jit(solution)/shard_map/ppermute | solution.py:288
  20.2 2.7 %copy-start.9 = (bf16[180,128,128]{2,1,0:T(8,128)(2,1)S(1)}, bf16[180,128,128]{2,1,0:T(8,128)(2,1)}, u32[]{:S(2)}) copy-start(bf16[180,128,128]{2,1,0:T(8,128)(2,1)} %tiles.1) | copy-start | bytes 17694724
  30.7 16.2 %collective-permute-start.7 = (bf16[160,2560]{1,0:T(8,128)(2,1)S(1)}, bf16[160,2560]{1,0:T(8,128)(2,1)S(1)}, u32[]{:S(2)}, u32[]{:S(2)}) collective-permute-start(bf16[160,2560]{1,0:T(8,128)(2,1)S(1)} %get-tuple-element.28.refs_5_.refs_4_), channel_id=1, source_target_pairs={{0,24},{1,25},{2,26},{3,27},{4,28},{5,29},{6,30},{7,31},{8,0},{9,1... | collective-permute-start | bytes 2457608 | tf_op jit(solution)/shard_map/ppermute | solution.py:31
  33.5 19.1 %collective-permute-start.8 = (bf16[160,2560]{1,0:T(8,128)(2,1)S(1)}, bf16[160,2560]{1,0:T(8,128)(2,1)S(1)}, u32[]{:S(2)}, u32[]{:S(2)}) collective-permute-start(bf16[160,2560]{1,0:T(8,128)(2,1)S(1)} %get-tuple-element.28.refs_5_.refs_4_), channel_id=1, source_target_pairs={{0,6},{1,7},{2,4},{3,5},{4,2},{5,3},{6,0},{7,1},{8,14},{9,15},{10,... | collective-permute-start | bytes 2457608 | tf_op jit(solution)/shard_map/ppermute | solution.py:36
  36.0 16.7 %collective-permute-start.3 = (bf16[160,2560]{1,0:T(8,128)(2,1)S(1)}, bf16[160,2560]{1,0:T(8,128)(2,1)S(1)}, u32[]{:S(2)}, u32[]{:S(2)}) collective-permute-start(bf16[160,2560]{1,0:T(8,128)(2,1)S(1)} %get-tuple-element.27.refs_0_), channel_id=1, source_target_pairs={{0,1},{1,0},{2,3},{3,2},{4,5},{5,4},{6,7},{7,6},{8,9},{9,8},{10,11... | collective-permute-start | bytes 2457608 | tf_op jit(solution)/shard_map/ppermute | solution.py:46
  36.0 17.7 %collective-permute-start.2 = (bf16[160,2560]{1,0:T(8,128)(2,1)S(1)}, bf16[160,2560]{1,0:T(8,128)(2,1)S(1)}, u32[]{:S(2)}, u32[]{:S(2)}) collective-permute-start(bf16[160,2560]{1,0:T(8,128)(2,1)S(1)} %get-tuple-element.27.refs_0_), channel_id=1, source_target_pairs={{0,2},{1,3},{2,0},{3,1},{4,6},{5,7},{6,4},{7,5},{8,10},{9,11},{10,... | collective-permute-start | bytes 2457608 | tf_op jit(solution)/shard_map/ppermute | solution.py:41
  46.9 25.1 %copy-start = (bf16[160,2560]{1,0:T(8,128)(2,1)}, bf16[160,2560]{1,0:T(8,128)(2,1)S(1)}, u32[]{:S(2)}) copy-start(bf16[160,2560]{1,0:T(8,128)(2,1)S(1)} %collective-permute-done.7.refs_7_.refs_6_) | copy-start | bytes 2457604
  46.9 13.4 %collective-permute-start.18 = (bf16[160,2560]{1,0:T(8,128)(2,1)S(1)}, bf16[160,2560]{1,0:T(8,128)(2,1)S(1)}, u32[]{:S(2)}, u32[]{:S(2)}) collective-permute-start(bf16[160,2560]{1,0:T(8,128)(2,1)S(1)} %collective-permute-done.7.refs_7_.refs_6_), channel_id=1, source_target_pairs={{0,24},{1,25},{2,26},{3,27},{4,28},{5,29},{6,30},{7,31},{8,0},{9,1... | collective-permute-start | bytes 2457608 | tf_op jit(solution)/shard_map/ppermute | solution.py:31
  50.2 14.5 %collective-permute-start.19 = (bf16[160,2560]{1,0:T(8,128)(2,1)S(1)}, bf16[160,2560]{1,0:T(8,128)(2,1)S(1)}, u32[]{:S(2)}, u32[]{:S(2)}) collective-permute-start(bf16[160,2560]{1,0:T(8,128)(2,1)S(1)} %collective-permute-done.7.refs_7_.refs_6_), channel_id=1, source_target_pairs={{0,6},{1,7},{2,4},{3,5},{4,2},{5,3},{6,0},{7,1},{8,14},{9,15},{10,... | collective-permute-start | bytes 2457608 | tf_op jit(solution)/shard_map/ppermute | solution.py:36
  52.7 19.3 %copy-start.3 = (bf16[160,2560]{1,0:T(8,128)(2,1)}, bf16[160,2560]{1,0:T(8,128)(2,1)S(1)}, u32[]{:S(2)}) copy-start(bf16[160,2560]{1,0:T(8,128)(2,1)S(1)} %collective-permute-done.8.refs_8_.refs_7_) | copy-start | bytes 2457604
  52.7 18.6 %collective-permute-start.17 = (bf16[160,2560]{1,0:T(8,128)(2,1)S(1)}, bf16[160,2560]{1,0:T(8,128)(2,1)S(1)}, u32[]{:S(2)}, u32[]{:S(2)}) collective-permute-start(bf16[160,2560]{1,0:T(8,128)(2,1)S(1)} %collective-permute-done.8.refs_8_.refs_7_), channel_id=1, source_target_pairs={{0,8},{1,9},{2,10},{3,11},{4,12},{5,13},{6,14},{7,15},{8,16},{9,17... | collective-permute-start | bytes 2457608 | tf_op jit(solution)/shard_map/ppermute | solution.py:31
  52.7 19.3 %copy-start.15 = (bf16[160,2560]{1,0:T(8,128)(2,1)}, bf16[160,2560]{1,0:T(8,128)(2,1)S(1)}, u32[]{:S(2)}) copy-start(bf16[160,2560]{1,0:T(8,128)(2,1)S(1)} %collective-permute-done.3.refs_2_) | copy-start | bytes 2457604
  52.7 30.0 %collective-permute-start.6 = (bf16[160,2560]{1,0:T(8,128)(2,1)S(1)}, bf16[160,2560]{1,0:T(8,128)(2,1)S(1)}, u32[]{:S(2)}, u32[]{:S(2)}) collective-permute-start(bf16[160,2560]{1,0:T(8,128)(2,1)S(1)} %get-tuple-element.28.refs_5_.refs_4_), channel_id=1, source_target_pairs={{0,8},{1,9},{2,10},{3,11},{4,12},{5,13},{6,14},{7,15},{8,16},{9,17... | collective-permute-start | bytes 2457608 | tf_op jit(solution)/shard_map/ppermute | solution.py:31
  53.8 29.8 %collective-permute-start.4 = (bf16[80,2560]{1,0:T(8,128)(2,1)}, bf16[80,2560]{1,0:T(8,128)(2,1)}, u32[]{:S(2)}, u32[]{:S(2)}) collective-permute-start(bf16[80,2560]{1,0:T(8,128)(2,1)} %slice.38), channel_id=1, source_target_pairs={{0,2},{1,3},{2,0},{3,1},{4,6},{5,7},{6,4},{7,5},{8,10},{9,11},{10,... | collective-permute-start | bytes 1228808 | tf_op jit(solution)/shard_map/ppermute | solution.py:41
  60.4 23.2 %collective-permute-start.5 = (bf16[80,2560]{1,0:T(8,128)(2,1)}, bf16[80,2560]{1,0:T(8,128)(2,1)}, u32[]{:S(2)}, u32[]{:S(2)}) collective-permute-start(bf16[80,2560]{1,0:T(8,128)(2,1)} %slice.39), channel_id=1, source_target_pairs={{0,1},{1,0},{2,3},{3,2},{4,5},{5,4},{6,7},{7,6},{8,9},{9,8},{10,11... | collective-permute-start | bytes 1228808 | tf_op jit(solution)/shard_map/ppermute | solution.py:46
  64.7 33.2 %collective-permute-start.20 = (bf16[64,2560]{1,0:T(8,128)(2,1)}, bf16[64,2560]{1,0:T(8,128)(2,1)}, u32[]{:S(2)}, u32[]{:S(2)}) collective-permute-start(bf16[64,2560]{1,0:T(8,128)(2,1)} %slice.40), channel_id=1, source_target_pairs={{0,6},{1,7},{2,4},{3,5},{4,2},{5,3},{6,0},{7,1},{8,14},{9,15},{10,... | collective-permute-start | bytes 983048 | tf_op jit(solution)/shard_map/ppermute | solution.py:36
  71.3 26.6 %collective-permute-start.22 = (bf16[48,2560]{1,0:T(8,128)(2,1)}, bf16[48,2560]{1,0:T(8,128)(2,1)S(1)}, u32[]{:S(2)}, u32[]{:S(2)}) collective-permute-start(bf16[48,2560]{1,0:T(8,128)(2,1)} %slice.42), channel_id=1, source_target_pairs={{0,24},{1,25},{2,26},{3,27},{4,28},{5,29},{6,30},{7,31},{8,0},{9,1... | collective-permute-start | bytes 737288 | tf_op jit(solution)/shard_map/ppermute | solution.py:31
  83.6 14.4 %collective-permute-start.21 = (bf16[48,2560]{1,0:T(8,128)(2,1)}, bf16[48,2560]{1,0:T(8,128)(2,1)}, u32[]{:S(2)}, u32[]{:S(2)}) collective-permute-start(bf16[48,2560]{1,0:T(8,128)(2,1)} %slice.41), channel_id=1, source_target_pairs={{0,8},{1,9},{2,10},{3,11},{4,12},{5,13},{6,14},{7,15},{8,16},{9,17... | collective-permute-start | bytes 737288 | tf_op jit(solution)/shard_map/ppermute | solution.py:31
  90.5 7.5 %copy-start.17 = (bf16[160,2560]{1,0:T(8,128)(2,1)S(1)}, bf16[160,2560]{1,0:T(8,128)(2,1)}, u32[]{:S(2)}) copy-start(bf16[160,2560]{1,0:T(8,128)(2,1)} %copy-done.15) | copy-start | bytes 2457604
  97.9 7.9 %copy-start.24 = (s32[4]{0:T(128)S(1)}, s32[4]{0:T(128)}, u32[]{:S(2)}) copy-start(s32[4]{0:T(128)} %constant.107.clone) | copy-start | bytes 52
  97.9 10.8 %copy-start.23 = (s32[2]{0:T(128)S(1)}, s32[2]{0:T(128)}, u32[]{:S(2)}) copy-start(s32[2]{0:T(128)} %param.12) | copy-start | bytes 28
  97.9 18.6 %collective-permute-start.9 = (bf16[320,640]{1,0:T(8,128)(2,1)}, bf16[320,640]{1,0:T(8,128)(2,1)}, u32[]{:S(2)}, u32[]{:S(2)}) collective-permute-start(bf16[320,640]{1,0:T(8,128)(2,1)} %get-tuple-element.30), channel_id=1, source_target_pairs={{0,32},{32,0},{64,96},{96,64},{128,160},{160,128},{192,224},{224,1... | collective-permute-start | bytes 1228808 | tf_op jit(solution)/shard_map/ppermute | solution.py:50
  105.4 36.9 %collective-permute-start.23 = (bf16[320,640]{1,0:T(8,128)(2,1)}, bf16[320,640]{1,0:T(8,128)(2,1)}, u32[]{:S(2)}, u32[]{:S(2)}) collective-permute-start(bf16[320,640]{1,0:T(8,128)(2,1)} %get-tuple-element.36), channel_id=1, source_target_pairs={{0,32},{32,0},{64,96},{96,64},{128,160},{160,128},{192,224},{224,1... | collective-permute-start | bytes 1228808 | tf_op jit(solution)/shard_map/ppermute | solution.py:50
  113.8 28.5 %copy-start.12 = (f32[320,640]{1,0:T(8,128)S(1)}, f32[320,640]{1,0:T(8,128)}, u32[]{:S(2)}) copy-start(f32[320,640]{1,0:T(8,128)} %copy-done.11) | copy-start | bytes 2457604
  118.8 26.8 %collective-permute-start.10 = (bf16[80,640]{1,0:T(8,128)(2,1)S(1)}, bf16[80,640]{1,0:T(8,128)(2,1)S(1)}, u32[]{:S(2)}, u32[]{:S(2)}) collective-permute-start(bf16[80,640]{1,0:T(8,128)(2,1)S(1)} %get-tuple-element.32), channel_id=1, source_target_pairs={{0,64},{32,96},{64,128},{96,160},{128,192},{160,224},{192,0},{224,... | collective-permute-start | bytes 307208 | tf_op jit(solution)/shard_map/ppermute | solution.py:54
  130.3 17.0 %collective-permute-start.11 = (bf16[80,640]{1,0:T(8,128)(2,1)S(1)}, bf16[80,640]{1,0:T(8,128)(2,1)S(1)}, u32[]{:S(2)}, u32[]{:S(2)}) collective-permute-start(bf16[80,640]{1,0:T(8,128)(2,1)S(1)} %get-tuple-element.33), channel_id=1, source_target_pairs={{0,128},{32,160},{64,192},{96,224},{128,0},{160,32},{192,64},{224,... | collective-permute-start | bytes 307208 | tf_op jit(solution)/shard_map/ppermute | solution.py:54
  138.7 8.5 %collective-permute-start.12 = (bf16[80,640]{1,0:T(8,128)(2,1)S(1)}, bf16[80,640]{1,0:T(8,128)(2,1)S(1)}, u32[]{:S(2)}, u32[]{:S(2)}) collective-permute-start(bf16[80,640]{1,0:T(8,128)(2,1)S(1)} %get-tuple-element.34), channel_id=1, source_target_pairs={{0,192},{32,224},{64,0},{96,32},{128,64},{160,96},{192,128},{224,1... | collective-permute-start | bytes 307208 | tf_op jit(solution)/shard_map/ppermute | solution.py:54
  143.4 37.6 %copy-start.2 = (bf16[160,2560]{1,0:T(8,128)(2,1)S(1)}, bf16[160,2560]{1,0:T(8,128)(2,1)}, u32[]{:S(2)}) copy-start(bf16[160,2560]{1,0:T(8,128)(2,1)} %copy-done) | copy-start | bytes 2457604
  143.4 37.6 %copy-start.5 = (bf16[160,2560]{1,0:T(8,128)(2,1)S(1)}, bf16[160,2560]{1,0:T(8,128)(2,1)}, u32[]{:S(2)}) copy-start(bf16[160,2560]{1,0:T(8,128)(2,1)} %copy-done.3) | copy-start | bytes 2457604
  143.4 37.6 %copy-start.8 = (bf16[160,2560]{1,0:T(8,128)(2,1)S(1)}, bf16[160,2560]{1,0:T(8,128)(2,1)}, u32[]{:S(2)}) copy-start(bf16[160,2560]{1,0:T(8,128)(2,1)} %copy-done.6) | copy-start | bytes 2457604
  143.4 6.4 %collective-permute-start.24 = (bf16[80,640]{1,0:T(8,128)(2,1)S(1)}, bf16[80,640]{1,0:T(8,128)(2,1)S(1)}, u32[]{:S(2)}, u32[]{:S(2)}) collective-permute-start(bf16[80,640]{1,0:T(8,128)(2,1)S(1)} %get-tuple-element.38), channel_id=1, source_target_pairs={{0,64},{32,96},{64,128},{96,160},{128,192},{160,224},{192,0},{224,... | collective-permute-start | bytes 307208 | tf_op jit(solution)/shard_map/ppermute | solution.py:54
  143.5 11.3 %collective-permute-start.25 = (bf16[80,640]{1,0:T(8,128)(2,1)S(1)}, bf16[80,640]{1,0:T(8,128)(2,1)S(1)}, u32[]{:S(2)}, u32[]{:S(2)}) collective-permute-start(bf16[80,640]{1,0:T(8,128)(2,1)S(1)} %get-tuple-element.39), channel_id=1, source_target_pairs={{0,128},{32,160},{64,192},{96,224},{128,0},{160,32},{192,64},{224,... | collective-permute-start | bytes 307208 | tf_op jit(solution)/shard_map/ppermute | solution.py:54
  145.6 11.0 %collective-permute-start.26 = (bf16[80,640]{1,0:T(8,128)(2,1)S(1)}, bf16[80,640]{1,0:T(8,128)(2,1)S(1)}, u32[]{:S(2)}, u32[]{:S(2)}) collective-permute-start(bf16[80,640]{1,0:T(8,128)(2,1)S(1)} %get-tuple-element.40), channel_id=1, source_target_pairs={{0,192},{32,224},{64,0},{96,32},{128,64},{160,96},{192,128},{224,1... | collective-permute-start | bytes 307208 | tf_op jit(solution)/shard_map/ppermute | solution.py:54
  156.7 9.0 %collective-permute-start.27 = (bf16[80,640]{1,0:T(8,128)(2,1)S(1)}, bf16[80,640]{1,0:T(8,128)(2,1)S(1)}, u32[]{:S(2)}, u32[]{:S(2)}) collective-permute-start(bf16[80,640]{1,0:T(8,128)(2,1)S(1)} %get-tuple-element.61), channel_id=1, source_target_pairs={{0,64},{32,96},{64,128},{96,160},{128,192},{160,224},{192,0},{224,... | collective-permute-start | bytes 307208 | tf_op jit(solution)/shard_map/ppermute | solution.py:54
  157.7 11.6 %collective-permute-start.28 = (bf16[80,640]{1,0:T(8,128)(2,1)S(1)}, bf16[80,640]{1,0:T(8,128)(2,1)S(1)}, u32[]{:S(2)}, u32[]{:S(2)}) collective-permute-start(bf16[80,640]{1,0:T(8,128)(2,1)S(1)} %get-tuple-element.61), channel_id=1, source_target_pairs={{0,128},{32,160},{64,192},{96,224},{128,0},{160,32},{192,64},{224,... | collective-permute-start | bytes 307208 | tf_op jit(solution)/shard_map/ppermute | solution.py:54
  160.4 16.4 %collective-permute-start.29 = (bf16[80,640]{1,0:T(8,128)(2,1)S(1)}, bf16[80,640]{1,0:T(8,128)(2,1)S(1)}, u32[]{:S(2)}, u32[]{:S(2)}) collective-permute-start(bf16[80,640]{1,0:T(8,128)(2,1)S(1)} %get-tuple-element.61), channel_id=1, source_target_pairs={{0,192},{32,224},{64,0},{96,32},{128,64},{160,96},{192,128},{224,1... | collective-permute-start | bytes 307208 | tf_op jit(solution)/shard_map/ppermute | solution.py:54
  163.5 14.0 %collective-permute-start.13 = (bf16[80,640]{1,0:T(8,128)(2,1)S(1)}, bf16[80,640]{1,0:T(8,128)(2,1)S(1)}, u32[]{:S(2)}, u32[]{:S(2)}) collective-permute-start(bf16[80,640]{1,0:T(8,128)(2,1)S(1)} %get-tuple-element.62), channel_id=1, source_target_pairs={{0,64},{32,96},{64,128},{96,160},{128,192},{160,224},{192,0},{224,... | collective-permute-start | bytes 307208 | tf_op jit(solution)/shard_map/ppermute | solution.py:54
  163.5 14.0 %collective-permute-start.14 = (bf16[80,640]{1,0:T(8,128)(2,1)S(1)}, bf16[80,640]{1,0:T(8,128)(2,1)S(1)}, u32[]{:S(2)}, u32[]{:S(2)}) collective-permute-start(bf16[80,640]{1,0:T(8,128)(2,1)S(1)} %get-tuple-element.62), channel_id=1, source_target_pairs={{0,128},{32,160},{64,192},{96,224},{128,0},{160,32},{192,64},{224,... | collective-permute-start | bytes 307208 | tf_op jit(solution)/shard_map/ppermute | solution.py:54
  165.8 13.2 %collective-permute-start.15 = (bf16[80,640]{1,0:T(8,128)(2,1)S(1)}, bf16[80,640]{1,0:T(8,128)(2,1)S(1)}, u32[]{:S(2)}, u32[]{:S(2)}) collective-permute-start(bf16[80,640]{1,0:T(8,128)(2,1)S(1)} %get-tuple-element.62), channel_id=1, source_target_pairs={{0,192},{32,224},{64,0},{96,32},{128,64},{160,96},{192,128},{224,1... | collective-permute-start | bytes 307208 | tf_op jit(solution)/shard_map/ppermute | solution.py:54
  176.8 2.9 %collective-permute-start.30 = (bf16[320,640]{1,0:T(8,128)(2,1)S(1)}, bf16[320,640]{1,0:T(8,128)(2,1)S(1)}, u32[]{:S(2)}, u32[]{:S(2)}) collective-permute-start(bf16[320,640]{1,0:T(8,128)(2,1)S(1)} %pad_maximum_fusion.2.refs_2_), channel_id=1, source_target_pairs={{0,32},{32,0},{64,96},{96,64},{128,160},{160,128},{192,224},{224,1... | collective-permute-start | bytes 1228808 | tf_op jit(solution)/shard_map/ppermute | solution.py:50
  179.0 2.0 collective-permute-start.16
  185.8 13.7 %collective-permute-start.32 = (bf16[80,2560]{1,0:T(8,128)(2,1)S(1)}, bf16[80,2560]{1,0:T(8,128)(2,1)S(1)}, u32[]{:S(2)}, u32[]{:S(2)}) collective-permute-start(bf16[80,2560]{1,0:T(8,128)(2,1)S(1)} %get-tuple-element.44), channel_id=1, source_target_pairs={{0,2},{1,3},{2,0},{3,1},{4,6},{5,7},{6,4},{7,5},{8,10},{9,11},{10,... | collective-permute-start | bytes 1228808 | tf_op jit(solution)/shard_map/ppermute | solution.py:41
  191.6 13.9 %collective-permute-start.31 = (bf16[80,2560]{1,0:T(8,128)(2,1)S(1)}, bf16[80,2560]{1,0:T(8,128)(2,1)S(1)}, u32[]{:S(2)}, u32[]{:S(2)}) collective-permute-start(bf16[80,2560]{1,0:T(8,128)(2,1)S(1)} %get-tuple-element.42), channel_id=1, source_target_pairs={{0,2},{1,3},{2,0},{3,1},{4,6},{5,7},{6,4},{7,5},{8,10},{9,11},{10,... | collective-permute-start | bytes 1228808 | tf_op jit(solution)/shard_map/ppermute | solution.py:41
  193.2 10.0 %collective-permute-start.34 = (bf16[80,2560]{1,0:T(8,128)(2,1)S(1)}, bf16[80,2560]{1,0:T(8,128)(2,1)S(1)}, u32[]{:S(2)}, u32[]{:S(2)}) collective-permute-start(bf16[80,2560]{1,0:T(8,128)(2,1)S(1)} %get-tuple-element.47), channel_id=1, source_target_pairs={{0,1},{1,0},{2,3},{3,2},{4,5},{5,4},{6,7},{7,6},{8,9},{9,8},{10,11... | collective-permute-start | bytes 1228808 | tf_op jit(solution)/shard_map/ppermute | solution.py:46
  193.3 27.6 %collective-permute-start.36 = (bf16[80,2560]{1,0:T(8,128)(2,1)S(1)}, bf16[80,2560]{1,0:T(8,128)(2,1)S(1)}, u32[]{:S(2)}, u32[]{:S(2)}) collective-permute-start(bf16[80,2560]{1,0:T(8,128)(2,1)S(1)} %get-tuple-element.48), channel_id=1, source_target_pairs={{0,1},{1,0},{2,3},{3,2},{4,5},{5,4},{6,7},{7,6},{8,9},{9,8},{10,11... | collective-permute-start | bytes 1228808 | tf_op jit(solution)/shard_map/ppermute | solution.py:46
  199.6 21.2 %collective-permute-start.33 = (bf16[80,2560]{1,0:T(8,128)(2,1)S(1)}, bf16[80,2560]{1,0:T(8,128)(2,1)S(1)}, u32[]{:S(2)}, u32[]{:S(2)}) collective-permute-start(bf16[80,2560]{1,0:T(8,128)(2,1)S(1)} %add_convert_fusion.3), channel_id=1, source_target_pairs={{0,1},{1,0},{2,3},{3,2},{4,5},{5,4},{6,7},{7,6},{8,9},{9,8},{10,11... | collective-permute-start | bytes 1228808 | tf_op jit(solution)/shard_map/ppermute | solution.py:46
  203.3 17.6 %collective-permute-start.35 = (bf16[80,2560]{1,0:T(8,128)(2,1)S(1)}, bf16[80,2560]{1,0:T(8,128)(2,1)S(1)}, u32[]{:S(2)}, u32[]{:S(2)}) collective-permute-start(bf16[80,2560]{1,0:T(8,128)(2,1)S(1)} %add_convert_fusion.1), channel_id=1, source_target_pairs={{0,2},{1,3},{2,0},{3,1},{4,6},{5,7},{6,4},{7,5},{8,10},{9,11},{10,... | collective-permute-start | bytes 1228808 | tf_op jit(solution)/shard_map/ppermute | solution.py:41
  (14 other events, 14.6 us)

commit v2 on v1

v2 whole, which is shorter than its diff:
```python
import functools

import jax
import jax.numpy as jnp
from jax import lax
from jax.experimental import pallas as pl
from jax.experimental.pallas import tpu as pltpu
from jax.sharding import PartitionSpec as P

TILE = 128
HB = 4
BAND = 2 * HB + 1
ROWS = 160
AUX = 2560
HALO = HB * TILE
bf16 = jnp.bfloat16
f32 = jnp.float32
MIB = 1 << 20


def blk_index(y, x, z):
    return ((y % 4) * 4 + x) * 2 + z


PLACES = [(y, x, z) for y in range(4) for x in range(4) for z in range(2)]
OUTER = (3, 2, 1, 0)


def send_y(v, step):
    pairs = [(blk_index(y, x, z), blk_index(y + step, x, z)) for y, x, z in PLACES]
    return lax.ppermute(v, "blk", pairs)


def send_outer(v):
    pairs = [(blk_index(y, x, z), blk_index(y, OUTER[x], z)) for y, x, z in PLACES]
    return lax.ppermute(v, "blk", pairs)


def send_inner(v):
    pairs = [(blk_index(y, x, z), blk_index(y, x ^ 1, z)) for y, x, z in PLACES]
    return lax.ppermute(v, "blk", pairs)


def send_z(v):
    pairs = [(blk_index(y, x, z), blk_index(y, x, 1 - z)) for y, x, z in PLACES]
    return lax.ppermute(v, "blk", pairs)


def send_core(v):
    return lax.ppermute(v, "grp", [(g, g ^ 1) for g in range(8)])


def send_high(v, step):
    return lax.ppermute(v, "grp", [(g, (g + 2 * step) % 8) for g in range(8)])


def params():
    return pltpu.CompilerParams(vmem_limit_bytes=56 * MIB)


def cost(flops, nbytes):
    return pl.CostEstimate(flops=int(flops), bytes_accessed=int(nbytes), transcendentals=0)


def position():
    group = lax.axis_index("grp").astype(jnp.int32)
    me = lax.axis_index("blk").astype(jnp.int32)
    return group // 2, group % 2, me // 8, (me // 2) % 4, me % 2


def fit_kernel(index_ref, *refs, pairs, edge):
    if edge:
        left, own, right, tiles, _, _, out_a, out_b, ext, weights = refs
    else:
        own, tiles, out_a, out_b, weights = refs
    step = pl.program_id(0)
    p = pairs(step)

    @pl.when(step == 0)
    def _():
        if edge:
            ext[:, :HALO] = left[...]
            ext[:, HALO : 3 * HALO] = own[:, : 2 * HALO]
            ext[:, 3 * HALO : 5 * HALO] = own[:, AUX - 2 * HALO :]
            ext[:, 5 * HALO :] = right[...]
        weights[...] = jnp.zeros_like(weights)

    for q in range(2):
        for o in range(BAND):
            slot = q * BAND + o
            listed = index_ref[1, p * (2 * BAND) + slot] == 1
            tile = tiles[slot]
            j = q + o
            weights[j * TILE : (j + 1) * TILE, q * TILE : (q + 1) * TILE] = jnp.where(
                listed, tile, jnp.zeros_like(tile)
            )
    if edge:
        at = jnp.where(step < 2, step * 2, 12 + (step - 2) * 2) * TILE
        window = ext[:, pl.ds(pl.multiple_of(at, 2 * TILE), (BAND + 1) * TILE)]
    else:
        at = (p * 2 - HB) * TILE
        window = own[:, pl.ds(pl.multiple_of(at, 2 * TILE), (BAND + 1) * TILE)]
    fitted = jnp.dot(window, weights[...], preferred_element_type=f32).astype(bf16)
    out_a[...] = fitted[:ROWS]
    out_b[...] = fitted[ROWS:]


def fit(index, own, tiles, halos=None, partial=None):
    edge = halos is not None
    pairs = (lambda p: jnp.where(p < 2, p, p + 6)) if edge else (lambda p: p + 2)
    whole = lambda shape: pl.BlockSpec(shape, lambda p, i: (0, 0))
    own_spec = whole((2 * ROWS, AUX))
    halo_spec = whole((2 * ROWS, HALO))
    tile_spec = pl.BlockSpec((2 * BAND, TILE, TILE), lambda p, i: (pairs(p), 0, 0))
    anywhere = pl.BlockSpec(memory_space=pl.ANY)
    scratch = [pltpu.VMEM(((BAND + 1) * TILE, 2 * TILE), bf16)]
    if edge:
        in_specs = [halo_spec, own_spec, halo_spec, tile_spec, anywhere, anywhere]
        scratch = [pltpu.VMEM((2 * ROWS, 6 * HALO), bf16)] + scratch
        args = (halos[0], own, halos[1], tiles, *partial)
    else:
        in_specs = [own_spec, tile_spec]
        args = (own, tiles)
    grid_spec = pltpu.PrefetchScalarGridSpec(
        num_scalar_prefetch=1,
        grid=(4 if edge else 6,),
        in_specs=in_specs,
        out_specs=[pl.BlockSpec((ROWS, 2 * TILE), lambda p, i: (0, pairs(p)))] * 2,
        scratch_shapes=scratch,
    )
    return pl.pallas_call(
        functools.partial(fit_kernel, pairs=pairs, edge=edge),
        grid_spec=grid_spec,
        out_shape=[jax.ShapeDtypeStruct((ROWS, AUX), bf16)] * 2,
        input_output_aliases={5: 0, 6: 1} if edge else {},
        compiler_params=params(),
        cost_estimate=cost(1e9, 5e6),
        name="fit_edge" if edge else "fit_inner",
    )(index, *args)


def pair_kernel(*refs, n_a, steps):
    a_refs, bs = refs[:n_a], refs[n_a : -4 if n_a == 1 else -5]
    if n_a == 1:
        (acat,) = a_refs
        keep, send, bcat, acc = refs[-4:]
    else:
        keep, send, bcat, acat, acc = refs[-5:]
    k = pl.program_id(0)
    if n_a > 1:
        core = position()[1]
        at = pl.multiple_of(core * (2 * ROWS), 2 * ROWS)
        for i, a in enumerate(a_refs):
            if i == 2:
                at = pl.multiple_of((1 - core) * (2 * ROWS), 2 * ROWS)
            acat[pl.ds(at, a.shape[0])] = a[...]
            at = at + a.shape[0]
    at = 0
    for b in bs:
        bcat[at : at + b.shape[0]] = b[...]
        at += b.shape[0]
    product = lax.dot_general(
        acat[...], bcat[...], (((1,), (1,)), ((), ())), preferred_element_type=f32
    )

    @pl.when(k == 0)
    def _():
        acc[...] = product

    @pl.when(k > 0)
    def _():
        acc[...] += product

    @pl.when(k == steps - 1)
    def _():
        keep[...] = acc[: 2 * ROWS]
        send[...] = acc[2 * ROWS :].astype(bf16)


def pair(a_parts, b_parts):
    width = sum(b.shape[0] for b in b_parts)
    chunk = 512
    steps = AUX // chunk
    spec = lambda rows: pl.BlockSpec((rows, chunk), lambda k: (0, k))
    whole = pl.BlockSpec((2 * ROWS, width), lambda k: (0, 0))
    n_a = len(a_parts)
    first = n_a > 1
    return pl.pallas_call(
        functools.partial(pair_kernel, n_a=n_a, steps=steps),
        grid=(steps,),
        in_specs=[spec(v.shape[0]) for v in (*a_parts, *b_parts)],
        out_specs=[whole, whole, spec(width)] + [spec(4 * ROWS)] * first,
        scratch_shapes=[pltpu.VMEM((4 * ROWS, width), f32)],
        out_shape=[
            jax.ShapeDtypeStruct((2 * ROWS, width), f32),
            jax.ShapeDtypeStruct((2 * ROWS, width), bf16),
            jax.ShapeDtypeStruct((width, AUX), bf16),
        ]
        + [jax.ShapeDtypeStruct((4 * ROWS, AUX), bf16)] * first,
        compiler_params=params(),
        cost_estimate=cost(2 * 4 * ROWS * width * AUX, 2 * (4 * ROWS + width) * AUX),
        name="pair",
    )(*a_parts, *b_parts)


SHARE = ROWS // 2


def core_sum_kernel(keep, got, own, s1, s2, s3):
    high = position()[0]
    for step, out in enumerate((own, s1, s2, s3)):
        at = pl.multiple_of(((high + step) % 4) * SHARE, SHARE)
        value = keep[pl.ds(at, SHARE)] + got[pl.ds(at, SHARE)].astype(f32)
        out[...] = value.astype(out.dtype)


def core_sum(keep, got):
    width = keep.shape[1]
    vmem = pl.BlockSpec(memory_space=pltpu.VMEM)
    return pl.pallas_call(
        core_sum_kernel,
        in_specs=[vmem, vmem],
        out_specs=[vmem] * 4,
        out_shape=[jax.ShapeDtypeStruct((SHARE, width), f32)]
        + [jax.ShapeDtypeStruct((SHARE, width), bf16)] * 3,
        compiler_params=params(),
        cost_estimate=cost(1e6, 3e6),
        name="core_sum",
    )(keep, got)


def amplitude_kernel(vir, occ, chosen, own, r1, r2, r3, out, *, offsets):
    high, core, y, x, z = position()
    outer = 3 - x
    occ_total = occ[chosen[0]] + occ[chosen[1]]
    inner = x + 1 - 2 * (x % 2)
    row_x = jnp.where(high < 2, x, inner)
    row_z = jnp.where(core == 0, z, 1 - z)
    block = vir[pl.ds((y * 4 + row_x) * 2 + row_z, 1), :]
    lane = lax.broadcasted_iota(jnp.int32, (SHARE, ROWS), 1)
    row = lax.broadcasted_iota(jnp.int32, (SHARE, ROWS), 0)
    chosen_lane = lane == row + (high % 2) * SHARE
    rows = jnp.sum(jnp.where(chosen_lane, block, 0.0), axis=1, keepdims=True)
    total = own[...] + r1[...].astype(f32) + r2[...].astype(f32) + r3[...].astype(f32)
    for i, (step, away) in enumerate(offsets):
        at = (((y + step) % 4) * 4 + (outer if away else x)) * 2 + z
        columns = slice(i * ROWS, (i + 1) * ROWS)
        denominator = (rows + vir[pl.ds(at, 1), :]) - occ_total
        out[:, columns] = (total[:, columns] / denominator).astype(bf16)


def amplitude(vir, occ, chosen, own, received, offsets):
    vmem = pl.BlockSpec(memory_space=pltpu.VMEM)
    smem = pl.BlockSpec(memory_space=pltpu.SMEM)
    return pl.pallas_call(
        functools.partial(amplitude_kernel, offsets=offsets),
        in_specs=[vmem, smem, smem] + [vmem] * 4,
        out_specs=vmem,
        out_shape=jax.ShapeDtypeStruct(own.shape, bf16),
        compiler_params=params(),
        cost_estimate=cost(1e6, 1e6),
        name="amplitude",
    )(vir, occ, chosen, own, *received)


def density_kernel(*refs, blocks, halves):
    shares, bs, outs, tcat = refs[:4], refs[4:6], refs[6:-1], refs[-1]
    high, core = position()[:2]

    @pl.when(pl.program_id(0) == 0)
    def _():
        for piece in range(2):
            mine, other = shares[2 * piece], shares[2 * piece + 1]
            columns = slice(piece * 4 * ROWS, (piece + 1) * 4 * ROWS)
            for k in range(4):
                at = ((high - k + 4) % 4) * SHARE
                here = pl.multiple_of(core * (2 * ROWS) + at, SHARE)
                there = pl.multiple_of((1 - core) * (2 * ROWS) + at, SHARE)
                tcat[pl.ds(here, SHARE), columns] = mine[k * SHARE : (k + 1) * SHARE]
                tcat[pl.ds(there, SHARE), columns] = other[k * SHARE : (k + 1) * SHARE]

    rows = slice(blocks[0] * ROWS, blocks[1] * ROWS)
    value = jnp.dot(tcat[rows, : 4 * ROWS], bs[0][...], preferred_element_type=f32)
    value += jnp.dot(tcat[rows, 4 * ROWS :], bs[1][...], preferred_element_type=f32)
    for i, out in enumerate(outs):
        rows = ROWS // 2 if halves else ROWS
        out[...] = value[i * rows : (i + 1) * rows].astype(out.dtype)


def density(shares, b_parts, blocks, halves, types):
    chunk = 512
    steps = AUX // chunk
    rows = ROWS // 2 if halves else ROWS
    whole = pl.BlockSpec((2 * ROWS, 4 * ROWS), lambda k: (0, 0))
    n = blocks[1] - blocks[0]
    return pl.pallas_call(
        functools.partial(density_kernel, blocks=blocks, halves=halves),
        grid=(steps,),
        in_specs=[whole] * 4 + [pl.BlockSpec((4 * ROWS, chunk), lambda k: (0, k))] * 2,
        out_specs=[pl.BlockSpec((rows, chunk), lambda k: (0, k)) for _ in types],
        scratch_shapes=[pltpu.VMEM((4 * ROWS, 8 * ROWS), bf16)],
        out_shape=[jax.ShapeDtypeStruct((rows, AUX), t) for t in types],
        compiler_params=params(),
        cost_estimate=cost(2 * n * ROWS * 8 * ROWS * AUX, 2 * 8 * ROWS * AUX),
        name="density",
    )(*shares, *b_parts)


def local(integrals, tiles, tile_index, vir_energy, occ_energy, pair_index):
    window = integrals.reshape(2 * ROWS, AUX)
    index = tile_index.T
    vir = vir_energy.reshape(-1, ROWS)
    up = [(g, g + 1) for g in range(7)]
    down = [(g + 1, g) for g in range(7)]
    left = lax.ppermute(window[:, AUX - HALO :], "grp", up)
    right = lax.ppermute(window[:, :HALO], "grp", down)
    inner = fit(index, window, tiles)
    a, b = fit(index, window, tiles, (left, right), inner)

    half = ROWS // 2
    ax = send_inner(a)
    az = send_z(a)
    bm = send_y(b, 1)
    bp = send_y(b, -1)
    bo = send_outer(b)
    d1 = send_inner(az[:half])
    d2 = send_z(ax[half:])
    bom = send_y(bo, 1)
    b2 = send_y(bp, -1)
    bop = send_outer(bp)
    c1 = send_outer(b2[:64])
    c2 = send_y(bom[64:112], 1)
    c3 = send_y(bop[112:], -1)

    def reduced(keep, send, offsets):
        own, s1, s2, s3 = core_sum(keep, send_core(send))
        received = [send_high(s1, 1), send_high(s2, 2), send_high(s3, 3)]
        mine = amplitude(vir, occ_energy, pair_index, own, received, offsets)
        mine = jnp.concatenate([mine] + [send_high(mine, k) for k in (1, 2, 3)], axis=0)
        return [mine, send_core(mine)]

    keep, send, b_first, acat = pair((a, ax, az, d1, d2), (b, bm, bp, bo))
    shares = reduced(keep, send, ((0, 0), (3, 0), (1, 0), (0, 1)))
    keep, send, b_second = pair((acat,), (bom, b2, bop, c1, c2, c3))
    shares += reduced(keep, send, ((3, 1), (2, 0), (1, 1), (2, 1)))

    dense = functools.partial(density, shares, (b_first, b_second))
    to_d1, to_d2 = dense((3, 4), True, (bf16, bf16))
    x1, x2, z1, z2 = dense((1, 3), True, (bf16, f32, f32, bf16))
    o1, o2 = dense((0, 1), True, (f32, f32))
    from_x = send_inner(to_d1)
    from_z = send_z(to_d2)
    got_x1 = send_inner(x1)
    got_z2 = send_z(z2)
    got_z1 = send_z((z1 + from_x.astype(f32)).astype(bf16))
    got_x2 = send_inner((x2 + from_z.astype(f32)).astype(bf16))
    h1 = o1 + got_x1.astype(f32) + got_z1.astype(f32)
    h2 = o2 + got_x2.astype(f32) + got_z2.astype(f32)
    return jnp.concatenate([h1, h2], axis=0).astype(bf16)


def solution(mesh):
    in_specs = (P(None, "blk", "grp"), P("grp", None, None), P("grp", None), P(), P(), P())
    return jax.shard_map(
        local, mesh=mesh, in_specs=in_specs, out_specs=P("blk", "grp"), check_vma=False
    )
```

time: 224 us -> 216 us (0.964)
  Pallas kernels: 36.1 us -> 60.7 us
  local copies, waits for them, and re-layouts: 26.6 us -> 8.72 us
  waiting for transfers between devices: 81.8 us -> 67.7 us
  between operations: 7.56 us -> 0.39 us
  starting transfers between devices: 68 us -> 72.8 us
    pallas_call x8 -> x11, Pallas kernels: 36.1 us -> 60.7 us  [the longest x3 21.2 us: density(): pl.pallas_call(functools.partial(density_kernel, blocks=blocks, halves=ha...]
    ppermute x5, waiting for transfers between devices: 18.6 us -> 0.01 us  [send_z(): return lax.ppermute(v, 'blk', pairs)]
    ppermute x5, waiting for transfers between devices: 1.79 us -> 17.1 us  [send_inner(): return lax.ppermute(v, 'blk', pairs)]
    ppermute x12, waiting for transfers between devices: 18.2 us -> 7.45 us  [send_high(): return lax.ppermute(v, 'grp', [(g, (g + 2 * step) % 8) for g in range(8)])]
    unnamed x50 -> x62, local copies, waits for them, and re-layouts: 17.3 us -> 6.8 us
    ppermute x6, waiting for transfers between devices: 29 us -> 38.2 us  [send_y(): return lax.ppermute(v, 'blk', pairs)]
    ppermute x4, starting transfers between devices: 1.75 us -> 9.08 us  [send_core(): return lax.ppermute(v, 'grp', [(g, g ^ 1) for g in range(8)])]
    ppermute x1, waiting for transfers between devices: 8.76 us -> 3.49 us  [local(): right = lax.ppermute(window[:, :HALO], 'grp', down)]
  transfers between devices with their start and end apart: 37 -> 37, of which waited for: 16 -> 10; matrix products, arithmetic and copies ran while one was open for 4% -> 1% of each run, Pallas kernels for 12% -> 23%
where the time goes in v2:
time: 216 us; the launch traced here: 213 us
  starting transfers between devices  72.8 us (34%)
  waiting for transfers between devices  67.7 us (31%)
  Pallas kernels  60.7 us (28%)
  local copies, waits for them, and re-layouts  8.72 us (4%)
  other arithmetic  3.19 us (1%)
    ppermute x6, waiting for transfers between devices, send_y(): return lax.ppermute(v, 'blk', pairs)  38.2 us
    ppermute x12, starting transfers between devices, send_high(): return lax.ppermute(v, 'grp', [(g, (g + 2 * step) % 8) for g in range(8)])  34.6 us
    pallas_call x3, Pallas kernels, density(): pl.pallas_call(functools.partial(density_kernel, blocks=blocks, halves=ha...  21.2 us
    pallas_call x2, Pallas kernels, pair(): pl.pallas_call(functools.partial(pair_kernel, n_a=n_a, steps=steps), grid...  17.9 us
    ppermute x5, waiting for transfers between devices, send_inner(): return lax.ppermute(v, 'blk', pairs)  17.1 us
    pallas_call x2, Pallas kernels, fit(): pl.pallas_call(functools.partial(fit_kernel, pairs=pairs, edge=edge), gri...  13.3 us
    ppermute x4, starting transfers between devices, send_core(): return lax.ppermute(v, 'grp', [(g, g ^ 1) for g in range(8)])  9.08 us
    ppermute x3, starting transfers between devices, send_outer(): return lax.ppermute(v, 'blk', pairs)  7.52 us
  transfers between devices with their start and end apart: 37, of which 10 were waited for; matrix products, arithmetic and copies ran while one was open for 1% of the time, Pallas kernels for 23%

profile of v2, /device:TPU:1, one launch (start us, length us, event | category | flops | bytes accessed | tf_op | source)
XLA Modules:
  0.0 213.4 jit_solution(13901642386289879918)
XLA Ops:
  0.0 1.1 fusion
  1.1 6.3 %collective-permute-start = (bf16[320,512]{1,0:T(8,128)(2,1)S(1)}, bf16[320,512]{1,0:T(8,128)(2,1)S(1)}, u32[]{:S(2)}, u32[]{:S(2)}) collective-permute-start(bf16[320,512]{1,0:T(8,128)(2,1)S(1)} %get-tuple-element.60), channel_id=1, source_target_pairs={{0,32},{32,64},{64,96},{96,128},{128,160},{160,192},{192,224},{1,3... | collective-permute-start | bytes 983048 | tf_op jit(solution)/shard_map/ppermute | solution.py:315
  7.4 1.9 collective-permute-start.1
  9.3 7.4 %fit_inner.1 = (bf16[160,2560]{1,0:T(8,128)(2,1)}, bf16[160,2560]{1,0:T(8,128)(2,1)}) custom-call(s32[2,180]{1,0:T(2,128)} %bitcast.5, bf16[320,2560]{1,0:T(8,128)(2,1)} %bitcast.3, bf16[180,128,128]{2,1,0:T(8,128)(2,1)} %refs_3_.1), custom_call_target="tpu_custom_call" | custom-call | flops 1000000000 | bytes 5000000 | tf_op jit(solution)/shard_map/fit_inner/pallas_call | solution.py:131
  16.7 3.5 %collective-permute-done.1.refs_2_ = bf16[320,512]{1,0:T(8,128)(2,1)S(1)} collective-permute-done((bf16[320,512]{1,0:T(8,128)(2,1)S(1)}, bf16[320,512]{1,0:T(8,128)(2,1)S(1)}, u32[]{:S(2)}, u32[]{:S(2)}) %collective-permute-start.1) | collective-permute-done | bytes 327712 | tf_op jit(solution)/shard_map/ppermute | solution.py:316
  20.9 6.0 %fit_edge.1 = (bf16[160,2560]{1,0:T(8,128)(2,1)}, bf16[160,2560]{1,0:T(8,128)(2,1)}) custom-call(s32[2,180]{1,0:T(2,128)} %bitcast.6, bf16[320,512]{1,0:T(8,128)(2,1)} %copy-done.10, bf16[320,2560]{1,0:T(8,128)(2,1)} %bitcast.4, bf16[320,512]{1,0:T(8,128)(2,1)} %copy-done.11, ...), custom_call_target="tpu_custom_call", output_to_operand_aliasing={{0}: (5, {}), {1}: (6, {})} | custom-call | flops 1000000000 | bytes 5000000 | tf_op jit(solution)/shard_map/fit_edge/pallas_call | solution.py:131
  26.9 2.7 %collective-permute-start.7 = (bf16[160,2560]{1,0:T(8,128)(2,1)}, bf16[160,2560]{1,0:T(8,128)(2,1)S(1)}, u32[]{:S(2)}, u32[]{:S(2)}) collective-permute-start(bf16[160,2560]{1,0:T(8,128)(2,1)} %get-tuple-element.35.refs_5_), channel_id=1, source_target_pairs={{0,24},{1,25},{2,26},{3,27},{4,28},{5,29},{6,30},{7,31},{8,0},{9,1... | collective-permute-start | bytes 2457608 | tf_op jit(solution)/shard_map/ppermute | solution.py:31
  29.6 2.5 %collective-permute-start.8 = (bf16[160,2560]{1,0:T(8,128)(2,1)}, bf16[160,2560]{1,0:T(8,128)(2,1)S(1)}, u32[]{:S(2)}, u32[]{:S(2)}) collective-permute-start(bf16[160,2560]{1,0:T(8,128)(2,1)} %get-tuple-element.35.refs_5_), channel_id=1, source_target_pairs={{0,6},{1,7},{2,4},{3,5},{4,2},{5,3},{6,0},{7,1},{8,14},{9,15},{10,... | collective-permute-start | bytes 2457608 | tf_op jit(solution)/shard_map/ppermute | solution.py:36
  32.1 11.7 %collective-permute-done.7.refs_7_ = bf16[160,2560]{1,0:T(8,128)(2,1)S(1)} collective-permute-done((bf16[160,2560]{1,0:T(8,128)(2,1)}, bf16[160,2560]{1,0:T(8,128)(2,1)S(1)}, u32[]{:S(2)}, u32[]{:S(2)}) %collective-permute-start.7) | collective-permute-done | bytes 819232 | tf_op jit(solution)/shard_map/ppermute | solution.py:31
  43.8 2.7 %collective-permute-start.18 = (bf16[160,2560]{1,0:T(8,128)(2,1)S(1)}, bf16[160,2560]{1,0:T(8,128)(2,1)S(1)}, u32[]{:S(2)}, u32[]{:S(2)}) collective-permute-start(bf16[160,2560]{1,0:T(8,128)(2,1)S(1)} %collective-permute-done.7.refs_7_), channel_id=1, source_target_pairs={{0,24},{1,25},{2,26},{3,27},{4,28},{5,29},{6,30},{7,31},{8,0},{9,1... | collective-permute-start | bytes 2457608 | tf_op jit(solution)/shard_map/ppermute | solution.py:31
  46.6 2.6 %collective-permute-start.19 = (bf16[160,2560]{1,0:T(8,128)(2,1)S(1)}, bf16[160,2560]{1,0:T(8,128)(2,1)S(1)}, u32[]{:S(2)}, u32[]{:S(2)}) collective-permute-start(bf16[160,2560]{1,0:T(8,128)(2,1)S(1)} %collective-permute-done.7.refs_7_), channel_id=1, source_target_pairs={{0,6},{1,7},{2,4},{3,5},{4,2},{5,3},{6,0},{7,1},{8,14},{9,15},{10,... | collective-permute-start | bytes 2457608 | tf_op jit(solution)/shard_map/ppermute | solution.py:36
  49.3 10.3 %collective-permute-done.18.refs_2_ = bf16[160,2560]{1,0:T(8,128)(2,1)S(1)} collective-permute-done((bf16[160,2560]{1,0:T(8,128)(2,1)S(1)}, bf16[160,2560]{1,0:T(8,128)(2,1)S(1)}, u32[]{:S(2)}, u32[]{:S(2)}) %collective-permute-start.18) | collective-permute-done | bytes 819232 | tf_op jit(solution)/shard_map/ppermute | solution.py:31
  59.7 2.4 %collective-permute-start.5 = (bf16[80,2560]{1,0:T(8,128)(2,1)S(1)}, bf16[80,2560]{1,0:T(8,128)(2,1)S(1)}, u32[]{:S(2)}, u32[]{:S(2)}) collective-permute-start(bf16[80,2560]{1,0:T(8,128)(2,1)S(1)} %slice.31), channel_id=1, source_target_pairs={{0,1},{1,0},{2,3},{3,2},{4,5},{5,4},{6,7},{7,6},{8,9},{9,8},{10,11... | collective-permute-start | bytes 1228808 | tf_op jit(solution)/shard_map/ppermute | solution.py:46
  62.1 6.1 %collective-permute-done.17.refs_1_ = bf16[160,2560]{1,0:T(8,128)(2,1)S(1)} collective-permute-done((bf16[160,2560]{1,0:T(8,128)(2,1)S(1)}, bf16[160,2560]{1,0:T(8,128)(2,1)S(1)}, u32[]{:S(2)}, u32[]{:S(2)}) %collective-permute-start.17) | collective-permute-done | bytes 819232 | tf_op jit(solution)/shard_map/ppermute | solution.py:31
  68.2 2.5 %collective-permute-start.20 = (bf16[64,2560]{1,0:T(8,128)(2,1)S(1)}, bf16[64,2560]{1,0:T(8,128)(2,1)}, u32[]{:S(2)}, u32[]{:S(2)}) collective-permute-start(bf16[64,2560]{1,0:T(8,128)(2,1)S(1)} %slice.32), channel_id=1, source_target_pairs={{0,6},{1,7},{2,4},{3,5},{4,2},{5,3},{6,0},{7,1},{8,14},{9,15},{10,... | collective-permute-start | bytes 983048 | tf_op jit(solution)/shard_map/ppermute | solution.py:36
  70.9 10.1 %collective-permute-done.6.refs_6_ = bf16[160,2560]{1,0:T(8,128)(2,1)S(1)} collective-permute-done((bf16[160,2560]{1,0:T(8,128)(2,1)}, bf16[160,2560]{1,0:T(8,128)(2,1)S(1)}, u32[]{:S(2)}, u32[]{:S(2)}) %collective-permute-start.6) | collective-permute-done | bytes 819232 | tf_op jit(solution)/shard_map/ppermute | solution.py:31
  81.0 0.9 copy-done.26
  82.8 9.5 %pair.2 = (f32[320,640]{1,0:T(8,128)}, bf16[320,640]{1,0:T(8,128)(2,1)}, bf16[640,2560]{1,0:T(8,128)(2,1)}, bf16[640,2560]{1,0:T(8,128)(2,1)}) custom-call(bf16[160,2560]{1,0:T(8,128)(2,1)} %get-tuple-element.34.refs_0_, bf16[160,2560]{1,0:T(8,128)(2,1)} %copy-done.13, bf16[160,2560]{1,0:T(8,128)(2,1)} %copy-done.12, bf16[80,2560]{1,0:T(8,128)(2,1)} %copy-done.27, ...), custom_call_target="tpu_custom_call" | custom-call | flops 2097152000 | bytes 6553600 | tf_op jit(solution)/shard_map/pair/pallas_call | solution.py:188
  93.4 8.3 %pair.3 = (f32[320,640]{1,0:T(8,128)}, bf16[320,640]{1,0:T(8,128)(2,1)}, bf16[640,2560]{1,0:T(8,128)(2,1)}) custom-call(bf16[640,2560]{1,0:T(8,128)(2,1)} %get-tuple-element.42.refs_0_, bf16[160,2560]{1,0:T(8,128)(2,1)} %copy-done.21, bf16[160,2560]{1,0:T(8,128)(2,1)} %copy-done.14, bf16[160,2560]{1,0:T(8,128)(2,1)} %copy-done.22, ...), custom_call_target="tpu_custom_call" | custom-call | flops 2097152000 | bytes 6553600 | tf_op jit(solution)/shard_map/pair/pallas_call | solution.py:188
  102.3 0.8 copy-done.8
  103.0 2.1 core_sum.2
  105.1 8.6 %collective-permute-start.10 = (bf16[80,640]{1,0:T(8,128)(2,1)}, bf16[80,640]{1,0:T(8,128)(2,1)S(1)}, u32[]{:S(2)}, u32[]{:S(2)}) collective-permute-start(bf16[80,640]{1,0:T(8,128)(2,1)} %get-tuple-element.39), channel_id=1, source_target_pairs={{0,64},{32,96},{64,128},{96,160},{128,192},{160,224},{192,0},{224,... | collective-permute-start | bytes 307208 | tf_op jit(solution)/shard_map/ppermute | solution.py:54
  113.8 7.1 %collective-permute-start.11 = (bf16[80,640]{1,0:T(8,128)(2,1)}, bf16[80,640]{1,0:T(8,128)(2,1)S(1)}, u32[]{:S(2)}, u32[]{:S(2)}) collective-permute-start(bf16[80,640]{1,0:T(8,128)(2,1)} %get-tuple-element.40), channel_id=1, source_target_pairs={{0,128},{32,160},{64,192},{96,224},{128,0},{160,32},{192,64},{224,... | collective-permute-start | bytes 307208 | tf_op jit(solution)/shard_map/ppermute | solution.py:54
  120.8 3.6 %collective-permute-start.12 = (bf16[80,640]{1,0:T(8,128)(2,1)}, bf16[80,640]{1,0:T(8,128)(2,1)S(1)}, u32[]{:S(2)}, u32[]{:S(2)}) collective-permute-start(bf16[80,640]{1,0:T(8,128)(2,1)} %get-tuple-element.41), channel_id=1, source_target_pairs={{0,192},{32,224},{64,0},{96,32},{128,64},{160,96},{192,128},{224,1... | collective-permute-start | bytes 307208 | tf_op jit(solution)/shard_map/ppermute | solution.py:54
  125.2 2.2 %core_sum.3 = (f32[80,640]{1,0:T(8,128)}, bf16[80,640]{1,0:T(8,128)(2,1)}, bf16[80,640]{1,0:T(8,128)(2,1)}, bf16[80,640]{1,0:T(8,128)(2,1)}) custom-call(f32[320,640]{1,0:T(8,128)} %get-tuple-element.43.keep, bf16[320,640]{1,0:T(8,128)(2,1)} %copy-done.9), custom_call_target="tpu_custom_call" | custom-call | flops 1000000 | bytes 3000000 | tf_op jit(solution)/shard_map/core_sum/pallas_call | solution.py:220
  128.0 2.1 collective-permute-start.25
  130.1 1.6 collective-permute-start.26
  132.4 2.0 amplitude.2
  134.4 2.0 collective-permute-start.15
  136.4 3.3 %collective-permute-start.14 = (bf16[80,640]{1,0:T(8,128)(2,1)}, bf16[80,640]{1,0:T(8,128)(2,1)S(1)}, u32[]{:S(2)}, u32[]{:S(2)}) collective-permute-start(bf16[80,640]{1,0:T(8,128)(2,1)} %amplitude.2), channel_id=1, source_target_pairs={{0,128},{32,160},{64,192},{96,224},{128,0},{160,32},{192,64},{224,... | collective-permute-start | bytes 307208 | tf_op jit(solution)/shard_map/ppermute | solution.py:54
  139.7 2.4 %collective-permute-start.13 = (bf16[80,640]{1,0:T(8,128)(2,1)}, bf16[80,640]{1,0:T(8,128)(2,1)S(1)}, u32[]{:S(2)}, u32[]{:S(2)}) collective-permute-start(bf16[80,640]{1,0:T(8,128)(2,1)} %amplitude.2), channel_id=1, source_target_pairs={{0,64},{32,96},{64,128},{96,160},{128,192},{160,224},{192,0},{224,... | collective-permute-start | bytes 307208 | tf_op jit(solution)/shard_map/ppermute | solution.py:54
  142.1 5.3 %collective-permute-done.26.r3 = bf16[80,640]{1,0:T(8,128)(2,1)S(1)} collective-permute-done((bf16[80,640]{1,0:T(8,128)(2,1)}, bf16[80,640]{1,0:T(8,128)(2,1)S(1)}, u32[]{:S(2)}, u32[]{:S(2)}) %collective-permute-start.26) | collective-permute-done | bytes 102432 | tf_op jit(solution)/shard_map/ppermute | solution.py:54
  148.0 2.0 amplitude.3
  150.0 3.6 %collective-permute-start.28 = (bf16[80,640]{1,0:T(8,128)(2,1)}, bf16[80,640]{1,0:T(8,128)(2,1)S(1)}, u32[]{:S(2)}, u32[]{:S(2)}) collective-permute-start(bf16[80,640]{1,0:T(8,128)(2,1)} %amplitude.3), channel_id=1, source_target_pairs={{0,128},{32,160},{64,192},{96,224},{128,0},{160,32},{192,64},{224,... | collective-permute-start | bytes 307208 | tf_op jit(solution)/shard_map/ppermute | solution.py:54
  153.9 0.9 pad_maximum_fusion.1.refs_0_
  154.9 4.4 %collective-permute-start.16 = (bf16[320,640]{1,0:T(8,128)(2,1)S(1)}, bf16[320,640]{1,0:T(8,128)(2,1)S(1)}, u32[]{:S(2)}, u32[]{:S(2)}) collective-permute-start(bf16[320,640]{1,0:T(8,128)(2,1)S(1)} %pad_maximum_fusion.1.refs_0_), channel_id=1, source_target_pairs={{0,32},{32,0},{64,96},{96,64},{128,160},{160,128},{192,224},{224,1... | collective-permute-start | bytes 1228808 | tf_op jit(solution)/shard_map/ppermute | solution.py:50
  159.3 2.2 %collective-permute-done.27 = bf16[80,640]{1,0:T(8,128)(2,1)S(1)} collective-permute-done((bf16[80,640]{1,0:T(8,128)(2,1)}, bf16[80,640]{1,0:T(8,128)(2,1)S(1)}, u32[]{:S(2)}, u32[]{:S(2)}) %collective-permute-start.27) | collective-permute-done | bytes 102432 | tf_op jit(solution)/shard_map/ppermute | solution.py:54
  161.4 0.9 pad_maximum_fusion.2.refs_2_
  162.4 3.8 %collective-permute-start.30 = (bf16[320,640]{1,0:T(8,128)(2,1)S(1)}, bf16[320,640]{1,0:T(8,128)(2,1)S(1)}, u32[]{:S(2)}, u32[]{:S(2)}) collective-permute-start(bf16[320,640]{1,0:T(8,128)(2,1)S(1)} %pad_maximum_fusion.2.refs_2_), channel_id=1, source_target_pairs={{0,32},{32,0},{64,96},{96,64},{128,160},{160,128},{192,224},{224,1... | collective-permute-start | bytes 1228808 | tf_op jit(solution)/shard_map/ppermute | solution.py:50
  166.2 1.4 collective-permute-done.30.refs_3_
  168.4 6.6 %density.5 = (bf16[80,2560]{1,0:T(8,128)(2,1)}, bf16[80,2560]{1,0:T(8,128)(2,1)}) custom-call(bf16[320,640]{1,0:T(8,128)(2,1)} %copy-done, bf16[320,640]{1,0:T(8,128)(2,1)} %copy-done.2, bf16[320,640]{1,0:T(8,128)(2,1)} %copy-done.1, bf16[320,640]{1,0:T(8,128)(2,1)} %copy-done.3, bf16[640,2560]{1,0:T(8,128)(2,1)} %get-tuple-element.49.refs_4_, ...), custom_call_target="tpu_custom_call" | custom-call | flops 1048576000 | bytes 6553600 | tf_op jit(solution)/shard_map/density/pallas_call | solution.py:296
  175.3 7.6 %density.4 = (bf16[80,2560]{1,0:T(8,128)(2,1)}, f32[80,2560]{1,0:T(8,128)}, f32[80,2560]{1,0:T(8,128)}, bf16[80,2560]{1,0:T(8,128)(2,1)}) custom-call(bf16[320,640]{1,0:T(8,128)(2,1)} %copy-done, bf16[320,640]{1,0:T(8,128)(2,1)} %copy-done.2, bf16[320,640]{1,0:T(8,128)(2,1)} %copy-done.1, bf16[320,640]{1,0:T(8,128)(2,1)} %copy-done.3, ...), custom_call_target="tpu_custom_call" | custom-call | flops 2097152000 | bytes 6553600 | tf_op jit(solution)/shard_map/density/pallas_call | solution.py:296
  182.9 1.5 collective-permute-start.36
  184.4 1.6 collective-permute-start.32
  186.0 7.0 %density.3 = (f32[80,2560]{1,0:T(8,128)}, f32[80,2560]{1,0:T(8,128)}) custom-call(bf16[320,640]{1,0:T(8,128)(2,1)} %copy-done, bf16[320,640]{1,0:T(8,128)(2,1)} %copy-done.2, bf16[320,640]{1,0:T(8,128)(2,1)} %copy-done.1, bf16[320,640]{1,0:T(8,128)(2,1)} %copy-done.3, bf16[640,2560]{1,0:T(8,128)(2,1)} %get-tuple-element.49.refs_4_, ...), custom_call_target="tpu_custom_call" | custom-call | flops 1048576000 | bytes 6553600 | tf_op jit(solution)/shard_map/density/pallas_call | solution.py:296
  193.1 1.4 collective-permute-start.35
  195.2 17.0 %collective-permute-done.35 = bf16[80,2560]{1,0:T(8,128)(2,1)S(1)} collective-permute-done((bf16[80,2560]{1,0:T(8,128)(2,1)S(1)}, bf16[80,2560]{1,0:T(8,128)(2,1)S(1)}, u32[]{:S(2)}, u32[]{:S(2)}) %collective-permute-start.35) | collective-permute-done | bytes 409632 | tf_op jit(solution)/shard_map/ppermute | solution.py:41
  212.5 0.9 pad_maximum_fusion
  (113 shorter events, 8.9 us)
Async XLA Ops:
  1.1 15.6 %collective-permute-start = (bf16[320,512]{1,0:T(8,128)(2,1)S(1)}, bf16[320,512]{1,0:T(8,128)(2,1)S(1)}, u32[]{:S(2)}, u32[]{:S(2)}) collective-permute-start(bf16[320,512]{1,0:T(8,128)(2,1)S(1)} %get-tuple-element.60), channel_id=1, source_target_pairs={{0,32},{32,64},{64,96},{96,128},{128,160},{160,192},{192,224},{1,3... | collective-permute-start | bytes 983048 | tf_op jit(solution)/shard_map/ppermute | solution.py:315
  7.4 12.8 %collective-permute-start.1 = (bf16[320,512]{1,0:T(8,128)(2,1)S(1)}, bf16[320,512]{1,0:T(8,128)(2,1)S(1)}, u32[]{:S(2)}, u32[]{:S(2)}) collective-permute-start(bf16[320,512]{1,0:T(8,128)(2,1)S(1)} %get-tuple-element.59), channel_id=1, source_target_pairs={{32,0},{64,32},{96,64},{128,96},{160,128},{192,160},{224,192},{33,... | collective-permute-start | bytes 983048 | tf_op jit(solution)/shard_map/ppermute | solution.py:316
  26.9 16.9 %collective-permute-start.7 = (bf16[160,2560]{1,0:T(8,128)(2,1)}, bf16[160,2560]{1,0:T(8,128)(2,1)S(1)}, u32[]{:S(2)}, u32[]{:S(2)}) collective-permute-start(bf16[160,2560]{1,0:T(8,128)(2,1)} %get-tuple-element.35.refs_5_), channel_id=1, source_target_pairs={{0,24},{1,25},{2,26},{3,27},{4,28},{5,29},{6,30},{7,31},{8,0},{9,1... | collective-permute-start | bytes 2457608 | tf_op jit(solution)/shard_map/ppermute | solution.py:31
  29.6 16.9 %collective-permute-start.8 = (bf16[160,2560]{1,0:T(8,128)(2,1)}, bf16[160,2560]{1,0:T(8,128)(2,1)S(1)}, u32[]{:S(2)}, u32[]{:S(2)}) collective-permute-start(bf16[160,2560]{1,0:T(8,128)(2,1)} %get-tuple-element.35.refs_5_), channel_id=1, source_target_pairs={{0,6},{1,7},{2,4},{3,5},{4,2},{5,3},{6,0},{7,1},{8,14},{9,15},{10,... | collective-permute-start | bytes 2457608 | tf_op jit(solution)/shard_map/ppermute | solution.py:36
  32.1 17.0 %collective-permute-start.3 = (bf16[160,2560]{1,0:T(8,128)(2,1)}, bf16[160,2560]{1,0:T(8,128)(2,1)S(1)}, u32[]{:S(2)}, u32[]{:S(2)}) collective-permute-start(bf16[160,2560]{1,0:T(8,128)(2,1)} %get-tuple-element.34.refs_0_), channel_id=1, source_target_pairs={{0,1},{1,0},{2,3},{3,2},{4,5},{5,4},{6,7},{7,6},{8,9},{9,8},{10,11... | collective-permute-start | bytes 2457608 | tf_op jit(solution)/shard_map/ppermute | solution.py:46
  32.1 17.1 %collective-permute-start.2 = (bf16[160,2560]{1,0:T(8,128)(2,1)}, bf16[160,2560]{1,0:T(8,128)(2,1)S(1)}, u32[]{:S(2)}, u32[]{:S(2)}) collective-permute-start(bf16[160,2560]{1,0:T(8,128)(2,1)} %get-tuple-element.34.refs_0_), channel_id=1, source_target_pairs={{0,2},{1,3},{2,0},{3,1},{4,6},{5,7},{6,4},{7,5},{8,10},{9,11},{10,... | collective-permute-start | bytes 2457608 | tf_op jit(solution)/shard_map/ppermute | solution.py:41
  43.8 27.0 %copy-start.24 = (bf16[160,2560]{1,0:T(8,128)(2,1)}, bf16[160,2560]{1,0:T(8,128)(2,1)S(1)}, u32[]{:S(2)}) copy-start(bf16[160,2560]{1,0:T(8,128)(2,1)S(1)} %collective-permute-done.7.refs_7_) | copy-start | bytes 2457604
  43.8 15.9 %collective-permute-start.18 = (bf16[160,2560]{1,0:T(8,128)(2,1)S(1)}, bf16[160,2560]{1,0:T(8,128)(2,1)S(1)}, u32[]{:S(2)}, u32[]{:S(2)}) collective-permute-start(bf16[160,2560]{1,0:T(8,128)(2,1)S(1)} %collective-permute-done.7.refs_7_), channel_id=1, source_target_pairs={{0,24},{1,25},{2,26},{3,27},{4,28},{5,29},{6,30},{7,31},{8,0},{9,1... | collective-permute-start | bytes 2457608 | tf_op jit(solution)/shard_map/ppermute | solution.py:31
  46.6 34.4 %copy-start.25 = (bf16[160,2560]{1,0:T(8,128)(2,1)}, bf16[160,2560]{1,0:T(8,128)(2,1)S(1)}, u32[]{:S(2)}) copy-start(bf16[160,2560]{1,0:T(8,128)(2,1)S(1)} %collective-permute-done.8.refs_8_) | copy-start | bytes 2457604
  46.6 21.6 %collective-permute-start.17 = (bf16[160,2560]{1,0:T(8,128)(2,1)S(1)}, bf16[160,2560]{1,0:T(8,128)(2,1)S(1)}, u32[]{:S(2)}, u32[]{:S(2)}) collective-permute-start(bf16[160,2560]{1,0:T(8,128)(2,1)S(1)} %collective-permute-done.8.refs_8_), channel_id=1, source_target_pairs={{0,8},{1,9},{2,10},{3,11},{4,12},{5,13},{6,14},{7,15},{8,16},{9,17... | collective-permute-start | bytes 2457608 | tf_op jit(solution)/shard_map/ppermute | solution.py:31
  46.6 24.1 %collective-permute-start.19 = (bf16[160,2560]{1,0:T(8,128)(2,1)S(1)}, bf16[160,2560]{1,0:T(8,128)(2,1)S(1)}, u32[]{:S(2)}, u32[]{:S(2)}) collective-permute-start(bf16[160,2560]{1,0:T(8,128)(2,1)S(1)} %collective-permute-done.7.refs_7_), channel_id=1, source_target_pairs={{0,6},{1,7},{2,4},{3,5},{4,2},{5,3},{6,0},{7,1},{8,14},{9,15},{10,... | collective-permute-start | bytes 2457608 | tf_op jit(solution)/shard_map/ppermute | solution.py:36
  49.1 21.7 %copy-start.12 = (bf16[160,2560]{1,0:T(8,128)(2,1)}, bf16[160,2560]{1,0:T(8,128)(2,1)S(1)}, u32[]{:S(2)}) copy-start(bf16[160,2560]{1,0:T(8,128)(2,1)S(1)} %collective-permute-done.3.refs_2_) | copy-start | bytes 2457604
  49.1 31.8 %collective-permute-start.6 = (bf16[160,2560]{1,0:T(8,128)(2,1)}, bf16[160,2560]{1,0:T(8,128)(2,1)S(1)}, u32[]{:S(2)}, u32[]{:S(2)}) collective-permute-start(bf16[160,2560]{1,0:T(8,128)(2,1)} %get-tuple-element.35.refs_5_), channel_id=1, source_target_pairs={{0,8},{1,9},{2,10},{3,11},{4,12},{5,13},{6,14},{7,15},{8,16},{9,17... | collective-permute-start | bytes 2457608 | tf_op jit(solution)/shard_map/ppermute | solution.py:31
  49.2 31.8 %copy-start.13 = (bf16[160,2560]{1,0:T(8,128)(2,1)}, bf16[160,2560]{1,0:T(8,128)(2,1)S(1)}, u32[]{:S(2)}) copy-start(bf16[160,2560]{1,0:T(8,128)(2,1)S(1)} %collective-permute-done.2.refs_1_) | copy-start | bytes 2457604
  49.2 31.8 %collective-permute-start.4 = (bf16[80,2560]{1,0:T(8,128)(2,1)S(1)}, bf16[80,2560]{1,0:T(8,128)(2,1)S(1)}, u32[]{:S(2)}, u32[]{:S(2)}) collective-permute-start(bf16[80,2560]{1,0:T(8,128)(2,1)S(1)} %slice.30), channel_id=1, source_target_pairs={{0,2},{1,3},{2,0},{3,1},{4,6},{5,7},{6,4},{7,5},{8,10},{9,11},{10,... | collective-permute-start | bytes 1228808 | tf_op jit(solution)/shard_map/ppermute | solution.py:41
  59.7 32.7 %copy-start.14 = (bf16[160,2560]{1,0:T(8,128)(2,1)}, bf16[160,2560]{1,0:T(8,128)(2,1)S(1)}, u32[]{:S(2)}) copy-start(bf16[160,2560]{1,0:T(8,128)(2,1)S(1)} %collective-permute-done.18.refs_2_) | copy-start | bytes 2457604
  59.7 21.3 %collective-permute-start.5 = (bf16[80,2560]{1,0:T(8,128)(2,1)S(1)}, bf16[80,2560]{1,0:T(8,128)(2,1)S(1)}, u32[]{:S(2)}, u32[]{:S(2)}) collective-permute-start(bf16[80,2560]{1,0:T(8,128)(2,1)S(1)} %slice.31), channel_id=1, source_target_pairs={{0,1},{1,0},{2,3},{3,2},{4,5},{5,4},{6,7},{7,6},{8,9},{9,8},{10,11... | collective-permute-start | bytes 1228808 | tf_op jit(solution)/shard_map/ppermute | solution.py:46
  68.2 24.1 %copy-start.21 = (bf16[160,2560]{1,0:T(8,128)(2,1)}, bf16[160,2560]{1,0:T(8,128)(2,1)S(1)}, u32[]{:S(2)}) copy-start(bf16[160,2560]{1,0:T(8,128)(2,1)S(1)} %collective-permute-done.17.refs_1_) | copy-start | bytes 2457604
  68.2 24.5 %collective-permute-start.20 = (bf16[64,2560]{1,0:T(8,128)(2,1)S(1)}, bf16[64,2560]{1,0:T(8,128)(2,1)}, u32[]{:S(2)}, u32[]{:S(2)}) collective-permute-start(bf16[64,2560]{1,0:T(8,128)(2,1)S(1)} %slice.32), channel_id=1, source_target_pairs={{0,6},{1,7},{2,4},{3,5},{4,2},{5,3},{6,0},{7,1},{8,14},{9,15},{10,... | collective-permute-start | bytes 983048 | tf_op jit(solution)/shard_map/ppermute | solution.py:36
  70.7 21.6 %copy-start.22 = (bf16[160,2560]{1,0:T(8,128)(2,1)}, bf16[160,2560]{1,0:T(8,128)(2,1)S(1)}, u32[]{:S(2)}) copy-start(bf16[160,2560]{1,0:T(8,128)(2,1)S(1)} %collective-permute-done.19.refs_3_) | copy-start | bytes 2457604
  70.7 21.9 %collective-permute-start.21 = (bf16[48,2560]{1,0:T(8,128)(2,1)S(1)}, bf16[48,2560]{1,0:T(8,128)(2,1)}, u32[]{:S(2)}, u32[]{:S(2)}) collective-permute-start(bf16[48,2560]{1,0:T(8,128)(2,1)S(1)} %slice.33), channel_id=1, source_target_pairs={{0,8},{1,9},{2,10},{3,11},{4,12},{5,13},{6,14},{7,15},{8,16},{9,17... | collective-permute-start | bytes 737288 | tf_op jit(solution)/shard_map/ppermute | solution.py:31
  81.0 11.7 %collective-permute-start.22 = (bf16[48,2560]{1,0:T(8,128)(2,1)S(1)}, bf16[48,2560]{1,0:T(8,128)(2,1)S(1)}, u32[]{:S(2)}, u32[]{:S(2)}) collective-permute-start(bf16[48,2560]{1,0:T(8,128)(2,1)S(1)} %slice.34), channel_id=1, source_target_pairs={{0,24},{1,25},{2,26},{3,27},{4,28},{5,29},{6,30},{7,31},{8,0},{9,1... | collective-permute-start | bytes 737288 | tf_op jit(solution)/shard_map/ppermute | solution.py:31
  92.4 9.9 %collective-permute-start.9 = (bf16[320,640]{1,0:T(8,128)(2,1)}, bf16[320,640]{1,0:T(8,128)(2,1)S(1)}, u32[]{:S(2)}, u32[]{:S(2)}) collective-permute-start(bf16[320,640]{1,0:T(8,128)(2,1)} %get-tuple-element.37), channel_id=1, source_target_pairs={{0,32},{32,0},{64,96},{96,64},{128,160},{160,128},{192,224},{224,1... | collective-permute-start | bytes 1228808 | tf_op jit(solution)/shard_map/ppermute | solution.py:50
  101.7 25.7 %copy-start.23 = (f32[5120]{0:T(1024)S(1)}, f32[5120]{0:T(1024)}, u32[]{:S(2)}) copy-start(f32[5120]{0:T(1024)} %param.9) | copy-start | bytes 61444
  101.7 22.7 %collective-permute-start.23 = (bf16[320,640]{1,0:T(8,128)(2,1)}, bf16[320,640]{1,0:T(8,128)(2,1)S(1)}, u32[]{:S(2)}, u32[]{:S(2)}) collective-permute-start(bf16[320,640]{1,0:T(8,128)(2,1)} %get-tuple-element.44), channel_id=1, source_target_pairs={{0,32},{32,0},{64,96},{96,64},{128,160},{160,128},{192,224},{224,1... | collective-permute-start | bytes 1228808 | tf_op jit(solution)/shard_map/ppermute | solution.py:50
  105.1 25.0 %collective-permute-start.10 = (bf16[80,640]{1,0:T(8,128)(2,1)}, bf16[80,640]{1,0:T(8,128)(2,1)S(1)}, u32[]{:S(2)}, u32[]{:S(2)}) collective-permute-start(bf16[80,640]{1,0:T(8,128)(2,1)} %get-tuple-element.39), channel_id=1, source_target_pairs={{0,64},{32,96},{64,128},{96,160},{128,192},{160,224},{192,0},{224,... | collective-permute-start | bytes 307208 | tf_op jit(solution)/shard_map/ppermute | solution.py:54
  113.8 17.9 %collective-permute-start.11 = (bf16[80,640]{1,0:T(8,128)(2,1)}, bf16[80,640]{1,0:T(8,128)(2,1)S(1)}, u32[]{:S(2)}, u32[]{:S(2)}) collective-permute-start(bf16[80,640]{1,0:T(8,128)(2,1)} %get-tuple-element.40), channel_id=1, source_target_pairs={{0,128},{32,160},{64,192},{96,224},{128,0},{160,32},{192,64},{224,... | collective-permute-start | bytes 307208 | tf_op jit(solution)/shard_map/ppermute | solution.py:54
  120.8 10.9 %collective-permute-start.12 = (bf16[80,640]{1,0:T(8,128)(2,1)}, bf16[80,640]{1,0:T(8,128)(2,1)S(1)}, u32[]{:S(2)}, u32[]{:S(2)}) collective-permute-start(bf16[80,640]{1,0:T(8,128)(2,1)} %get-tuple-element.41), channel_id=1, source_target_pairs={{0,192},{32,224},{64,0},{96,32},{128,64},{160,96},{192,128},{224,1... | collective-permute-start | bytes 307208 | tf_op jit(solution)/shard_map/ppermute | solution.py:54
  127.3 12.4 %collective-permute-start.24 = (bf16[80,640]{1,0:T(8,128)(2,1)}, bf16[80,640]{1,0:T(8,128)(2,1)S(1)}, u32[]{:S(2)}, u32[]{:S(2)}) collective-permute-start(bf16[80,640]{1,0:T(8,128)(2,1)} %get-tuple-element.46), channel_id=1, source_target_pairs={{0,64},{32,96},{64,128},{96,160},{128,192},{160,224},{192,0},{224,... | collective-permute-start | bytes 307208 | tf_op jit(solution)/shard_map/ppermute | solution.py:54
  128.0 14.0 %collective-permute-start.25 = (bf16[80,640]{1,0:T(8,128)(2,1)}, bf16[80,640]{1,0:T(8,128)(2,1)S(1)}, u32[]{:S(2)}, u32[]{:S(2)}) collective-permute-start(bf16[80,640]{1,0:T(8,128)(2,1)} %get-tuple-element.47), channel_id=1, source_target_pairs={{0,128},{32,160},{64,192},{96,224},{128,0},{160,32},{192,64},{224,... | collective-permute-start | bytes 307208 | tf_op jit(solution)/shard_map/ppermute | solution.py:54
  130.1 17.2 %collective-permute-start.26 = (bf16[80,640]{1,0:T(8,128)(2,1)}, bf16[80,640]{1,0:T(8,128)(2,1)S(1)}, u32[]{:S(2)}, u32[]{:S(2)}) collective-permute-start(bf16[80,640]{1,0:T(8,128)(2,1)} %get-tuple-element.48), channel_id=1, source_target_pairs={{0,192},{32,224},{64,0},{96,32},{128,64},{160,96},{192,128},{224,1... | collective-permute-start | bytes 307208 | tf_op jit(solution)/shard_map/ppermute | solution.py:54
  134.4 19.2 %collective-permute-start.15 = (bf16[80,640]{1,0:T(8,128)(2,1)}, bf16[80,640]{1,0:T(8,128)(2,1)S(1)}, u32[]{:S(2)}, u32[]{:S(2)}) collective-permute-start(bf16[80,640]{1,0:T(8,128)(2,1)} %amplitude.2), channel_id=1, source_target_pairs={{0,192},{32,224},{64,0},{96,32},{128,64},{160,96},{192,128},{224,1... | collective-permute-start | bytes 307208 | tf_op jit(solution)/shard_map/ppermute | solution.py:54
  136.4 17.5 %collective-permute-start.14 = (bf16[80,640]{1,0:T(8,128)(2,1)}, bf16[80,640]{1,0:T(8,128)(2,1)S(1)}, u32[]{:S(2)}, u32[]{:S(2)}) collective-permute-start(bf16[80,640]{1,0:T(8,128)(2,1)} %amplitude.2), channel_id=1, source_target_pairs={{0,128},{32,160},{64,192},{96,224},{128,0},{160,32},{192,64},{224,... | collective-permute-start | bytes 307208 | tf_op jit(solution)/shard_map/ppermute | solution.py:54
  139.7 14.2 %collective-permute-start.13 = (bf16[80,640]{1,0:T(8,128)(2,1)}, bf16[80,640]{1,0:T(8,128)(2,1)S(1)}, u32[]{:S(2)}, u32[]{:S(2)}) collective-permute-start(bf16[80,640]{1,0:T(8,128)(2,1)} %amplitude.2), channel_id=1, source_target_pairs={{0,64},{32,96},{64,128},{96,160},{128,192},{160,224},{192,0},{224,... | collective-permute-start | bytes 307208 | tf_op jit(solution)/shard_map/ppermute | solution.py:54
  150.0 9.3 %collective-permute-start.29 = (bf16[80,640]{1,0:T(8,128)(2,1)}, bf16[80,640]{1,0:T(8,128)(2,1)S(1)}, u32[]{:S(2)}, u32[]{:S(2)}) collective-permute-start(bf16[80,640]{1,0:T(8,128)(2,1)} %amplitude.3), channel_id=1, source_target_pairs={{0,192},{32,224},{64,0},{96,32},{128,64},{160,96},{192,128},{224,1... | collective-permute-start | bytes 307208 | tf_op jit(solution)/shard_map/ppermute | solution.py:54
  150.0 9.3 %collective-permute-start.28 = (bf16[80,640]{1,0:T(8,128)(2,1)}, bf16[80,640]{1,0:T(8,128)(2,1)S(1)}, u32[]{:S(2)}, u32[]{:S(2)}) collective-permute-start(bf16[80,640]{1,0:T(8,128)(2,1)} %amplitude.3), channel_id=1, source_target_pairs={{0,128},{32,160},{64,192},{96,224},{128,0},{160,32},{192,64},{224,... | collective-permute-start | bytes 307208 | tf_op jit(solution)/shard_map/ppermute | solution.py:54
  153.6 7.9 %collective-permute-start.27 = (bf16[80,640]{1,0:T(8,128)(2,1)}, bf16[80,640]{1,0:T(8,128)(2,1)S(1)}, u32[]{:S(2)}, u32[]{:S(2)}) collective-permute-start(bf16[80,640]{1,0:T(8,128)(2,1)} %amplitude.3), channel_id=1, source_target_pairs={{0,64},{32,96},{64,128},{96,160},{128,192},{160,224},{192,0},{224,... | collective-permute-start | bytes 307208 | tf_op jit(solution)/shard_map/ppermute | solution.py:54
  154.9 12.7 %copy-start = (bf16[320,640]{1,0:T(8,128)(2,1)}, bf16[320,640]{1,0:T(8,128)(2,1)S(1)}, u32[]{:S(2)}) copy-start(bf16[320,640]{1,0:T(8,128)(2,1)S(1)} %pad_maximum_fusion.1.refs_0_) | copy-start | bytes 1228804
  154.9 11.4 %collective-permute-start.16 = (bf16[320,640]{1,0:T(8,128)(2,1)S(1)}, bf16[320,640]{1,0:T(8,128)(2,1)S(1)}, u32[]{:S(2)}, u32[]{:S(2)}) collective-permute-start(bf16[320,640]{1,0:T(8,128)(2,1)S(1)} %pad_maximum_fusion.1.refs_0_), channel_id=1, source_target_pairs={{0,32},{32,0},{64,96},{96,64},{128,160},{160,128},{192,224},{224,1... | collective-permute-start | bytes 1228808 | tf_op jit(solution)/shard_map/ppermute | solution.py:50
  162.4 5.2 %collective-permute-start.30 = (bf16[320,640]{1,0:T(8,128)(2,1)S(1)}, bf16[320,640]{1,0:T(8,128)(2,1)S(1)}, u32[]{:S(2)}, u32[]{:S(2)}) collective-permute-start(bf16[320,640]{1,0:T(8,128)(2,1)S(1)} %pad_maximum_fusion.2.refs_2_), channel_id=1, source_target_pairs={{0,32},{32,0},{64,96},{96,64},{128,160},{160,128},{192,224},{224,1... | collective-permute-start | bytes 1228808 | tf_op jit(solution)/shard_map/ppermute | solution.py:50
  175.0 18.0 %collective-permute-start.34 = (bf16[80,2560]{1,0:T(8,128)(2,1)}, bf16[80,2560]{1,0:T(8,128)(2,1)S(1)}, u32[]{:S(2)}, u32[]{:S(2)}) collective-permute-start(bf16[80,2560]{1,0:T(8,128)(2,1)} %get-tuple-element.57), channel_id=1, source_target_pairs={{0,1},{1,0},{2,3},{3,2},{4,5},{5,4},{6,7},{7,6},{8,9},{9,8},{10,11... | collective-permute-start | bytes 1228808 | tf_op jit(solution)/shard_map/ppermute | solution.py:46
  182.9 12.3 %collective-permute-start.36 = (bf16[80,2560]{1,0:T(8,128)(2,1)}, bf16[80,2560]{1,0:T(8,128)(2,1)S(1)}, u32[]{:S(2)}, u32[]{:S(2)}) collective-permute-start(bf16[80,2560]{1,0:T(8,128)(2,1)} %get-tuple-element.58), channel_id=1, source_target_pairs={{0,1},{1,0},{2,3},{3,2},{4,5},{5,4},{6,7},{7,6},{8,9},{9,8},{10,11... | collective-permute-start | bytes 1228808 | tf_op jit(solution)/shard_map/ppermute | solution.py:46
  184.4 10.3 %collective-permute-start.32 = (bf16[80,2560]{1,0:T(8,128)(2,1)S(1)}, bf16[80,2560]{1,0:T(8,128)(2,1)S(1)}, u32[]{:S(2)}, u32[]{:S(2)}) collective-permute-start(bf16[80,2560]{1,0:T(8,128)(2,1)S(1)} %copy-done.29), channel_id=1, source_target_pairs={{0,2},{1,3},{2,0},{3,1},{4,6},{5,7},{6,4},{7,5},{8,10},{9,11},{10,... | collective-permute-start | bytes 1228808 | tf_op jit(solution)/shard_map/ppermute | solution.py:41
  185.9 26.4 %collective-permute-start.31 = (bf16[80,2560]{1,0:T(8,128)(2,1)}, bf16[80,2560]{1,0:T(8,128)(2,1)S(1)}, u32[]{:S(2)}, u32[]{:S(2)}) collective-permute-start(bf16[80,2560]{1,0:T(8,128)(2,1)} %get-tuple-element.52), channel_id=1, source_target_pairs={{0,2},{1,3},{2,0},{3,1},{4,6},{5,7},{6,4},{7,5},{8,10},{9,11},{10,... | collective-permute-start | bytes 1228808 | tf_op jit(solution)/shard_map/ppermute | solution.py:41
  193.0 19.2 %copy-start.7 = (f32[80,2560]{1,0:T(8,128)S(1)}, f32[80,2560]{1,0:T(8,128)}, u32[]{:S(2)}) copy-start(f32[80,2560]{1,0:T(8,128)} %get-tuple-element.55) | copy-start | bytes 2457604
  193.1 19.1 %collective-permute-start.35 = (bf16[80,2560]{1,0:T(8,128)(2,1)S(1)}, bf16[80,2560]{1,0:T(8,128)(2,1)S(1)}, u32[]{:S(2)}, u32[]{:S(2)}) collective-permute-start(bf16[80,2560]{1,0:T(8,128)(2,1)S(1)} %add_convert_fusion.1), channel_id=1, source_target_pairs={{0,2},{1,3},{2,0},{3,1},{4,6},{5,7},{6,4},{7,5},{8,10},{9,11},{10,... | collective-permute-start | bytes 1228808 | tf_op jit(solution)/shard_map/ppermute | solution.py:41
  194.6 17.7 %copy-start.6 = (f32[80,2560]{1,0:T(8,128)S(1)}, f32[80,2560]{1,0:T(8,128)}, u32[]{:S(2)}) copy-start(f32[80,2560]{1,0:T(8,128)} %get-tuple-element.51) | copy-start | bytes 2457604
  194.7 17.6 %collective-permute-start.33 = (bf16[80,2560]{1,0:T(8,128)(2,1)S(1)}, bf16[80,2560]{1,0:T(8,128)(2,1)S(1)}, u32[]{:S(2)}, u32[]{:S(2)}) collective-permute-start(bf16[80,2560]{1,0:T(8,128)(2,1)S(1)} %add_convert_fusion.3), channel_id=1, source_target_pairs={{0,1},{1,0},{2,3},{3,2},{4,5},{5,4},{6,7},{7,6},{8,9},{9,8},{10,11... | collective-permute-start | bytes 1228808 | tf_op jit(solution)/shard_map/ppermute | solution.py:46
  (20 other events, 51.1 us)

commit v3 on v0

v3 whole, which is shorter than its diff:
```python
import functools

import jax
import jax.numpy as jnp
from jax import lax
from jax.experimental import pallas as pl
from jax.experimental.pallas import tpu as pltpu
from jax.sharding import PartitionSpec as P

TILE = 128
HB = 4
BAND = 2 * HB + 1
ROWS = 160
AUX = 2560
HALO = HB * TILE
bf16 = jnp.bfloat16
f32 = jnp.float32
MIB = 1 << 20


def blk_index(y, x, z):
    return ((y % 4) * 4 + x) * 2 + z


PLACES = [(y, x, z) for y in range(4) for x in range(4) for z in range(2)]
OUTER = (3, 2, 1, 0)


def send_y(v, step):
    pairs = [(blk_index(y, x, z), blk_index(y + step, x, z)) for y, x, z in PLACES]
    return lax.ppermute(v, "blk", pairs)


def send_outer(v):
    pairs = [(blk_index(y, x, z), blk_index(y, OUTER[x], z)) for y, x, z in PLACES]
    return lax.ppermute(v, "blk", pairs)


def send_inner(v):
    pairs = [(blk_index(y, x, z), blk_index(y, x ^ 1, z)) for y, x, z in PLACES]
    return lax.ppermute(v, "blk", pairs)


def send_z(v):
    pairs = [(blk_index(y, x, z), blk_index(y, x, 1 - z)) for y, x, z in PLACES]
    return lax.ppermute(v, "blk", pairs)


def send_core(v):
    return lax.ppermute(v, "grp", [(g, g ^ 1) for g in range(8)])


def send_high(v, step):
    return lax.ppermute(v, "grp", [(g, (g + 2 * step) % 8) for g in range(8)])


def params(mib=40):
    return pltpu.CompilerParams(vmem_limit_bytes=mib * MIB)


def cost(flops, nbytes):
    return pl.CostEstimate(flops=int(flops), bytes_accessed=int(nbytes), transcendentals=0)


def position():
    group = lax.axis_index("grp").astype(jnp.int32)
    me = lax.axis_index("blk").astype(jnp.int32)
    return group // 2, group % 2, me // 8, (me // 2) % 4, me % 2


ANY = pl.BlockSpec(memory_space=pl.ANY)
VMEM = pl.BlockSpec(memory_space=pltpu.VMEM)
SMEM = pl.BlockSpec(memory_space=pltpu.SMEM)
DMA = pltpu.SemaphoreType.DMA
HALF = ROWS // 2
SHARE = ROWS // 2
WIDE = 4 * ROWS
K2 = AUX // 2


def hbm(shape, dtype=bf16):
    return jax.ShapeDtypeStruct(shape, dtype)


def vmem(shape, dtype=bf16):
    return pltpu.VMEM(shape, dtype)


def call(kernel, args, outs, scratch=(), name=None, flops=1e6, nbytes=1e6, aliases=None, mib=40):
    return pl.pallas_call(
        kernel,
        in_specs=[spec for _, spec in args],
        out_specs=[VMEM] * len(outs),
        out_shape=list(outs),
        scratch_shapes=list(scratch),
        input_output_aliases=aliases or {},
        compiler_params=params(mib),
        cost_estimate=cost(flops, nbytes),
        name=name,
    )(*[a for a, _ in args])


INNER = (2, 3, 4, 5, 6, 7)
EDGE = (0, 1, 8, 9)


def fit_inner_kernel(index, own_in, tiles_in, _, a, b, own, edge, tiles, weights, own_sem, sems):
    own_copies = [
        pltpu.make_async_copy(
            own_in.at[pl.ds(i * ROWS, ROWS)], own.at[pl.ds(i * ROWS, ROWS)], own_sem.at[i]
        )
        for i in range(2)
    ]
    copies = {}
    for p in INNER + EDGE:
        part = pl.ds(p * 2 * BAND, 2 * BAND)
        copies[p] = pltpu.make_async_copy(tiles_in.at[part], tiles.at[part], sems.at[p])
    copies[INNER[0]].start()
    for c in own_copies:
        c.start()
    for p in (INNER + EDGE)[1:]:
        copies[p].start()
    zero = jnp.zeros((TILE, TILE), bf16)

    def build(p, out):
        out[:TILE, TILE:] = zero
        out[BAND * TILE :, :TILE] = zero
        for q in range(2):
            for o in range(BAND):
                slot = p * 2 * BAND + q * BAND + o
                at = (q + o) * TILE
                out[at : at + TILE, q * TILE : (q + 1) * TILE] = jnp.where(
                    index[1, slot] == 1, tiles[slot], zero
                )

    for p in INNER:
        copies[p].wait()
        if p == INNER[0]:
            for c in own_copies:
                c.wait()
        build(p, weights)
        window = own[:, (2 * p - HB) * TILE : (2 * p + HB + 2) * TILE]
        fitted = jnp.dot(window, weights[...], preferred_element_type=f32).astype(bf16)
        columns = slice(p * 2 * TILE, (p + 1) * 2 * TILE)
        a[:, columns] = fitted[:ROWS]
        b[:, columns] = fitted[ROWS:]
    for n, p in enumerate(EDGE):
        copies[p].wait()
        build(p, edge.at[n])


def fit_edge_kernel(left, right, own, edge, _, __, a, b, ext):
    ext[:, :HALO] = left[...]
    ext[:, HALO : 3 * HALO] = own[:, : 2 * HALO]
    ext[:, 3 * HALO : 5 * HALO] = own[:, AUX - 2 * HALO :]
    ext[:, 5 * HALO :] = right[...]
    for n, p in enumerate(EDGE):
        at = (0, 2, 12, 14)[n] * TILE
        window = ext[:, at : at + (BAND + 1) * TILE]
        fitted = jnp.dot(window, edge[n], preferred_element_type=f32).astype(bf16)
        columns = slice(p * 2 * TILE, (p + 1) * 2 * TILE)
        a[:, columns] = fitted[:ROWS]
        b[:, columns] = fitted[ROWS:]


def fit(index, own, tiles, left, right, early):
    banded = ((BAND + 1) * TILE, 2 * TILE)
    a, b, own, edge = call(
        fit_inner_kernel,
        [(index, SMEM), (own, ANY), (tiles, ANY), (early, ANY)],
        [vmem((ROWS, AUX)), vmem((ROWS, AUX)), vmem((2 * ROWS, AUX)), vmem((4, *banded))],
        [pltpu.VMEM(tiles.shape, bf16), pltpu.VMEM(banded, bf16), DMA((2,)), DMA((10,))],
        name="fit_inner",
        mib=56,
        flops=1.2e9,
        nbytes=9e6,
    )
    return call(
        fit_edge_kernel,
        [(v, VMEM) for v in (left, right, own, edge, a, b)],
        [vmem((ROWS, AUX))] * 2,
        [pltpu.VMEM((2 * ROWS, 6 * HALO), bf16)],
        name="fit_edge",
        flops=8e8,
        aliases={4: 0, 5: 1},
    )


def cut(parts, after=(), name=None):
    def kernel(*refs):
        ins, outs, sems = refs[: len(parts)], refs[-1 - len(parts) : -1], refs[-1]
        copies = [
            pltpu.make_async_copy(i.at[pl.ds(at, n)], o, sems.at[j])
            for j, (i, o, (_, at, n)) in enumerate(zip(ins, outs, parts))
        ]
        for c in copies:
            c.start()
        for c in copies:
            c.wait()

    return pl.pallas_call(
        kernel,
        in_specs=[ANY] * (len(parts) + len(after)),
        out_specs=[ANY] * len(parts),
        out_shape=[hbm((n, AUX)) for _, _, n in parts],
        scratch_shapes=[DMA((len(parts),))],
        compiler_params=params(),
        cost_estimate=cost(1e5, 2e6),
        name=name,
    )(*[v for v, _, _ in parts], *after)


def row_copies(parts, out, sems, offsets):
    copies = []
    for h in range(2):
        columns = pl.ds(h * K2, K2)
        copies.append(
            [
                pltpu.make_async_copy(
                    p.at[:, columns], out.at[pl.ds(at, p.shape[0]), columns], sems.at[i, h]
                )
                for i, (p, at) in enumerate(zip(parts, offsets))
            ]
        )
    return copies


def b_offsets(parts, at=0):
    offsets = []
    for p in parts:
        offsets.append(at)
        at += p.shape[0]
    return offsets


def products(acat, bcat, rows, copies):
    total = None
    for h in range(2):
        for c in copies[h]:
            c.wait()
        columns = slice(h * K2, (h + 1) * K2)
        part = lax.dot_general(
            acat[:, columns], bcat[rows, columns], (((1,), (1,)), ((), ())),
            preferred_element_type=f32,
        )
        total = part if total is None else total + part
    return total


def pair_first_kernel(*refs):
    a_refs, b_refs = refs[:5], refs[5:9]
    keep, send, bcat, acat, a_sems, b_sems = refs[9:]
    core = position()[1]
    first = pl.multiple_of(core * (2 * ROWS), 2 * ROWS)
    second = pl.multiple_of((1 - core) * (2 * ROWS), 2 * ROWS)
    a_at = (first, first + ROWS, second, second + ROWS, second + ROWS + HALF)
    a_copies = row_copies(a_refs, acat, a_sems, a_at)
    b_copies = row_copies(b_refs, bcat, b_sems, b_offsets(b_refs))
    copies = [x + y for x, y in zip(a_copies, b_copies)]
    for half in copies:
        for c in half:
            c.start()
    total = products(acat, bcat, slice(0, WIDE), copies)
    keep[...] = total[: 2 * ROWS]
    send[...] = total[2 * ROWS :].astype(bf16)


def pair_first(a_parts, b_parts):
    return call(
        pair_first_kernel,
        [(v, ANY) for v in (*a_parts, *b_parts)],
        [
            vmem((2 * ROWS, WIDE), f32),
            hbm((2 * ROWS, WIDE)),
            vmem((WIDE, AUX)),
            vmem((WIDE, AUX)),
        ],
        [DMA((5, 2)), DMA((4, 2))],
        name="pair_first",
        flops=2 * WIDE * WIDE * AUX,
        nbytes=8e6,
    )


def pair_early_kernel(acat, *refs):
    b_refs = refs[:3]
    total, bcat, sems = refs[-3:]
    copies = row_copies(b_refs, bcat, sems, b_offsets(b_refs))
    for half in copies:
        for c in half:
            c.start()
    total[...] = products(acat, bcat, slice(0, 3 * ROWS), copies)


def pair_early(acat, b_parts):
    return call(
        pair_early_kernel,
        [(acat, VMEM)] + [(v, ANY) for v in b_parts],
        [vmem((WIDE, 3 * ROWS), f32), vmem((WIDE, AUX))],
        [DMA((3, 2))],
        name="pair_early",
        flops=2 * WIDE * 3 * ROWS * AUX,
        nbytes=4e6,
    )


def pair_late_kernel(acat, early, bcat_in, *refs):
    b_refs = refs[:3]
    keep, send, bcat, sems = refs[-4:]
    copies = row_copies(b_refs, bcat, sems, b_offsets(b_refs, 3 * ROWS))
    for half in copies:
        for c in half:
            c.start()
    columns = slice(0, 3 * ROWS)
    keep[:, columns] = early[: 2 * ROWS]
    send[:, columns] = early[2 * ROWS :].astype(bf16)
    total = products(acat, bcat, slice(3 * ROWS, WIDE), copies)
    columns = slice(3 * ROWS, WIDE)
    keep[:, columns] = total[: 2 * ROWS]
    send[:, columns] = total[2 * ROWS :].astype(bf16)


def pair_late(acat, early, bcat, b_parts, after):
    return call(
        pair_late_kernel,
        [(acat, VMEM), (early, VMEM), (bcat, VMEM)] + [(v, ANY) for v in (*b_parts, *after)],
        [vmem((2 * ROWS, WIDE), f32), hbm((2 * ROWS, WIDE)), vmem((WIDE, AUX))],
        [DMA((3, 2))],
        name="pair_late",
        flops=2 * WIDE * ROWS * AUX,
        nbytes=2e6,
        aliases={2: 2},
    )


def core_sum_kernel(keep, got_in, *refs):
    own, s1, s2, s3, got, sem = refs[-6:]
    copy = pltpu.make_async_copy(got_in, got, sem)
    copy.start()
    copy.wait()
    high = position()[0]
    for step, out in enumerate((own, s1, s2, s3)):
        at = pl.multiple_of(((high + step) % 4) * SHARE, SHARE)
        value = keep[pl.ds(at, SHARE)] + got[pl.ds(at, SHARE)].astype(f32)
        out[...] = value.astype(out.dtype)


def core_sum(keep, got, after):
    width = keep.shape[1]
    return call(
        core_sum_kernel,
        [(keep, VMEM), (got, ANY)] + [(v, ANY) for v in after],
        [vmem((SHARE, width), f32)] + [hbm((SHARE, width))] * 3,
        [pltpu.VMEM(got.shape, bf16), DMA(())],
        name="core_sum",
    )


def amplitude_kernel(vir, occ, chosen, own, *refs, offsets):
    arrived, out, got, sems = refs[:3], refs[-3], refs[-2], refs[-1]
    copies = [
        pltpu.make_async_copy(r, got.at[i], sems.at[i]) for i, r in enumerate(arrived)
    ]
    for c in copies:
        c.start()
    high, core, y, x, z = position()
    occ_total = occ[chosen[0]] + occ[chosen[1]]
    inner = x + 1 - 2 * (x % 2)
    row_x = jnp.where(high < 2, x, inner)
    row_z = jnp.where(core == 0, z, 1 - z)
    block = vir[pl.ds((y * 4 + row_x) * 2 + row_z, 1), :]
    lane = lax.broadcasted_iota(jnp.int32, (SHARE, ROWS), 1)
    row = lax.broadcasted_iota(jnp.int32, (SHARE, ROWS), 0)
    own_lane = lane == row + (high % 2) * SHARE
    rows = jnp.sum(jnp.where(own_lane, block, 0.0), axis=1, keepdims=True)
    columns = jnp.concatenate(
        [
            vir[pl.ds((((y + step) % 4) * 4 + (3 - x if away else x)) * 2 + z, 1), :]
            for step, away in offsets
        ],
        axis=1,
    )
    denominator = (rows + columns) - occ_total
    for c in copies:
        c.wait()
    total = own[...]
    for i in range(3):
        total = total + got[i].astype(f32)
    out[...] = (total / denominator).astype(bf16)


def amplitude(vir, occ, chosen, own, arrived, offsets, after=()):
    return call(
        functools.partial(amplitude_kernel, offsets=offsets),
        [(vir, VMEM), (occ, SMEM), (chosen, SMEM), (own, VMEM)]
        + [(v, ANY) for v in (*arrived, *after)],
        [hbm(own.shape)],
        [pltpu.VMEM((3, *own.shape), bf16), DMA((3,))],
        name="amplitude",
    )[0]


def density_part(tcat, b1, b2, blocks, outs):
    rows = slice(blocks[0] * ROWS, blocks[1] * ROWS)
    for h in range(2):
        columns = slice(h * K2, (h + 1) * K2)
        value = jnp.dot(tcat[rows, :WIDE], b1[:, columns], preferred_element_type=f32)
        value += jnp.dot(tcat[rows, WIDE:], b2[:, columns], preferred_element_type=f32)
        for i, out in enumerate(outs):
            out[:, columns] = value[i * HALF : (i + 1) * HALF].astype(out.dtype)


def density_first_kernel(*refs):
    mine, other = (refs[0:4], refs[4:8]), refs[8:10]
    b1, b2, o1, o2, tcat, sems = refs[10:]
    high, core = position()[:2]
    copies = []
    for k in range(4):
        at = ((high - k + 4) % 4) * SHARE
        here = pl.multiple_of(core * (2 * ROWS) + at, SHARE)
        there = pl.multiple_of((1 - core) * (2 * ROWS) + at, SHARE)
        for piece in range(2):
            columns = pl.ds(piece * WIDE, WIDE)
            copies.append(
                pltpu.make_async_copy(
                    mine[piece][k], tcat.at[pl.ds(here, SHARE), columns], sems.at[piece, k, 0]
                )
            )
            copies.append(
                pltpu.make_async_copy(
                    other[piece].at[pl.ds(k * SHARE, SHARE)],
                    tcat.at[pl.ds(there, SHARE), columns],
                    sems.at[piece, k, 1],
                )
            )
    for c in copies:
        c.start()
    for c in copies:
        c.wait()
    density_part(tcat, b1, b2, (3, 4), (o1, o2))


def density_first(mine, other, b1, b2):
    return call(
        density_first_kernel,
        [(v, ANY) for v in (*mine[0], *mine[1], *other)] + [(b1, VMEM), (b2, VMEM)],
        [hbm((HALF, AUX))] * 2 + [vmem((WIDE, 2 * WIDE))],
        [DMA((2, 4, 2))],
        name="density_first",
        flops=2 * ROWS * 2 * WIDE * AUX,
    )


def density(tcat, b1, b2, blocks, types):
    def kernel(tcat, b1, b2, *outs):
        density_part(tcat, b1, b2, blocks, outs)

    return call(
        kernel,
        [(tcat, VMEM), (b1, VMEM), (b2, VMEM)],
        [hbm((HALF, AUX), t) for t in types],
        name="density",
        flops=2 * (blocks[1] - blocks[0]) * ROWS * 2 * WIDE * AUX,
    )


def local(integrals, tiles, tile_index, vir_energy, occ_energy, pair_index):
    window = integrals.reshape(2 * ROWS, AUX)
    vir = vir_energy.reshape(-1, ROWS)
    up = [(g, g + 1) for g in range(7)]
    down = [(g + 1, g) for g in range(7)]
    left = lax.ppermute(window[:, AUX - HALO :], "grp", up)
    right = lax.ppermute(window[:, :HALO], "grp", down)
    a, b = fit(tile_index.T, window, tiles, left, right, vir)

    with jax.named_scope("first"):
        bm = send_y(b, 1)
        bp = send_y(b, -1)
        bo = send_outer(b)
        ax = send_inner(a)
        az = send_z(a)
    az1, ax2 = cut([(az, 0, HALF), (ax, HALF, HALF)], (bm, bp, bo), name="cut_a")
    with jax.named_scope("second"):
        d1 = send_inner(az1)
        d2 = send_z(ax2)
        bom = send_y(bo, 1)
        b2 = send_y(bp, -1)
        bop = send_outer(bp)

    def core_total(keep, send, after=()):
        with jax.named_scope("core"):
            return core_sum(keep, send_core(send), after)

    def shares(s):
        with jax.named_scope("shares"):
            return [send_high(v, k + 1) for k, v in enumerate(s)]

    def spread(mine):
        with jax.named_scope("spread"):
            return [mine] + [send_high(mine, k) for k in (1, 2, 3)]

    def other_core(mine):
        with jax.named_scope("other"):
            return send_core(jnp.concatenate(mine, axis=0))

    keep, send, b_first, acat = pair_first((a, ax, az, d1, d2), (b, bm, bp, bo))
    own, *s = core_total(keep, send)
    arrived = shares(s)
    c1, c2, c3 = cut([(b2, 0, 64), (bom, 64, 48), (bop, 112, 48)], (own,), name="cut_b")
    with jax.named_scope("third"):
        c1 = send_outer(c1)
        c2 = send_y(c2, 1)
        c3 = send_y(c3, -1)
    early, b_second = pair_early(acat, (bom, b2, bop))
    offsets = ((0, 0), (3, 0), (1, 0), (0, 1))
    mine1 = amplitude(vir, occ_energy, pair_index, own, arrived, offsets, (early,))
    keep, send, b_second = pair_late(acat, early, b_second, (c1, c2, c3), (mine1,))
    mine1 = spread(mine1)
    own, *s = core_total(keep, send, (mine1[1], mine1[3]))
    arrived = shares(s)
    offsets = ((3, 1), (2, 0), (1, 1), (2, 1))
    mine2 = spread(amplitude(vir, occ_energy, pair_index, own, arrived, offsets))
    other = (other_core(mine1), other_core(mine2))

    to_d1, to_d2, tcat = density_first((mine1, mine2), other, b_first, b_second)
    x1, x2, z1, z2 = density(tcat, b_first, b_second, (1, 3), (bf16, f32, f32, bf16))
    o1, o2 = density(tcat, b_first, b_second, (0, 1), (f32, f32))
    with jax.named_scope("out"):
        from_x = send_inner(to_d1)
        from_z = send_z(to_d2)
        got_x1 = send_inner(x1)
        got_z2 = send_z(z2)
        got_z1 = send_z((z1 + from_x.astype(f32)).astype(bf16))
        got_x2 = send_inner((x2 + from_z.astype(f32)).astype(bf16))
    h1 = o1 + got_x1.astype(f32) + got_z1.astype(f32)
    h2 = o2 + got_x2.astype(f32) + got_z2.astype(f32)
    return jnp.concatenate([h1, h2], axis=0).astype(bf16)


def solution(mesh):
    in_specs = (P(None, "blk", "grp"), P("grp", None, None), P("grp", None), P(), P(), P())
    return jax.shard_map(
        local, mesh=mesh, in_specs=in_specs, out_specs=P("blk", "grp"), check_vma=False
    )
```

time: 763 us -> 179 us (0.23)
  waiting for transfers between devices: 656 us -> 85.3 us
  matrix products: 53.8 us -> 0 us
  starting transfers between devices: 8.43 us -> 61.3 us
  Pallas kernels: 0 us -> 26.8 us
  between operations: 18.6 us -> 0.28 us
  local copies, waits for them, and re-layouts: 17.6 us -> 3.37 us
    all_gather x1 -> x0, waiting for transfers between devices: 566 us -> none  [local(): partner_all = lax.all_gather(partner, 'blk', axis=0, tiled=True)]
    psum x1 -> x0, waiting for transfers between devices: 90.5 us -> none  [local(): pair_sum = lax.psum(partial_value, 'grp')]
    ppermute x2 -> x37, waiting for transfers between devices: 0.01 us -> 85.3 us  [the longest x12 24.7 us: send_high(): return lax.ppermute(v, 'grp', [(g, (g + 2 * step) % 8) for g in range(8)])]
    dot_general x11 -> x0, matrix products: 53.8 us -> none  [the longest x9 23.8 us: fit_window(): jnp.einsum('xck,ckn->xcn', shifted, grouped[:, offset], preferred_element...]
    ppermute x2 -> x37, starting transfers between devices: 8.21 us -> 61.3 us  [the longest x12 27.1 us: send_high(): return lax.ppermute(v, 'grp', [(g, (g + 2 * step) % 8) for g in range(8)])]
    pallas_call x0 -> x14, Pallas kernels: none -> 26.8 us  [the longest x12 25.6 us: call(): pl.pallas_call(kernel, in_specs=[spec for _, spec in args], out_specs=[VM...]
  transfers between devices with their start and end apart: 4 -> 37, of which waited for: 2 -> 23; matrix products, arithmetic and copies ran while one was open for 1% -> 1% of each run, Pallas kernels for 0% -> 12%
where the time goes in v3:
time: 179 us; the launch traced here: 178 us
  waiting for transfers between devices  85.3 us (48%)
  starting transfers between devices  61.3 us (34%)
  Pallas kernels  26.8 us (15%)
  local copies, waits for them, and re-layouts  3.37 us (2%)
    ppermute x12, starting transfers between devices, send_high(): return lax.ppermute(v, 'grp', [(g, (g + 2 * step) % 8) for g in range(8)])  27.1 us
    pallas_call x12, Pallas kernels, call(): pl.pallas_call(kernel, in_specs=[spec for _, spec in args], out_specs=[VM...  25.6 us
    ppermute x12, waiting for transfers between devices, send_high(): return lax.ppermute(v, 'grp', [(g, (g + 2 * step) % 8) for g in range(8)])  24.7 us
    ppermute x6, waiting for transfers between devices, send_y(): return lax.ppermute(v, 'blk', pairs)  20.3 us
    ppermute x5, waiting for transfers between devices, send_z(): return lax.ppermute(v, 'blk', pairs)  18.1 us
    ppermute x5, waiting for transfers between devices, send_inner(): return lax.ppermute(v, 'blk', pairs)  11.1 us
    ppermute x6, starting transfers between devices, send_y(): return lax.ppermute(v, 'blk', pairs)  8.74 us
    ppermute x3, waiting for transfers between devices, send_outer(): return lax.ppermute(v, 'blk', pairs)  6.34 us
  transfers between devices with their start and end apart: 37, of which 23 were waited for; matrix products, arithmetic and copies ran while one was open for 1% of the time, Pallas kernels for 12%

profile of v3, /device:TPU:1, one launch (start us, length us, event | category | flops | bytes accessed | tf_op | source)
XLA Modules:
  0.0 178.4 jit_solution(12820525159655295216)
XLA Ops:
  0.0 1.9 %fusion = (bf16[320,512]{1,0:T(8,128)(2,1)}, bf16[320,512]{1,0:T(8,128)(2,1)}) fusion(bf16[320,2560]{1,0:T(8,128)(2,1)} %bitcast.2), kind=kLoop, calls=%fused_computation.7 | loop fusion | bytes 1310720 | tf_op jit(solution)/shard_map/slice | solution.py:473
  1.9 6.3 %collective-permute-start = (bf16[320,512]{1,0:T(8,128)(2,1)}, bf16[320,512]{1,0:T(8,128)(2,1)S(1)}, u32[]{:S(2)}, u32[]{:S(2)}) collective-permute-start(bf16[320,512]{1,0:T(8,128)(2,1)} %get-tuple-element.80), channel_id=1, source_target_pairs={{0,32},{32,64},{64,96},{96,128},{128,160},{160,192},{192,224},{1,3... | collective-permute-start | bytes 983048 | tf_op jit(solution)/shard_map/ppermute | solution.py:472
  8.2 1.9 %collective-permute-start.1 = (bf16[320,512]{1,0:T(8,128)(2,1)}, bf16[320,512]{1,0:T(8,128)(2,1)S(1)}, u32[]{:S(2)}, u32[]{:S(2)}) collective-permute-start(bf16[320,512]{1,0:T(8,128)(2,1)} %get-tuple-element.79), channel_id=1, source_target_pairs={{32,0},{64,32},{96,64},{128,96},{160,128},{192,160},{224,192},{33,... | collective-permute-start | bytes 983048 | tf_op jit(solution)/shard_map/ppermute | solution.py:473
  10.2 1.4 reshape.6._.vir
  11.6 8.0 %fit_inner.1 = (bf16[160,2560]{1,0:T(8,128)(2,1)S(1)}, bf16[160,2560]{1,0:T(8,128)(2,1)S(1)}, bf16[320,2560]{1,0:T(8,128)(2,1)S(1)}, bf16[4,1280,256]{2,1,0:T(8,128)(2,1)S(1)}) custom-call(s32[2,180]{1,0:T(2,128)} %bitcast.4, bf16[320,2560]{1,0:T(8,128)(2,1)} %bitcast.3, bf16[180,128,128]{2,1,0:T(8,128)(2,1)} %tiles_in.1, f32[32,160]{1,0:T(8,128)} %reshape.6._.vir), custom_call_target="tpu_custom_call" | custom-call | flops 1200000000 | bytes 9000000 | tf_op jit(solution)/shard_map/fit_inner/pallas_call | solution.py:90
  19.6 1.7 collective-permute-done.1.right
  22.3 3.1 %collective-permute-start.5 = (bf16[160,2560]{1,0:T(8,128)(2,1)S(1)}, bf16[160,2560]{1,0:T(8,128)(2,1)S(1)}, u32[]{:S(2)}, u32[]{:S(2)}) collective-permute-start(bf16[160,2560]{1,0:T(8,128)(2,1)S(1)} %get-tuple-element.47.refs_5_), channel_id=1, source_target_pairs={{0,24},{1,25},{2,26},{3,27},{4,28},{5,29},{6,30},{7,31},{8,0},{9,1... | collective-permute-start | bytes 2457608 | tf_op jit(solution)/shard_map/first/ppermute | solution.py:31
  25.4 2.5 %collective-permute-start.6 = (bf16[160,2560]{1,0:T(8,128)(2,1)S(1)}, bf16[160,2560]{1,0:T(8,128)(2,1)S(1)}, u32[]{:S(2)}, u32[]{:S(2)}) collective-permute-start(bf16[160,2560]{1,0:T(8,128)(2,1)S(1)} %get-tuple-element.47.refs_5_), channel_id=1, source_target_pairs={{0,6},{1,7},{2,4},{3,5},{4,2},{5,3},{6,0},{7,1},{8,14},{9,15},{10,... | collective-permute-start | bytes 2457608 | tf_op jit(solution)/shard_map/first/ppermute | solution.py:36
  27.9 11.2 %collective-permute-done.5.refs_3_.refs_7_ = bf16[160,2560]{1,0:T(8,128)(2,1)S(1)} collective-permute-done((bf16[160,2560]{1,0:T(8,128)(2,1)S(1)}, bf16[160,2560]{1,0:T(8,128)(2,1)S(1)}, u32[]{:S(2)}, u32[]{:S(2)}) %collective-permute-start.5) | collective-permute-done | bytes 819232 | tf_op jit(solution)/shard_map/first/ppermute | solution.py:31
  39.1 2.6 %collective-permute-done.6.refs_4_.refs_8_ = bf16[160,2560]{1,0:T(8,128)(2,1)S(1)} collective-permute-done((bf16[160,2560]{1,0:T(8,128)(2,1)S(1)}, bf16[160,2560]{1,0:T(8,128)(2,1)S(1)}, u32[]{:S(2)}, u32[]{:S(2)}) %collective-permute-start.6) | collective-permute-done | bytes 819232 | tf_op jit(solution)/shard_map/first/ppermute | solution.py:36
  41.7 2.8 %collective-permute-done.4.refs_2_.refs_6_ = bf16[160,2560]{1,0:T(8,128)(2,1)S(1)} collective-permute-done((bf16[160,2560]{1,0:T(8,128)(2,1)S(1)}, bf16[160,2560]{1,0:T(8,128)(2,1)S(1)}, u32[]{:S(2)}, u32[]{:S(2)}) %collective-permute-start.4) | collective-permute-done | bytes 819232 | tf_op jit(solution)/shard_map/first/ppermute | solution.py:31
  45.5 1.6 collective-permute-start.8
  47.2 3.0 %collective-permute-start.14 = (bf16[160,2560]{1,0:T(8,128)(2,1)S(1)}, bf16[160,2560]{1,0:T(8,128)(2,1)S(1)}, u32[]{:S(2)}, u32[]{:S(2)}) collective-permute-start(bf16[160,2560]{1,0:T(8,128)(2,1)S(1)} %collective-permute-done.5.refs_3_.refs_7_), channel_id=1, source_target_pairs={{0,24},{1,25},{2,26},{3,27},{4,28},{5,29},{6,30},{7,31},{8,0},{9,1... | collective-permute-start | bytes 2457608 | tf_op jit(solution)/shard_map/second/ppermute | solution.py:31
  50.3 3.0 %collective-permute-done.7.refs_3_ = bf16[80,2560]{1,0:T(8,128)(2,1)S(1)} collective-permute-done((bf16[80,2560]{1,0:T(8,128)(2,1)S(1)}, bf16[80,2560]{1,0:T(8,128)(2,1)S(1)}, u32[]{:S(2)}, u32[]{:S(2)}) %collective-permute-start.7) | collective-permute-done | bytes 409632 | tf_op jit(solution)/shard_map/second/ppermute | solution.py:41
  53.3 2.3 %collective-permute-done.8.refs_4_ = bf16[80,2560]{1,0:T(8,128)(2,1)S(1)} collective-permute-done((bf16[80,2560]{1,0:T(8,128)(2,1)S(1)}, bf16[80,2560]{1,0:T(8,128)(2,1)S(1)}, u32[]{:S(2)}, u32[]{:S(2)}) %collective-permute-start.8) | collective-permute-done | bytes 409632 | tf_op jit(solution)/shard_map/second/ppermute | solution.py:46
  55.6 3.6 %pair_first.1 = (f32[320,640]{1,0:T(8,128)S(1)}, bf16[320,640]{1,0:T(8,128)(2,1)S(1)}, bf16[640,2560]{1,0:T(8,128)(2,1)S(1)}, bf16[640,2560]{1,0:T(8,128)(2,1)S(1)}) custom-call(bf16[160,2560]{1,0:T(8,128)(2,1)S(1)} %get-tuple-element.46.refs_0_, bf16[160,2560]{1,0:T(8,128)(2,1)S(1)} %collective-permute-done.2.refs_1_, ...), custom_call_target="tpu_custom_call" | custom-call | flops 2097152000 | bytes 8000000 | tf_op jit(solution)/shard_map/pair_first/pallas_call | solution.py:90
  59.3 1.7 collective-permute-done.9.got_in
  61.4 6.0 %collective-permute-done.14.refs_1_.refs_0_ = bf16[160,2560]{1,0:T(8,128)(2,1)S(1)} collective-permute-done((bf16[160,2560]{1,0:T(8,128)(2,1)S(1)}, bf16[160,2560]{1,0:T(8,128)(2,1)S(1)}, u32[]{:S(2)}, u32[]{:S(2)}) %collective-permute-start.14) | collective-permute-done | bytes 819232 | tf_op jit(solution)/shard_map/second/ppermute | solution.py:31
  67.4 3.7 %collective-permute-done.15.refs_2_ = bf16[160,2560]{1,0:T(8,128)(2,1)S(1)} collective-permute-done((bf16[160,2560]{1,0:T(8,128)(2,1)S(1)}, bf16[160,2560]{1,0:T(8,128)(2,1)S(1)}, u32[]{:S(2)}, u32[]{:S(2)}) %collective-permute-start.15) | collective-permute-done | bytes 819232 | tf_op jit(solution)/shard_map/second/ppermute | solution.py:36
  72.2 2.6 %collective-permute-start.19 = (bf16[64,2560]{1,0:T(8,128)(2,1)S(1)}, bf16[64,2560]{1,0:T(8,128)(2,1)S(1)}, u32[]{:S(2)}, u32[]{:S(2)}) collective-permute-start(bf16[64,2560]{1,0:T(8,128)(2,1)S(1)} %get-tuple-element.59), channel_id=1, source_target_pairs={{0,6},{1,7},{2,4},{3,5},{4,2},{5,3},{6,0},{7,1},{8,14},{9,15},{10,... | collective-permute-start | bytes 983048 | tf_op jit(solution)/shard_map/third/ppermute | solution.py:36
  74.8 6.0 %collective-permute-start.10 = (bf16[80,640]{1,0:T(8,128)(2,1)S(1)}, bf16[80,640]{1,0:T(8,128)(2,1)S(1)}, u32[]{:S(2)}, u32[]{:S(2)}) collective-permute-start(bf16[80,640]{1,0:T(8,128)(2,1)S(1)} %get-tuple-element.53), channel_id=1, source_target_pairs={{0,64},{32,96},{64,128},{96,160},{128,192},{160,224},{192,0},{224,... | collective-permute-start | bytes 307208 | tf_op jit(solution)/shard_map/shares/ppermute | solution.py:54
  80.8 2.7 %collective-permute-start.21 = (bf16[48,2560]{1,0:T(8,128)(2,1)S(1)}, bf16[48,2560]{1,0:T(8,128)(2,1)S(1)}, u32[]{:S(2)}, u32[]{:S(2)}) collective-permute-start(bf16[48,2560]{1,0:T(8,128)(2,1)S(1)} %get-tuple-element.61), channel_id=1, source_target_pairs={{0,24},{1,25},{2,26},{3,27},{4,28},{5,29},{6,30},{7,31},{8,0},{9,1... | collective-permute-start | bytes 737288 | tf_op jit(solution)/shard_map/third/ppermute | solution.py:31
  83.4 3.3 %collective-permute-start.12 = (bf16[80,640]{1,0:T(8,128)(2,1)S(1)}, bf16[80,640]{1,0:T(8,128)(2,1)S(1)}, u32[]{:S(2)}, u32[]{:S(2)}) collective-permute-start(bf16[80,640]{1,0:T(8,128)(2,1)S(1)} %get-tuple-element.55), channel_id=1, source_target_pairs={{0,192},{32,224},{64,0},{96,32},{128,64},{160,96},{192,128},{224,1... | collective-permute-start | bytes 307208 | tf_op jit(solution)/shard_map/shares/ppermute | solution.py:54
  86.7 2.3 %pair_early.1 = (f32[640,480]{1,0:T(8,128)S(1)}, bf16[640,2560]{1,0:T(8,128)(2,1)S(1)}) custom-call(bf16[640,2560]{1,0:T(8,128)(2,1)S(1)} %get-tuple-element.56.acat, bf16[160,2560]{1,0:T(8,128)(2,1)S(1)} %collective-permute-done.13.refs_0_.refs_1_, bf16[160,2560]{1,0:T(8,128)(2,1)S(1)} %collective-permute-done.14.refs_1_.refs_0_, ...), custom_call_target="tpu_custom_call" | custom-call | flops 1572864000 | bytes 4000000 | tf_op jit(solution)/shard_map/pair_early/pallas_call | solution.py:90
  89.0 2.2 %collective-permute-done.11.refs_1_ = bf16[80,640]{1,0:T(8,128)(2,1)S(1)} collective-permute-done((bf16[80,640]{1,0:T(8,128)(2,1)S(1)}, bf16[80,640]{1,0:T(8,128)(2,1)S(1)}, u32[]{:S(2)}, u32[]{:S(2)}) %collective-permute-start.11) | collective-permute-done | bytes 102432 | tf_op jit(solution)/shard_map/shares/ppermute | solution.py:54
  92.5 1.5 pair_late.1
  94.0 3.7 %collective-permute-start.22 = (bf16[320,640]{1,0:T(8,128)(2,1)S(1)}, bf16[320,640]{1,0:T(8,128)(2,1)S(1)}, u32[]{:S(2)}, u32[]{:S(2)}) collective-permute-start(bf16[320,640]{1,0:T(8,128)(2,1)S(1)} %get-tuple-element.63), channel_id=1, source_target_pairs={{0,32},{32,0},{64,96},{96,64},{128,160},{160,128},{192,224},{224,1... | collective-permute-start | bytes 1228808 | tf_op jit(solution)/shard_map/core/ppermute | solution.py:50
  97.7 4.5 %collective-permute-start.16 = (bf16[80,640]{1,0:T(8,128)(2,1)S(1)}, bf16[80,640]{1,0:T(8,128)(2,1)S(1)}, u32[]{:S(2)}, u32[]{:S(2)}) collective-permute-start(bf16[80,640]{1,0:T(8,128)(2,1)S(1)} %amplitude.2.refs_3_.refs_0_), channel_id=1, source_target_pairs={{0,64},{32,96},{64,128},{96,160},{128,192},{160,224},{192,0},{224,... | collective-permute-start | bytes 307208 | tf_op jit(solution)/shard_map/spread/ppermute | solution.py:54
  102.2 4.3 %collective-permute-done.16.refs_0_.refs_1_ = bf16[80,640]{1,0:T(8,128)(2,1)S(1)} collective-permute-done((bf16[80,640]{1,0:T(8,128)(2,1)S(1)}, bf16[80,640]{1,0:T(8,128)(2,1)S(1)}, u32[]{:S(2)}, u32[]{:S(2)}) %collective-permute-start.16) | collective-permute-done | bytes 102432 | tf_op jit(solution)/shard_map/spread/ppermute | solution.py:54
  106.5 2.7 %collective-permute-done.18.refs_1_.refs_3_ = bf16[80,640]{1,0:T(8,128)(2,1)S(1)} collective-permute-done((bf16[80,640]{1,0:T(8,128)(2,1)S(1)}, bf16[80,640]{1,0:T(8,128)(2,1)S(1)}, u32[]{:S(2)}, u32[]{:S(2)}) %collective-permute-start.18) | collective-permute-done | bytes 102432 | tf_op jit(solution)/shard_map/spread/ppermute | solution.py:54
  109.6 2.2 %collective-permute-start.23 = (bf16[80,640]{1,0:T(8,128)(2,1)S(1)}, bf16[80,640]{1,0:T(8,128)(2,1)S(1)}, u32[]{:S(2)}, u32[]{:S(2)}) collective-permute-start(bf16[80,640]{1,0:T(8,128)(2,1)S(1)} %get-tuple-element.65), channel_id=1, source_target_pairs={{0,64},{32,96},{64,128},{96,160},{128,192},{160,224},{192,0},{224,... | collective-permute-start | bytes 307208 | tf_op jit(solution)/shard_map/shares/ppermute | solution.py:54
  111.8 1.8 collective-permute-start.24
  113.6 2.0 %collective-permute-start.25 = (bf16[80,640]{1,0:T(8,128)(2,1)S(1)}, bf16[80,640]{1,0:T(8,128)(2,1)S(1)}, u32[]{:S(2)}, u32[]{:S(2)}) collective-permute-start(bf16[80,640]{1,0:T(8,128)(2,1)S(1)} %get-tuple-element.67), channel_id=1, source_target_pairs={{0,192},{32,224},{64,0},{96,32},{128,64},{160,96},{192,128},{224,1... | collective-permute-start | bytes 307208 | tf_op jit(solution)/shard_map/shares/ppermute | solution.py:54
  115.6 3.2 %collective-permute-start.17 = (bf16[80,640]{1,0:T(8,128)(2,1)S(1)}, bf16[80,640]{1,0:T(8,128)(2,1)S(1)}, u32[]{:S(2)}, u32[]{:S(2)}) collective-permute-start(bf16[80,640]{1,0:T(8,128)(2,1)S(1)} %amplitude.2.refs_3_.refs_0_), channel_id=1, source_target_pairs={{0,128},{32,160},{64,192},{96,224},{128,0},{160,32},{192,64},{224,... | collective-permute-start | bytes 307208 | tf_op jit(solution)/shard_map/spread/ppermute | solution.py:54
  118.8 2.0 %collective-permute-done.24.refs_1_ = bf16[80,640]{1,0:T(8,128)(2,1)S(1)} collective-permute-done((bf16[80,640]{1,0:T(8,128)(2,1)S(1)}, bf16[80,640]{1,0:T(8,128)(2,1)S(1)}, u32[]{:S(2)}, u32[]{:S(2)}) %collective-permute-start.24) | collective-permute-done | bytes 102432 | tf_op jit(solution)/shard_map/shares/ppermute | solution.py:54
  120.8 7.9 %collective-permute-done.25.refs_2_ = bf16[80,640]{1,0:T(8,128)(2,1)S(1)} collective-permute-done((bf16[80,640]{1,0:T(8,128)(2,1)S(1)}, bf16[80,640]{1,0:T(8,128)(2,1)S(1)}, u32[]{:S(2)}, u32[]{:S(2)}) %collective-permute-start.25) | collective-permute-done | bytes 102432 | tf_op jit(solution)/shard_map/shares/ppermute | solution.py:54
  130.5 3.5 %collective-permute-start.28 = (bf16[80,640]{1,0:T(8,128)(2,1)S(1)}, bf16[80,640]{1,0:T(8,128)(2,1)S(1)}, u32[]{:S(2)}, u32[]{:S(2)}) collective-permute-start(bf16[80,640]{1,0:T(8,128)(2,1)S(1)} %amplitude.3.refs_4_), channel_id=1, source_target_pairs={{0,192},{32,224},{64,0},{96,32},{128,64},{160,96},{192,128},{224,1... | collective-permute-start | bytes 307208 | tf_op jit(solution)/shard_map/spread/ppermute | solution.py:54
  134.0 1.7 collective-permute-start.29
  137.9 3.5 %collective-permute-done.28.refs_7_ = bf16[80,640]{1,0:T(8,128)(2,1)S(1)} collective-permute-done((bf16[80,640]{1,0:T(8,128)(2,1)S(1)}, bf16[80,640]{1,0:T(8,128)(2,1)S(1)}, u32[]{:S(2)}, u32[]{:S(2)}) %collective-permute-start.28) | collective-permute-done | bytes 102432 | tf_op jit(solution)/shard_map/spread/ppermute | solution.py:54
  143.4 1.8 %density_first.1 = (bf16[80,2560]{1,0:T(8,128)(2,1)S(1)}, bf16[80,2560]{1,0:T(8,128)(2,1)S(1)}, bf16[640,1280]{1,0:T(8,128)(2,1)S(1)}) custom-call(bf16[80,640]{1,0:T(8,128)(2,1)S(1)} %amplitude.2.refs_3_.refs_0_, bf16[80,640]{1,0:T(8,128)(2,1)S(1)} %collective-permute-done.16.refs_0_.refs_1_, bf16[80,640]{1,0:T(8,128)(2,1)S(1)} %collective-permute-done.17.refs_2_, ...), custom_call_target="tpu_custom_call" | custom-call | flops 1048576000 | bytes 1000000 | tf_op jit(solution)/shard_map/density_first/pallas_call | solution.py:90
  145.4 2.7 %density.3 = (bf16[80,2560]{1,0:T(8,128)(2,1)S(1)}, f32[80,2560]{1,0:T(8,128)S(1)}, f32[80,2560]{1,0:T(8,128)S(1)}, bf16[80,2560]{1,0:T(8,128)(2,1)S(1)}) custom-call(bf16[640,1280]{1,0:T(8,128)(2,1)S(1)} %get-tuple-element.70.tcat, bf16[640,2560]{1,0:T(8,128)(2,1)S(1)} %get-tuple-element.68.refs_10_.b1, bf16[640,2560]{1,0:T(8,128)(2,1)S(1)} %get-tuple-element.69.refs_11_.b2), custom_call_target="tpu_custom_call" | custom-call | flops 2097152000 | bytes 1000000 | tf_op jit(solution)/shard_map/density/pallas_call | solution.py:90
  148.1 1.5 collective-permute-start.31
  149.6 1.5 collective-permute-start.36
  151.1 1.4 density.2
  152.5 3.5 %collective-permute-done.32 = bf16[80,2560]{1,0:T(8,128)(2,1)S(1)} collective-permute-done((bf16[80,2560]{1,0:T(8,128)(2,1)S(1)}, bf16[80,2560]{1,0:T(8,128)(2,1)S(1)}, u32[]{:S(2)}, u32[]{:S(2)}) %collective-permute-start.32) | collective-permute-done | bytes 409632 | tf_op jit(solution)/shard_map/out/ppermute | solution.py:41
  156.2 3.4 %collective-permute-done.34 = bf16[80,2560]{1,0:T(8,128)(2,1)S(1)} collective-permute-done((bf16[80,2560]{1,0:T(8,128)(2,1)S(1)}, bf16[80,2560]{1,0:T(8,128)(2,1)S(1)}, u32[]{:S(2)}, u32[]{:S(2)}) %collective-permute-start.34) | collective-permute-done | bytes 409632 | tf_op jit(solution)/shard_map/out/ppermute | solution.py:46
  160.2 4.6 %collective-permute-done.31 = bf16[80,2560]{1,0:T(8,128)(2,1)S(1)} collective-permute-done((bf16[80,2560]{1,0:T(8,128)(2,1)S(1)}, bf16[80,2560]{1,0:T(8,128)(2,1)S(1)}, u32[]{:S(2)}, u32[]{:S(2)}) %collective-permute-start.31) | collective-permute-done | bytes 409632 | tf_op jit(solution)/shard_map/out/ppermute | solution.py:41
  164.8 12.4 %collective-permute-done.33 = bf16[80,2560]{1,0:T(8,128)(2,1)S(1)} collective-permute-done((bf16[80,2560]{1,0:T(8,128)(2,1)S(1)}, bf16[80,2560]{1,0:T(8,128)(2,1)S(1)}, u32[]{:S(2)}, u32[]{:S(2)}) %collective-permute-start.33) | collective-permute-done | bytes 409632 | tf_op jit(solution)/shard_map/out/ppermute | solution.py:46
  (55 shorter events, 13.5 us)
Async XLA Ops:
  1.9 17.6 %collective-permute-start = (bf16[320,512]{1,0:T(8,128)(2,1)}, bf16[320,512]{1,0:T(8,128)(2,1)S(1)}, u32[]{:S(2)}, u32[]{:S(2)}) collective-permute-start(bf16[320,512]{1,0:T(8,128)(2,1)} %get-tuple-element.80), channel_id=1, source_target_pairs={{0,32},{32,64},{64,96},{96,128},{128,160},{160,192},{192,224},{1,3... | collective-permute-start | bytes 983048 | tf_op jit(solution)/shard_map/ppermute | solution.py:472
  8.2 13.0 %collective-permute-start.1 = (bf16[320,512]{1,0:T(8,128)(2,1)}, bf16[320,512]{1,0:T(8,128)(2,1)S(1)}, u32[]{:S(2)}, u32[]{:S(2)}) collective-permute-start(bf16[320,512]{1,0:T(8,128)(2,1)} %get-tuple-element.79), channel_id=1, source_target_pairs={{32,0},{64,32},{96,64},{128,96},{160,128},{192,160},{224,192},{33,... | collective-permute-start | bytes 983048 | tf_op jit(solution)/shard_map/ppermute | solution.py:473
  22.3 16.8 %collective-permute-start.5 = (bf16[160,2560]{1,0:T(8,128)(2,1)S(1)}, bf16[160,2560]{1,0:T(8,128)(2,1)S(1)}, u32[]{:S(2)}, u32[]{:S(2)}) collective-permute-start(bf16[160,2560]{1,0:T(8,128)(2,1)S(1)} %get-tuple-element.47.refs_5_), channel_id=1, source_target_pairs={{0,24},{1,25},{2,26},{3,27},{4,28},{5,29},{6,30},{7,31},{8,0},{9,1... | collective-permute-start | bytes 2457608 | tf_op jit(solution)/shard_map/first/ppermute | solution.py:31
  25.4 16.3 %collective-permute-start.6 = (bf16[160,2560]{1,0:T(8,128)(2,1)S(1)}, bf16[160,2560]{1,0:T(8,128)(2,1)S(1)}, u32[]{:S(2)}, u32[]{:S(2)}) collective-permute-start(bf16[160,2560]{1,0:T(8,128)(2,1)S(1)} %get-tuple-element.47.refs_5_), channel_id=1, source_target_pairs={{0,6},{1,7},{2,4},{3,5},{4,2},{5,3},{6,0},{7,1},{8,14},{9,15},{10,... | collective-permute-start | bytes 2457608 | tf_op jit(solution)/shard_map/first/ppermute | solution.py:36
  27.8 16.6 %collective-permute-start.4 = (bf16[160,2560]{1,0:T(8,128)(2,1)S(1)}, bf16[160,2560]{1,0:T(8,128)(2,1)S(1)}, u32[]{:S(2)}, u32[]{:S(2)}) collective-permute-start(bf16[160,2560]{1,0:T(8,128)(2,1)S(1)} %get-tuple-element.47.refs_5_), channel_id=1, source_target_pairs={{0,8},{1,9},{2,10},{3,11},{4,12},{5,13},{6,14},{7,15},{8,16},{9,17... | collective-permute-start | bytes 2457608 | tf_op jit(solution)/shard_map/first/ppermute | solution.py:31
  27.9 16.6 %collective-permute-start.2 = (bf16[160,2560]{1,0:T(8,128)(2,1)S(1)}, bf16[160,2560]{1,0:T(8,128)(2,1)S(1)}, u32[]{:S(2)}, u32[]{:S(2)}) collective-permute-start(bf16[160,2560]{1,0:T(8,128)(2,1)S(1)} %get-tuple-element.46.refs_0_), channel_id=1, source_target_pairs={{0,2},{1,3},{2,0},{3,1},{4,6},{5,7},{6,4},{7,5},{8,10},{9,11},{10,... | collective-permute-start | bytes 2457608 | tf_op jit(solution)/shard_map/first/ppermute | solution.py:41
  27.9 16.6 %collective-permute-start.3 = (bf16[160,2560]{1,0:T(8,128)(2,1)S(1)}, bf16[160,2560]{1,0:T(8,128)(2,1)S(1)}, u32[]{:S(2)}, u32[]{:S(2)}) collective-permute-start(bf16[160,2560]{1,0:T(8,128)(2,1)S(1)} %get-tuple-element.46.refs_0_), channel_id=1, source_target_pairs={{0,1},{1,0},{2,3},{3,2},{4,5},{5,4},{6,7},{7,6},{8,9},{9,8},{10,11... | collective-permute-start | bytes 2457608 | tf_op jit(solution)/shard_map/first/ppermute | solution.py:46
  44.9 8.4 %collective-permute-start.7 = (bf16[80,2560]{1,0:T(8,128)(2,1)S(1)}, bf16[80,2560]{1,0:T(8,128)(2,1)S(1)}, u32[]{:S(2)}, u32[]{:S(2)}) collective-permute-start(bf16[80,2560]{1,0:T(8,128)(2,1)S(1)} %get-tuple-element.48), channel_id=1, source_target_pairs={{0,2},{1,3},{2,0},{3,1},{4,6},{5,7},{6,4},{7,5},{8,10},{9,11},{10,... | collective-permute-start | bytes 1228808 | tf_op jit(solution)/shard_map/second/ppermute | solution.py:41
  45.5 10.1 %collective-permute-start.8 = (bf16[80,2560]{1,0:T(8,128)(2,1)S(1)}, bf16[80,2560]{1,0:T(8,128)(2,1)S(1)}, u32[]{:S(2)}, u32[]{:S(2)}) collective-permute-start(bf16[80,2560]{1,0:T(8,128)(2,1)S(1)} %get-tuple-element.49), channel_id=1, source_target_pairs={{0,1},{1,0},{2,3},{3,2},{4,5},{5,4},{6,7},{7,6},{8,9},{9,8},{10,11... | collective-permute-start | bytes 1228808 | tf_op jit(solution)/shard_map/second/ppermute | solution.py:46
  47.2 20.3 %collective-permute-start.14 = (bf16[160,2560]{1,0:T(8,128)(2,1)S(1)}, bf16[160,2560]{1,0:T(8,128)(2,1)S(1)}, u32[]{:S(2)}, u32[]{:S(2)}) collective-permute-start(bf16[160,2560]{1,0:T(8,128)(2,1)S(1)} %collective-permute-done.5.refs_3_.refs_7_), channel_id=1, source_target_pairs={{0,24},{1,25},{2,26},{3,27},{4,28},{5,29},{6,30},{7,31},{8,0},{9,1... | collective-permute-start | bytes 2457608 | tf_op jit(solution)/shard_map/second/ppermute | solution.py:31
  50.1 21.0 %collective-permute-start.15 = (bf16[160,2560]{1,0:T(8,128)(2,1)S(1)}, bf16[160,2560]{1,0:T(8,128)(2,1)S(1)}, u32[]{:S(2)}, u32[]{:S(2)}) collective-permute-start(bf16[160,2560]{1,0:T(8,128)(2,1)S(1)} %collective-permute-done.5.refs_3_.refs_7_), channel_id=1, source_target_pairs={{0,6},{1,7},{2,4},{3,5},{4,2},{5,3},{6,0},{7,1},{8,14},{9,15},{10,... | collective-permute-start | bytes 2457608 | tf_op jit(solution)/shard_map/second/ppermute | solution.py:36
  50.3 21.1 %collective-permute-start.13 = (bf16[160,2560]{1,0:T(8,128)(2,1)S(1)}, bf16[160,2560]{1,0:T(8,128)(2,1)S(1)}, u32[]{:S(2)}, u32[]{:S(2)}) collective-permute-start(bf16[160,2560]{1,0:T(8,128)(2,1)S(1)} %collective-permute-done.6.refs_4_.refs_8_), channel_id=1, source_target_pairs={{0,8},{1,9},{2,10},{3,11},{4,12},{5,13},{6,14},{7,15},{8,16},{9,17... | collective-permute-start | bytes 2457608 | tf_op jit(solution)/shard_map/second/ppermute | solution.py:31
  59.2 1.8 %collective-permute-start.9 = (bf16[320,640]{1,0:T(8,128)(2,1)S(1)}, bf16[320,640]{1,0:T(8,128)(2,1)S(1)}, u32[]{:S(2)}, u32[]{:S(2)}) collective-permute-start(bf16[320,640]{1,0:T(8,128)(2,1)S(1)} %get-tuple-element.51), channel_id=1, source_target_pairs={{0,32},{32,0},{64,96},{96,64},{128,160},{160,128},{192,224},{224,1... | collective-permute-start | bytes 1228808 | tf_op jit(solution)/shard_map/core/ppermute | solution.py:50
  72.2 20.3 %collective-permute-start.19 = (bf16[64,2560]{1,0:T(8,128)(2,1)S(1)}, bf16[64,2560]{1,0:T(8,128)(2,1)S(1)}, u32[]{:S(2)}, u32[]{:S(2)}) collective-permute-start(bf16[64,2560]{1,0:T(8,128)(2,1)S(1)} %get-tuple-element.59), channel_id=1, source_target_pairs={{0,6},{1,7},{2,4},{3,5},{4,2},{5,3},{6,0},{7,1},{8,14},{9,15},{10,... | collective-permute-start | bytes 983048 | tf_op jit(solution)/shard_map/third/ppermute | solution.py:36
  74.8 8.7 %collective-permute-start.10 = (bf16[80,640]{1,0:T(8,128)(2,1)S(1)}, bf16[80,640]{1,0:T(8,128)(2,1)S(1)}, u32[]{:S(2)}, u32[]{:S(2)}) collective-permute-start(bf16[80,640]{1,0:T(8,128)(2,1)S(1)} %get-tuple-element.53), channel_id=1, source_target_pairs={{0,64},{32,96},{64,128},{96,160},{128,192},{160,224},{192,0},{224,... | collective-permute-start | bytes 307208 | tf_op jit(solution)/shard_map/shares/ppermute | solution.py:54
  80.7 11.7 %collective-permute-start.20 = (bf16[48,2560]{1,0:T(8,128)(2,1)S(1)}, bf16[48,2560]{1,0:T(8,128)(2,1)S(1)}, u32[]{:S(2)}, u32[]{:S(2)}) collective-permute-start(bf16[48,2560]{1,0:T(8,128)(2,1)S(1)} %get-tuple-element.60), channel_id=1, source_target_pairs={{0,8},{1,9},{2,10},{3,11},{4,12},{5,13},{6,14},{7,15},{8,16},{9,17... | collective-permute-start | bytes 737288 | tf_op jit(solution)/shard_map/third/ppermute | solution.py:31
  80.8 11.7 %collective-permute-start.21 = (bf16[48,2560]{1,0:T(8,128)(2,1)S(1)}, bf16[48,2560]{1,0:T(8,128)(2,1)S(1)}, u32[]{:S(2)}, u32[]{:S(2)}) collective-permute-start(bf16[48,2560]{1,0:T(8,128)(2,1)S(1)} %get-tuple-element.61), channel_id=1, source_target_pairs={{0,24},{1,25},{2,26},{3,27},{4,28},{5,29},{6,30},{7,31},{8,0},{9,1... | collective-permute-start | bytes 737288 | tf_op jit(solution)/shard_map/third/ppermute | solution.py:31
  83.4 7.8 %collective-permute-start.11 = (bf16[80,640]{1,0:T(8,128)(2,1)S(1)}, bf16[80,640]{1,0:T(8,128)(2,1)S(1)}, u32[]{:S(2)}, u32[]{:S(2)}) collective-permute-start(bf16[80,640]{1,0:T(8,128)(2,1)S(1)} %get-tuple-element.54), channel_id=1, source_target_pairs={{0,128},{32,160},{64,192},{96,224},{128,0},{160,32},{192,64},{224,... | collective-permute-start | bytes 307208 | tf_op jit(solution)/shard_map/shares/ppermute | solution.py:54
  83.4 7.8 %collective-permute-start.12 = (bf16[80,640]{1,0:T(8,128)(2,1)S(1)}, bf16[80,640]{1,0:T(8,128)(2,1)S(1)}, u32[]{:S(2)}, u32[]{:S(2)}) collective-permute-start(bf16[80,640]{1,0:T(8,128)(2,1)S(1)} %get-tuple-element.55), channel_id=1, source_target_pairs={{0,192},{32,224},{64,0},{96,32},{128,64},{160,96},{192,128},{224,1... | collective-permute-start | bytes 307208 | tf_op jit(solution)/shard_map/shares/ppermute | solution.py:54
  86.7 4.5 %copy-start = (f32[32,160]{1,0:T(8,128)S(1)}, f32[32,160]{1,0:T(8,128)}, u32[]{:S(2)}) copy-start(f32[32,160]{1,0:T(8,128)} %reshape.6._.vir) | copy-start | bytes 61444
  86.7 4.5 %copy-start.1 = (f32[1000]{0:T(1024)S(1)}, f32[1000]{0:T(1024)}, u32[]{:S(2)}) copy-start(f32[1000]{0:T(1024)} %occ.3) | copy-start | bytes 12004
  86.7 4.5 %copy-start.2 = (s32[2]{0:T(128)S(1)}, s32[2]{0:T(128)}, u32[]{:S(2)}) copy-start(s32[2]{0:T(128)} %chosen.3) | copy-start | bytes 28
  94.0 15.2 %collective-permute-start.22 = (bf16[320,640]{1,0:T(8,128)(2,1)S(1)}, bf16[320,640]{1,0:T(8,128)(2,1)S(1)}, u32[]{:S(2)}, u32[]{:S(2)}) collective-permute-start(bf16[320,640]{1,0:T(8,128)(2,1)S(1)} %get-tuple-element.63), channel_id=1, source_target_pairs={{0,32},{32,0},{64,96},{96,64},{128,160},{160,128},{192,224},{224,1... | collective-permute-start | bytes 1228808 | tf_op jit(solution)/shard_map/core/ppermute | solution.py:50
  97.7 8.8 %collective-permute-start.16 = (bf16[80,640]{1,0:T(8,128)(2,1)S(1)}, bf16[80,640]{1,0:T(8,128)(2,1)S(1)}, u32[]{:S(2)}, u32[]{:S(2)}) collective-permute-start(bf16[80,640]{1,0:T(8,128)(2,1)S(1)} %amplitude.2.refs_3_.refs_0_), channel_id=1, source_target_pairs={{0,64},{32,96},{64,128},{96,160},{128,192},{160,224},{192,0},{224,... | collective-permute-start | bytes 307208 | tf_op jit(solution)/shard_map/spread/ppermute | solution.py:54
  102.2 7.0 %collective-permute-start.18 = (bf16[80,640]{1,0:T(8,128)(2,1)S(1)}, bf16[80,640]{1,0:T(8,128)(2,1)S(1)}, u32[]{:S(2)}, u32[]{:S(2)}) collective-permute-start(bf16[80,640]{1,0:T(8,128)(2,1)S(1)} %amplitude.2.refs_3_.refs_0_), channel_id=1, source_target_pairs={{0,192},{32,224},{64,0},{96,32},{128,64},{160,96},{192,128},{224,1... | collective-permute-start | bytes 307208 | tf_op jit(solution)/shard_map/spread/ppermute | solution.py:54
  109.6 9.3 %collective-permute-start.23 = (bf16[80,640]{1,0:T(8,128)(2,1)S(1)}, bf16[80,640]{1,0:T(8,128)(2,1)S(1)}, u32[]{:S(2)}, u32[]{:S(2)}) collective-permute-start(bf16[80,640]{1,0:T(8,128)(2,1)S(1)} %get-tuple-element.65), channel_id=1, source_target_pairs={{0,64},{32,96},{64,128},{96,160},{128,192},{160,224},{192,0},{224,... | collective-permute-start | bytes 307208 | tf_op jit(solution)/shard_map/shares/ppermute | solution.py:54
  111.8 9.0 %collective-permute-start.24 = (bf16[80,640]{1,0:T(8,128)(2,1)S(1)}, bf16[80,640]{1,0:T(8,128)(2,1)S(1)}, u32[]{:S(2)}, u32[]{:S(2)}) collective-permute-start(bf16[80,640]{1,0:T(8,128)(2,1)S(1)} %get-tuple-element.66), channel_id=1, source_target_pairs={{0,128},{32,160},{64,192},{96,224},{128,0},{160,32},{192,64},{224,... | collective-permute-start | bytes 307208 | tf_op jit(solution)/shard_map/shares/ppermute | solution.py:54
  113.6 15.1 %collective-permute-start.25 = (bf16[80,640]{1,0:T(8,128)(2,1)S(1)}, bf16[80,640]{1,0:T(8,128)(2,1)S(1)}, u32[]{:S(2)}, u32[]{:S(2)}) collective-permute-start(bf16[80,640]{1,0:T(8,128)(2,1)S(1)} %get-tuple-element.67), channel_id=1, source_target_pairs={{0,192},{32,224},{64,0},{96,32},{128,64},{160,96},{192,128},{224,1... | collective-permute-start | bytes 307208 | tf_op jit(solution)/shard_map/shares/ppermute | solution.py:54
  115.6 18.4 %collective-permute-start.17 = (bf16[80,640]{1,0:T(8,128)(2,1)S(1)}, bf16[80,640]{1,0:T(8,128)(2,1)S(1)}, u32[]{:S(2)}, u32[]{:S(2)}) collective-permute-start(bf16[80,640]{1,0:T(8,128)(2,1)S(1)} %amplitude.2.refs_3_.refs_0_), channel_id=1, source_target_pairs={{0,128},{32,160},{64,192},{96,224},{128,0},{160,32},{192,64},{224,... | collective-permute-start | bytes 307208 | tf_op jit(solution)/shard_map/spread/ppermute | solution.py:54
  129.9 6.7 %collective-permute-start.26 = (bf16[80,640]{1,0:T(8,128)(2,1)S(1)}, bf16[80,640]{1,0:T(8,128)(2,1)S(1)}, u32[]{:S(2)}, u32[]{:S(2)}) collective-permute-start(bf16[80,640]{1,0:T(8,128)(2,1)S(1)} %amplitude.3.refs_4_), channel_id=1, source_target_pairs={{0,64},{32,96},{64,128},{96,160},{128,192},{160,224},{192,0},{224,... | collective-permute-start | bytes 307208 | tf_op jit(solution)/shard_map/spread/ppermute | solution.py:54
  130.4 7.5 %collective-permute-start.27 = (bf16[80,640]{1,0:T(8,128)(2,1)S(1)}, bf16[80,640]{1,0:T(8,128)(2,1)S(1)}, u32[]{:S(2)}, u32[]{:S(2)}) collective-permute-start(bf16[80,640]{1,0:T(8,128)(2,1)S(1)} %amplitude.3.refs_4_), channel_id=1, source_target_pairs={{0,128},{32,160},{64,192},{96,224},{128,0},{160,32},{192,64},{224,... | collective-permute-start | bytes 307208 | tf_op jit(solution)/shard_map/spread/ppermute | solution.py:54
  130.5 10.9 %collective-permute-start.28 = (bf16[80,640]{1,0:T(8,128)(2,1)S(1)}, bf16[80,640]{1,0:T(8,128)(2,1)S(1)}, u32[]{:S(2)}, u32[]{:S(2)}) collective-permute-start(bf16[80,640]{1,0:T(8,128)(2,1)S(1)} %amplitude.3.refs_4_), channel_id=1, source_target_pairs={{0,192},{32,224},{64,0},{96,32},{128,64},{160,96},{192,128},{224,1... | collective-permute-start | bytes 307208 | tf_op jit(solution)/shard_map/spread/ppermute | solution.py:54
  134.0 8.0 %collective-permute-start.29 = (bf16[320,640]{1,0:T(8,128)(2,1)S(1)}, bf16[320,640]{1,0:T(8,128)(2,1)S(1)}, u32[]{:S(2)}, u32[]{:S(2)}) collective-permute-start(bf16[320,640]{1,0:T(8,128)(2,1)S(1)} %pad_maximum_fusion.1), channel_id=1, source_target_pairs={{0,32},{32,0},{64,96},{96,64},{128,160},{160,128},{192,224},{224,1... | collective-permute-start | bytes 1228808 | tf_op jit(solution)/shard_map/other/ppermute | solution.py:50
  141.5 2.0 %collective-permute-start.30 = (bf16[320,640]{1,0:T(8,128)(2,1)S(1)}, bf16[320,640]{1,0:T(8,128)(2,1)S(1)}, u32[]{:S(2)}, u32[]{:S(2)}) collective-permute-start(bf16[320,640]{1,0:T(8,128)(2,1)S(1)} %pad_maximum_fusion.2), channel_id=1, source_target_pairs={{0,32},{32,0},{64,96},{96,64},{128,160},{160,128},{192,224},{224,1... | collective-permute-start | bytes 1228808 | tf_op jit(solution)/shard_map/other/ppermute | solution.py:50
  145.3 10.8 %collective-permute-start.32 = (bf16[80,2560]{1,0:T(8,128)(2,1)S(1)}, bf16[80,2560]{1,0:T(8,128)(2,1)S(1)}, u32[]{:S(2)}, u32[]{:S(2)}) collective-permute-start(bf16[80,2560]{1,0:T(8,128)(2,1)S(1)} %get-tuple-element.74), channel_id=1, source_target_pairs={{0,2},{1,3},{2,0},{3,1},{4,6},{5,7},{6,4},{7,5},{8,10},{9,11},{10,... | collective-permute-start | bytes 1228808 | tf_op jit(solution)/shard_map/out/ppermute | solution.py:41
  148.1 16.7 %collective-permute-start.31 = (bf16[80,2560]{1,0:T(8,128)(2,1)S(1)}, bf16[80,2560]{1,0:T(8,128)(2,1)S(1)}, u32[]{:S(2)}, u32[]{:S(2)}) collective-permute-start(bf16[80,2560]{1,0:T(8,128)(2,1)S(1)} %get-tuple-element.72), channel_id=1, source_target_pairs={{0,2},{1,3},{2,0},{3,1},{4,6},{5,7},{6,4},{7,5},{8,10},{9,11},{10,... | collective-permute-start | bytes 1228808 | tf_op jit(solution)/shard_map/out/ppermute | solution.py:41
  149.6 10.0 %collective-permute-start.34 = (bf16[80,2560]{1,0:T(8,128)(2,1)S(1)}, bf16[80,2560]{1,0:T(8,128)(2,1)S(1)}, u32[]{:S(2)}, u32[]{:S(2)}) collective-permute-start(bf16[80,2560]{1,0:T(8,128)(2,1)S(1)} %get-tuple-element.77), channel_id=1, source_target_pairs={{0,1},{1,0},{2,3},{3,2},{4,5},{5,4},{6,7},{7,6},{8,9},{9,8},{10,11... | collective-permute-start | bytes 1228808 | tf_op jit(solution)/shard_map/out/ppermute | solution.py:46
  149.6 27.7 %collective-permute-start.36 = (bf16[80,2560]{1,0:T(8,128)(2,1)S(1)}, bf16[80,2560]{1,0:T(8,128)(2,1)S(1)}, u32[]{:S(2)}, u32[]{:S(2)}) collective-permute-start(bf16[80,2560]{1,0:T(8,128)(2,1)S(1)} %get-tuple-element.78), channel_id=1, source_target_pairs={{0,1},{1,0},{2,3},{3,2},{4,5},{5,4},{6,7},{7,6},{8,9},{9,8},{10,11... | collective-permute-start | bytes 1228808 | tf_op jit(solution)/shard_map/out/ppermute | solution.py:46
  156.1 21.1 %collective-permute-start.33 = (bf16[80,2560]{1,0:T(8,128)(2,1)S(1)}, bf16[80,2560]{1,0:T(8,128)(2,1)S(1)}, u32[]{:S(2)}, u32[]{:S(2)}) collective-permute-start(bf16[80,2560]{1,0:T(8,128)(2,1)S(1)} %add_convert_fusion.3), channel_id=1, source_target_pairs={{0,1},{1,0},{2,3},{3,2},{4,5},{5,4},{6,7},{7,6},{8,9},{9,8},{10,11... | collective-permute-start | bytes 1228808 | tf_op jit(solution)/shard_map/out/ppermute | solution.py:46
  159.7 17.6 %collective-permute-start.35 = (bf16[80,2560]{1,0:T(8,128)(2,1)S(1)}, bf16[80,2560]{1,0:T(8,128)(2,1)S(1)}, u32[]{:S(2)}, u32[]{:S(2)}) collective-permute-start(bf16[80,2560]{1,0:T(8,128)(2,1)S(1)} %add_convert_fusion.1), channel_id=1, source_target_pairs={{0,2},{1,3},{2,0},{3,1},{4,6},{5,7},{6,4},{7,5},{8,10},{9,11},{10,... | collective-permute-start | bytes 1228808 | tf_op jit(solution)/shard_map/out/ppermute | solution.py:41

commit v4 on v3

--- a/solution.py
+++ b/solution.py
@@ -58,8 +58,8 @@
     return pltpu.CompilerParams(vmem_limit_bytes=mib * MIB)
 
 
-def cost(flops, nbytes):
-    return pl.CostEstimate(flops=int(flops), bytes_accessed=int(nbytes), transcendentals=0)
+def cost():
+    return pl.CostEstimate(flops=1000, bytes_accessed=1000, transcendentals=0)
 
 
 def position():
@@ -86,7 +86,7 @@
     return pltpu.VMEM(shape, dtype)
 
 
-def call(kernel, args, outs, scratch=(), name=None, flops=1e6, nbytes=1e6, aliases=None, mib=40):
+def call(kernel, args, outs, scratch=(), name=None, aliases=None, mib=40):
     return pl.pallas_call(
         kernel,
         in_specs=[spec for _, spec in args],
@@ -95,7 +95,7 @@
         scratch_shapes=list(scratch),
         input_output_aliases=aliases or {},
         compiler_params=params(mib),
-        cost_estimate=cost(flops, nbytes),
+        cost_estimate=cost(),
         name=name,
     )(*[a for a, _ in args])
 
@@ -104,49 +104,61 @@
 EDGE = (0, 1, 8, 9)
 
 
-def fit_inner_kernel(index, own_in, tiles_in, _, a, b, own, edge, tiles, weights, own_sem, sems):
+def fit_inner_kernel(index, own_in, tiles_in, a, b, own, edge, inner, own_sem, sems):
     own_copies = [
         pltpu.make_async_copy(
             own_in.at[pl.ds(i * ROWS, ROWS)], own.at[pl.ds(i * ROWS, ROWS)], own_sem.at[i]
         )
         for i in range(2)
     ]
-    copies = {}
-    for p in INNER + EDGE:
-        part = pl.ds(p * 2 * BAND, 2 * BAND)
-        copies[p] = pltpu.make_async_copy(tiles_in.at[part], tiles.at[part], sems.at[p])
-    copies[INNER[0]].start()
-    for c in own_copies:
+    where = {p: inner.at[n] for n, p in enumerate(INNER)}
+    where |= {p: edge.at[n] for n, p in enumerate(EDGE)}
+    depth = BAND * TILE
+    copies = {
+        p: [
+            pltpu.make_async_copy(
+                tiles_in.at[pl.ds((2 * p + q) * depth, depth)],
+                where[p].at[pl.ds(q * TILE, depth), pl.ds(q * TILE, TILE)],
+                sems.at[p, q],
+            )
+            for q in range(2)
+        ]
+        for p in INNER + EDGE
+    }
+    order = INNER + EDGE
+    for c in copies[order[0]] + own_copies:
         c.start()
-    for p in (INNER + EDGE)[1:]:
-        copies[p].start()
+    for p in order[1:]:
+        for c in copies[p]:
+            c.start()
     zero = jnp.zeros((TILE, TILE), bf16)
-
-    def build(p, out):
-        out[:TILE, TILE:] = zero
-        out[BAND * TILE :, :TILE] = zero
+    for p in order:
+        where[p][:TILE, TILE:] = zero
+        where[p][depth:, :TILE] = zero
+
+    def ready(p):
+        for c in copies[p]:
+            c.wait()
         for q in range(2):
             for o in range(BAND):
-                slot = p * 2 * BAND + q * BAND + o
                 at = (q + o) * TILE
-                out[at : at + TILE, q * TILE : (q + 1) * TILE] = jnp.where(
-                    index[1, slot] == 1, tiles[slot], zero
-                )
-
-    for p in INNER:
-        copies[p].wait()
-        if p == INNER[0]:
+
+                @pl.when(index[1, p * 2 * BAND + q * BAND + o] == 0)
+                def _():
+                    where[p][at : at + TILE, q * TILE : (q + 1) * TILE] = zero
+
+    for n, p in enumerate(INNER):
+        ready(p)
+        if n == 0:
             for c in own_copies:
                 c.wait()
-        build(p, weights)
         window = own[:, (2 * p - HB) * TILE : (2 * p + HB + 2) * TILE]
-        fitted = jnp.dot(window, weights[...], preferred_element_type=f32).astype(bf16)
+        fitted = jnp.dot(window, inner[n], preferred_element_type=f32).astype(bf16)
         columns = slice(p * 2 * TILE, (p + 1) * 2 * TILE)
         a[:, columns] = fitted[:ROWS]
         b[:, columns] = fitted[ROWS:]
-    for n, p in enumerate(EDGE):
-        copies[p].wait()
-        build(p, edge.at[n])
+    for p in EDGE:
+        ready(p)
 
 
 def fit_edge_kernel(left, right, own, edge, _, __, a, b, ext):
@@ -163,17 +175,15 @@
         b[:, columns] = fitted[ROWS:]
 
 
-def fit(index, own, tiles, left, right, early):
+def fit(index, own, tiles, left, right):
     banded = ((BAND + 1) * TILE, 2 * TILE)
     a, b, own, edge = call(
         fit_inner_kernel,
-        [(index, SMEM), (own, ANY), (tiles, ANY), (early, ANY)],
+        [(index, SMEM), (own, ANY), (tiles.reshape(-1, TILE), ANY)],
         [vmem((ROWS, AUX)), vmem((ROWS, AUX)), vmem((2 * ROWS, AUX)), vmem((4, *banded))],
-        [pltpu.VMEM(tiles.shape, bf16), pltpu.VMEM(banded, bf16), DMA((2,)), DMA((10,))],
+        [pltpu.VMEM((6, *banded), bf16), DMA((2,)), DMA((10, 2))],
         name="fit_inner",
         mib=56,
-        flops=1.2e9,
-        nbytes=9e6,
     )
     return call(
         fit_edge_kernel,
@@ -181,17 +191,18 @@
         [vmem((ROWS, AUX))] * 2,
         [pltpu.VMEM((2 * ROWS, 6 * HALO), bf16)],
         name="fit_edge",
-        flops=8e8,
         aliases={4: 0, 5: 1},
     )
 
 
-def cut(parts, after=(), name=None):
+def cut(parts, after=(), name=None, mib=40):
+    parts = [(*p, 0, AUX)[:5] for p in parts]
+
     def kernel(*refs):
         ins, outs, sems = refs[: len(parts)], refs[-1 - len(parts) : -1], refs[-1]
         copies = [
-            pltpu.make_async_copy(i.at[pl.ds(at, n)], o, sems.at[j])
-            for j, (i, o, (_, at, n)) in enumerate(zip(ins, outs, parts))
+            pltpu.make_async_copy(i.at[pl.ds(r, n), pl.ds(c, m)], o, sems.at[j])
+            for j, (i, o, (_, r, n, c, m)) in enumerate(zip(ins, outs, parts))
         ]
         for c in copies:
             c.start()
@@ -202,12 +213,12 @@
         kernel,
         in_specs=[ANY] * (len(parts) + len(after)),
         out_specs=[ANY] * len(parts),
-        out_shape=[hbm((n, AUX)) for _, _, n in parts],
+        out_shape=[hbm((n, m)) for _, _, n, _, m in parts],
         scratch_shapes=[DMA((len(parts),))],
-        compiler_params=params(),
-        cost_estimate=cost(1e5, 2e6),
+        compiler_params=params(mib),
+        cost_estimate=cost(),
         name=name,
-    )(*[v for v, _, _ in parts], *after)
+    )(*[p[0] for p in parts], *after)
 
 
 def row_copies(parts, out, sems, offsets):
@@ -277,8 +288,6 @@
         ],
         [DMA((5, 2)), DMA((4, 2))],
         name="pair_first",
-        flops=2 * WIDE * WIDE * AUX,
-        nbytes=8e6,
     )
 
 
@@ -299,8 +308,6 @@
         [vmem((WIDE, 3 * ROWS), f32), vmem((WIDE, AUX))],
         [DMA((3, 2))],
         name="pair_early",
-        flops=2 * WIDE * 3 * ROWS * AUX,
-        nbytes=4e6,
     )
 
 
@@ -327,14 +334,11 @@
         [vmem((2 * ROWS, WIDE), f32), hbm((2 * ROWS, WIDE)), vmem((WIDE, AUX))],
         [DMA((3, 2))],
         name="pair_late",
-        flops=2 * WIDE * ROWS * AUX,
-        nbytes=2e6,
         aliases={2: 2},
     )
 
 
-def core_sum_kernel(keep, got_in, *refs):
-    own, s1, s2, s3, got, sem = refs[-6:]
+def core_sum_kernel(keep, got_in, own, s1, s2, s3, got, sem):
     copy = pltpu.make_async_copy(got_in, got, sem)
     copy.start()
     copy.wait()
@@ -345,19 +349,22 @@
         out[...] = value.astype(out.dtype)
 
 
-def core_sum(keep, got, after):
+def core_sum(keep, got):
     width = keep.shape[1]
     return call(
         core_sum_kernel,
-        [(keep, VMEM), (got, ANY)] + [(v, ANY) for v in after],
+        [(keep, VMEM), (got, ANY)],
         [vmem((SHARE, width), f32)] + [hbm((SHARE, width))] * 3,
         [pltpu.VMEM(got.shape, bf16), DMA(())],
         name="core_sum",
     )
 
 
-def amplitude_kernel(vir, occ, chosen, own, *refs, offsets):
-    arrived, out, got, sems = refs[:3], refs[-3], refs[-2], refs[-1]
+BLOCKS = ((0, 0), (3, 0), (1, 0), (0, 1), (3, 1), (2, 0), (1, 1), (2, 1))
+
+
+def amplitude_kernel(vir, occ, chosen, own1, own2, *refs):
+    arrived, out, got, sems = refs[:6], refs[-3], refs[-2], refs[-1]
     copies = [
         pltpu.make_async_copy(r, got.at[i], sems.at[i]) for i, r in enumerate(arrived)
     ]
@@ -376,92 +383,127 @@
     columns = jnp.concatenate(
         [
             vir[pl.ds((((y + step) % 4) * 4 + (3 - x if away else x)) * 2 + z, 1), :]
-            for step, away in offsets
+            for step, away in BLOCKS
         ],
         axis=1,
     )
     denominator = (rows + columns) - occ_total
     for c in copies:
         c.wait()
-    total = own[...]
-    for i in range(3):
-        total = total + got[i].astype(f32)
-    out[...] = (total / denominator).astype(bf16)
-
-
-def amplitude(vir, occ, chosen, own, arrived, offsets, after=()):
-    return call(
-        functools.partial(amplitude_kernel, offsets=offsets),
-        [(vir, VMEM), (occ, SMEM), (chosen, SMEM), (own, VMEM)]
-        + [(v, ANY) for v in (*arrived, *after)],
-        [hbm(own.shape)],
-        [pltpu.VMEM((3, *own.shape), bf16), DMA((3,))],
+    for piece, own in enumerate((own1, own2)):
+        total = own[...]
+        for i in range(3):
+            total = total + got[3 * piece + i].astype(f32)
+        part = slice(piece * WIDE, (piece + 1) * WIDE)
+        out[:, part] = (total / denominator[:, part]).astype(bf16)
+
+
+def amplitude(vir, occ, chosen, own1, own2, arrived):
+    return call(
+        amplitude_kernel,
+        [(vir, VMEM), (occ, SMEM), (chosen, SMEM), (own1, VMEM), (own2, VMEM)]
+        + [(v, ANY) for v in arrived],
+        [hbm((SHARE, 2 * WIDE))],
+        [pltpu.VMEM((6, SHARE, WIDE), bf16), DMA((6,))],
         name="amplitude",
     )[0]
 
 
-def density_part(tcat, b1, b2, blocks, outs):
-    rows = slice(blocks[0] * ROWS, blocks[1] * ROWS)
-    for h in range(2):
-        columns = slice(h * K2, (h + 1) * K2)
-        value = jnp.dot(tcat[rows, :WIDE], b1[:, columns], preferred_element_type=f32)
-        value += jnp.dot(tcat[rows, WIDE:], b2[:, columns], preferred_element_type=f32)
-        for i, out in enumerate(outs):
-            out[:, columns] = value[i * HALF : (i + 1) * HALF].astype(out.dtype)
+def product(tcat, b1, b2, rows, half):
+    columns = slice(half * K2, (half + 1) * K2)
+    value = jnp.dot(tcat[rows, :WIDE], b1[:, columns], preferred_element_type=f32)
+    return value + jnp.dot(tcat[rows, WIDE:], b2[:, columns], preferred_element_type=f32)
 
 
 def density_first_kernel(*refs):
-    mine, other = (refs[0:4], refs[4:8]), refs[8:10]
-    b1, b2, o1, o2, tcat, sems = refs[10:]
+    mine, other = refs[:4], refs[4]
+    b1, b2, d1, d2, x1, z2, tcat, sems = refs[5:]
     high, core = position()[:2]
     copies = []
     for k in range(4):
         at = ((high - k + 4) % 4) * SHARE
         here = pl.multiple_of(core * (2 * ROWS) + at, SHARE)
         there = pl.multiple_of((1 - core) * (2 * ROWS) + at, SHARE)
-        for piece in range(2):
-            columns = pl.ds(piece * WIDE, WIDE)
-            copies.append(
-                pltpu.make_async_copy(
-                    mine[piece][k], tcat.at[pl.ds(here, SHARE), columns], sems.at[piece, k, 0]
-                )
-            )
-            copies.append(
-                pltpu.make_async_copy(
-                    other[piece].at[pl.ds(k * SHARE, SHARE)],
-                    tcat.at[pl.ds(there, SHARE), columns],
-                    sems.at[piece, k, 1],
-                )
-            )
+        away = other.at[pl.ds(k * SHARE, SHARE)]
+        copies += [
+            pltpu.make_async_copy(mine[k], tcat.at[pl.ds(here, SHARE)], sems.at[k, 0]),
+            pltpu.make_async_copy(away, tcat.at[pl.ds(there, SHARE)], sems.at[k, 1]),
+        ]
     for c in copies:
         c.start()
     for c in copies:
         c.wait()
-    density_part(tcat, b1, b2, (3, 4), (o1, o2))
+    for half in range(2):
+        columns = slice(half * K2, (half + 1) * K2)
+        value = product(tcat, b1, b2, slice(3 * ROWS, 4 * ROWS), half).astype(bf16)
+        d1[:, columns] = value[:HALF]
+        d2[:, columns] = value[HALF:]
+        rows = slice(ROWS, ROWS + HALF)
+        x1[:, columns] = product(tcat, b1, b2, rows, half).astype(bf16)
+        rows = slice(2 * ROWS + HALF, 3 * ROWS)
+        z2[:, columns] = product(tcat, b1, b2, rows, half).astype(bf16)
 
 
 def density_first(mine, other, b1, b2):
     return call(
         density_first_kernel,
-        [(v, ANY) for v in (*mine[0], *mine[1], *other)] + [(b1, VMEM), (b2, VMEM)],
-        [hbm((HALF, AUX))] * 2 + [vmem((WIDE, 2 * WIDE))],
-        [DMA((2, 4, 2))],
+        [(v, ANY) for v in (*mine, other)] + [(b1, VMEM), (b2, VMEM)],
+        [hbm((HALF, AUX))] * 4 + [vmem((WIDE, 2 * WIDE))],
+        [DMA((4, 2))],
         name="density_first",
-        flops=2 * ROWS * 2 * WIDE * AUX,
-    )
-
-
-def density(tcat, b1, b2, blocks, types):
-    def kernel(tcat, b1, b2, *outs):
-        density_part(tcat, b1, b2, blocks, outs)
-
-    return call(
-        kernel,
-        [(tcat, VMEM), (b1, VMEM), (b2, VMEM)],
-        [hbm((HALF, AUX), t) for t in types],
-        name="density",
-        flops=2 * (blocks[1] - blocks[0]) * ROWS * 2 * WIDE * AUX,
-    )
+    )
+
+
+def density_second_kernel(tcat, b1, b2, from_x, from_z, x2, z1, own, got_x, got_z, sems):
+    copies = [
+        pltpu.make_async_copy(from_x, got_x, sems.at[0]),
+        pltpu.make_async_copy(from_z, got_z, sems.at[1]),
+    ]
+    for c in copies:
+        c.start()
+    for half in range(2):
+        columns = slice(half * K2, (half + 1) * K2)
+        value = product(tcat, b1, b2, slice(ROWS + HALF, 2 * ROWS + HALF), half)
+        if half == 0:
+            for c in copies:
+                c.wait()
+        x2[:, columns] = (value[:HALF] + got_z[:, columns].astype(f32)).astype(bf16)
+        z1[:, columns] = (value[HALF:] + got_x[:, columns].astype(f32)).astype(bf16)
+        own[:, columns] = product(tcat, b1, b2, slice(0, ROWS), half)
+
+
+def density_second(tcat, b1, b2, from_x, from_z):
+    return call(
+        density_second_kernel,
+        [(v, VMEM) for v in (tcat, b1, b2)] + [(from_x, ANY), (from_z, ANY)],
+        [hbm((HALF, AUX))] * 2 + [vmem((ROWS, AUX), f32)],
+        [pltpu.VMEM((HALF, AUX), bf16)] * 2 + [DMA((2,))],
+        name="density_second",
+    )
+
+
+def total_kernel(own, x1, z1, x2, z2, out, got, sems):
+    copies = [
+        pltpu.make_async_copy(v, got.at[i], sems.at[i]) for i, v in enumerate((x1, z1, x2, z2))
+    ]
+    for c in copies:
+        c.start()
+    for h in range(2):
+        rows = slice(h * HALF, (h + 1) * HALF)
+        for c in copies[2 * h : 2 * h + 2]:
+            c.wait()
+        value = own[rows] + got[2 * h].astype(f32) + got[2 * h + 1].astype(f32)
+        out[rows] = value.astype(bf16)
+
+
+def total(own, x1, z1, x2, z2):
+    return call(
+        total_kernel,
+        [(own, VMEM)] + [(v, ANY) for v in (x1, z1, x2, z2)],
+        [hbm((ROWS, AUX))],
+        [pltpu.VMEM((4, HALF, AUX), bf16), DMA((4,))],
+        name="total",
+    )[0]
 
 
 def local(integrals, tiles, tile_index, vir_energy, occ_energy, pair_index):
@@ -469,9 +511,14 @@
     vir = vir_energy.reshape(-1, ROWS)
     up = [(g, g + 1) for g in range(7)]
     down = [(g + 1, g) for g in range(7)]
-    left = lax.ppermute(window[:, AUX - HALO :], "grp", up)
-    right = lax.ppermute(window[:, :HALO], "grp", down)
-    a, b = fit(tile_index.T, window, tiles, left, right, vir)
+    last, first = cut(
+        [(window, 0, 2 * ROWS, AUX - HALO, HALO), (window, 0, 2 * ROWS, 0, HALO)],
+        name="cut_halo",
+        mib=60,
+    )
+    left = lax.ppermute(last, "grp", up)
+    right = lax.ppermute(first, "grp", down)
+    a, b = fit(tile_index.T, window, tiles, left, right)
 
     with jax.named_scope("first"):
         bm = send_y(b, 1)
@@ -479,7 +526,7 @@
         bo = send_outer(b)
         ax = send_inner(a)
         az = send_z(a)
-    az1, ax2 = cut([(az, 0, HALF), (ax, HALF, HALF)], (bm, bp, bo), name="cut_a")
+    az1, ax2 = cut([(az, 0, HALF), (ax, HALF, HALF)], (bm, bp, bo, vir), name="cut_a")
     with jax.named_scope("second"):
         d1 = send_inner(az1)
         d2 = send_z(ax2)
@@ -487,9 +534,9 @@
         b2 = send_y(bp, -1)
         bop = send_outer(bp)
 
-    def core_total(keep, send, after=()):
+    def core_total(keep, send):
         with jax.named_scope("core"):
-            return core_sum(keep, send_core(send), after)
+            return core_sum(keep, send_core(send))
 
     def shares(s):
         with jax.named_scope("shares"):
@@ -512,29 +559,22 @@
         c2 = send_y(c2, 1)
         c3 = send_y(c3, -1)
     early, b_second = pair_early(acat, (bom, b2, bop))
-    offsets = ((0, 0), (3, 0), (1, 0), (0, 1))
-    mine1 = amplitude(vir, occ_energy, pair_index, own, arrived, offsets, (early,))
-    keep, send, b_second = pair_late(acat, early, b_second, (c1, c2, c3), (mine1,))
-    mine1 = spread(mine1)
-    own, *s = core_total(keep, send, (mine1[1], mine1[3]))
-    arrived = shares(s)
-    offsets = ((3, 1), (2, 0), (1, 1), (2, 1))
-    mine2 = spread(amplitude(vir, occ_energy, pair_index, own, arrived, offsets))
-    other = (other_core(mine1), other_core(mine2))
-
-    to_d1, to_d2, tcat = density_first((mine1, mine2), other, b_first, b_second)
-    x1, x2, z1, z2 = density(tcat, b_first, b_second, (1, 3), (bf16, f32, f32, bf16))
-    o1, o2 = density(tcat, b_first, b_second, (0, 1), (f32, f32))
+    keep, send, b_second = pair_late(acat, early, b_second, (c1, c2, c3), arrived)
+    own2, *s = core_total(keep, send)
+    arrived += shares(s)
+    mine = spread(amplitude(vir, occ_energy, pair_index, own, own2, arrived))
+    other = other_core(mine)
+    to_d1, to_d2, x1, z2, tcat = density_first(mine, other, b_first, b_second)
     with jax.named_scope("out"):
         from_x = send_inner(to_d1)
         from_z = send_z(to_d2)
         got_x1 = send_inner(x1)
         got_z2 = send_z(z2)
-        got_z1 = send_z((z1 + from_x.astype(f32)).astype(bf16))
-        got_x2 = send_inner((x2 + from_z.astype(f32)).astype(bf16))
-    h1 = o1 + got_x1.astype(f32) + got_z1.astype(f32)
-    h2 = o2 + got_x2.astype(f32) + got_z2.astype(f32)
-    return jnp.concatenate([h1, h2], axis=0).astype(bf16)
+    x2, z1, own = density_second(tcat, b_first, b_second, from_x, from_z)
+    with jax.named_scope("out"):
+        got_z1 = send_z(z1)
+        got_x2 = send_inner(x2)
+    return total(own, got_x1, got_z1, got_x2, got_z2)
 
 
 def solution(mesh):

time: 179 us -> 196 us (1.095)
  Pallas kernels: 26.8 us -> 55 us
  waiting for transfers between devices: 85.3 us -> 79.4 us
  local copies, waits for them, and re-layouts: 3.37 us -> 0.09 us
    pallas_call x2 -> x3, Pallas kernels: 1.19 us -> 22.9 us  [cut(): pl.pallas_call(kernel, in_specs=[ANY] * (len(parts) + len(after)), out_sp...]
    ppermute x6, waiting for transfers between devices: 20.3 us -> 8.1 us  [send_y(): return lax.ppermute(v, 'blk', pairs)]
    ppermute x5, waiting for transfers between devices: 18.1 us -> 27.2 us  [send_z(): return lax.ppermute(v, 'blk', pairs)]
    pallas_call x12 -> x11, Pallas kernels: 25.6 us -> 32.1 us  [call(): pl.pallas_call(kernel, in_specs=[spec for _, spec in args], out_specs=[VM...]
    ppermute x12 -> x9, starting transfers between devices: 27.1 us -> 22.1 us  [send_high(): return lax.ppermute(v, 'grp', [(g, (g + 2 * step) % 8) for g in range(8)])]
    ppermute x5, starting transfers between devices: 3.2 us -> 6.99 us  [send_z(): return lax.ppermute(v, 'blk', pairs)]
    ppermute x3, waiting for transfers between devices: 6.34 us -> 2.63 us  [send_outer(): return lax.ppermute(v, 'blk', pairs)]
    ppermute x4 -> x3, waiting for transfers between devices: 3.11 us -> 5.07 us  [send_core(): return lax.ppermute(v, 'grp', [(g, g ^ 1) for g in range(8)])]
  transfers between devices with their start and end apart: 37 -> 33, of which waited for: 23 -> 23; matrix products, arithmetic and copies ran while one was open for 1% -> 0% of each run, Pallas kernels for 12% -> 10%
where the time goes in v4:
time: 196 us
  waiting for transfers between devices  79.4 us (41%)
  starting transfers between devices  60.7 us (31%)
  Pallas kernels  55 us (28%)
    pallas_call x11, Pallas kernels, call(): pl.pallas_call(kernel, in_specs=[spec for _, spec in args], out_specs=[VM...  32.1 us
    ppermute x5, waiting for transfers between devices, send_z(): return lax.ppermute(v, 'blk', pairs)  27.2 us
    ppermute x9, waiting for transfers between devices, send_high(): return lax.ppermute(v, 'grp', [(g, (g + 2 * step) % 8) for g in range(8)])  24.5 us
    pallas_call x3, Pallas kernels, cut(): pl.pallas_call(kernel, in_specs=[ANY] * (len(parts) + len(after)), out_sp...  22.9 us
    ppermute x9, starting transfers between devices, send_high(): return lax.ppermute(v, 'grp', [(g, (g + 2 * step) % 8) for g in range(8)])  22.1 us
    ppermute x5, waiting for transfers between devices, send_inner(): return lax.ppermute(v, 'blk', pairs)  9.58 us
    ppermute x6, starting transfers between devices, send_y(): return lax.ppermute(v, 'blk', pairs)  8.44 us
    ppermute x6, waiting for transfers between devices, send_y(): return lax.ppermute(v, 'blk', pairs)  8.1 us
  transfers between devices with their start and end apart: 33, of which 23 were waited for; matrix products, arithmetic and copies ran while one was open for 0% of the time, Pallas kernels for 10%

profile of v4, /device:TPU:1, one launch (start us, length us, event | category | flops | bytes accessed | tf_op | source)
XLA Modules:
  0.0 195.7 jit_solution(4377044279020747648)
XLA Ops:
  0.0 21.0 %cut_halo.1 = (bf16[320,512]{1,0:T(8,128)(2,1)}, bf16[320,512]{1,0:T(8,128)(2,1)}) custom-call(bf16[320,2560]{1,0:T(8,128)(2,1)} %bitcast.3, bf16[320,2560]{1,0:T(8,128)(2,1)} %bitcast.4), custom_call_target="tpu_custom_call" | custom-call | flops 1000 | bytes 1000 | tf_op jit(solution)/shard_map/cut_halo/pallas_call | solution.py:212
  21.0 6.3 %collective-permute-start = (bf16[320,512]{1,0:T(8,128)(2,1)}, bf16[320,512]{1,0:T(8,128)(2,1)S(1)}, u32[]{:S(2)}, u32[]{:S(2)}) collective-permute-start(bf16[320,512]{1,0:T(8,128)(2,1)} %get-tuple-element.43), channel_id=1, source_target_pairs={{0,32},{32,64},{64,96},{96,128},{128,160},{160,192},{192,224},{1,3... | collective-permute-start | bytes 983048 | tf_op jit(solution)/shard_map/ppermute | solution.py:519
  27.3 1.9 collective-permute-start.1
  29.2 8.8 %fit_inner.1 = (bf16[160,2560]{1,0:T(8,128)(2,1)S(1)}, bf16[160,2560]{1,0:T(8,128)(2,1)S(1)}, bf16[320,2560]{1,0:T(8,128)(2,1)S(1)}, bf16[4,1280,256]{2,1,0:T(8,128)(2,1)S(1)}) custom-call(s32[2,180]{1,0:T(2,128)} %bitcast.7, bf16[320,2560]{1,0:T(8,128)(2,1)} %bitcast.5, bf16[23040,128]{1,0:T(8,128)(2,1)} %bitcast.6), custom_call_target="tpu_custom_call" | custom-call | flops 1000 | bytes 1000 | tf_op jit(solution)/shard_map/fit_inner/pallas_call | solution.py:90
  38.0 2.4 %collective-permute-done.1.right = bf16[320,512]{1,0:T(8,128)(2,1)S(1)} collective-permute-done((bf16[320,512]{1,0:T(8,128)(2,1)}, bf16[320,512]{1,0:T(8,128)(2,1)S(1)}, u32[]{:S(2)}, u32[]{:S(2)}) %collective-permute-start.1) | collective-permute-done | bytes 327712 | tf_op jit(solution)/shard_map/ppermute | solution.py:520
  41.5 1.3 collective-permute-start.2
  42.8 1.8 collective-permute-start.6
  44.6 2.7 %collective-permute-start.5 = (bf16[160,2560]{1,0:T(8,128)(2,1)S(1)}, bf16[160,2560]{1,0:T(8,128)(2,1)S(1)}, u32[]{:S(2)}, u32[]{:S(2)}) collective-permute-start(bf16[160,2560]{1,0:T(8,128)(2,1)S(1)} %get-tuple-element.50.refs_5_), channel_id=1, source_target_pairs={{0,24},{1,25},{2,26},{3,27},{4,28},{5,29},{6,30},{7,31},{8,0},{9,1... | collective-permute-start | bytes 2457608 | tf_op jit(solution)/shard_map/first/ppermute | solution.py:31
  47.4 10.8 %collective-permute-done.3.refs_0_.refs_2_ = bf16[160,2560]{1,0:T(8,128)(2,1)} collective-permute-done((bf16[160,2560]{1,0:T(8,128)(2,1)S(1)}, bf16[160,2560]{1,0:T(8,128)(2,1)}, u32[]{:S(2)}, u32[]{:S(2)}) %collective-permute-start.3) | collective-permute-done | bytes 819232 | tf_op jit(solution)/shard_map/first/ppermute | solution.py:46
  58.2 2.6 %collective-permute-done.6.refs_4_.refs_8_ = bf16[160,2560]{1,0:T(8,128)(2,1)} collective-permute-done((bf16[160,2560]{1,0:T(8,128)(2,1)S(1)}, bf16[160,2560]{1,0:T(8,128)(2,1)}, u32[]{:S(2)}, u32[]{:S(2)}) %collective-permute-start.6) | collective-permute-done | bytes 819232 | tf_op jit(solution)/shard_map/first/ppermute | solution.py:36
  60.9 1.3 collective-permute-done.5.refs_3_.refs_7_
  62.2 3.5 %collective-permute-done.4.refs_2_.refs_6_ = bf16[160,2560]{1,0:T(8,128)(2,1)} collective-permute-done((bf16[160,2560]{1,0:T(8,128)(2,1)S(1)}, bf16[160,2560]{1,0:T(8,128)(2,1)}, u32[]{:S(2)}, u32[]{:S(2)}) %collective-permute-start.4) | collective-permute-done | bytes 819232 | tf_op jit(solution)/shard_map/first/ppermute | solution.py:31
  65.7 1.1 cut_a.1
  68.1 2.6 %collective-permute-start.11 = (bf16[160,2560]{1,0:T(8,128)(2,1)S(1)}, bf16[160,2560]{1,0:T(8,128)(2,1)S(1)}, u32[]{:S(2)}, u32[]{:S(2)}) collective-permute-start(bf16[160,2560]{1,0:T(8,128)(2,1)S(1)} %collective-permute-done.5.refs_3_.refs_7_), channel_id=1, source_target_pairs={{0,24},{1,25},{2,26},{3,27},{4,28},{5,29},{6,30},{7,31},{8,0},{9,1... | collective-permute-start | bytes 2457608 | tf_op jit(solution)/shard_map/second/ppermute | solution.py:31
  70.7 5.9 %collective-permute-done.7.refs_3_ = bf16[80,2560]{1,0:T(8,128)(2,1)S(1)} collective-permute-done((bf16[80,2560]{1,0:T(8,128)(2,1)S(1)}, bf16[80,2560]{1,0:T(8,128)(2,1)S(1)}, u32[]{:S(2)}, u32[]{:S(2)}) %collective-permute-start.7) | collective-permute-done | bytes 409632 | tf_op jit(solution)/shard_map/second/ppermute | solution.py:41
  77.1 4.8 %pair_first.1 = (f32[320,640]{1,0:T(8,128)S(1)}, bf16[320,640]{1,0:T(8,128)(2,1)S(1)}, bf16[640,2560]{1,0:T(8,128)(2,1)S(1)}, bf16[640,2560]{1,0:T(8,128)(2,1)S(1)}) custom-call(bf16[160,2560]{1,0:T(8,128)(2,1)S(1)} %get-tuple-element.49.refs_0_, bf16[160,2560]{1,0:T(8,128)(2,1)} %collective-permute-done.2.refs_1_, ...), custom_call_target="tpu_custom_call" | custom-call | flops 1000 | bytes 1000 | tf_op jit(solution)/shard_map/pair_first/pallas_call | solution.py:90
  82.1 1.7 collective-permute-done.9.got_in
  84.1 2.9 %collective-permute-done.10.refs_0_.refs_1_ = bf16[160,2560]{1,0:T(8,128)(2,1)S(1)} collective-permute-done((bf16[160,2560]{1,0:T(8,128)(2,1)}, bf16[160,2560]{1,0:T(8,128)(2,1)S(1)}, u32[]{:S(2)}, u32[]{:S(2)}) %collective-permute-start.10) | collective-permute-done | bytes 819232 | tf_op jit(solution)/shard_map/second/ppermute | solution.py:31
  88.2 2.3 %collective-permute-start.13 = (bf16[64,2560]{1,0:T(8,128)(2,1)S(1)}, bf16[64,2560]{1,0:T(8,128)(2,1)S(1)}, u32[]{:S(2)}, u32[]{:S(2)}) collective-permute-start(bf16[64,2560]{1,0:T(8,128)(2,1)S(1)} %get-tuple-element.59), channel_id=1, source_target_pairs={{0,6},{1,7},{2,4},{3,5},{4,2},{5,3},{6,0},{7,1},{8,14},{9,15},{10,... | collective-permute-start | bytes 983048 | tf_op jit(solution)/shard_map/third/ppermute | solution.py:36
  90.5 3.1 %collective-permute-start.15 = (bf16[48,2560]{1,0:T(8,128)(2,1)S(1)}, bf16[48,2560]{1,0:T(8,128)(2,1)S(1)}, u32[]{:S(2)}, u32[]{:S(2)}) collective-permute-start(bf16[48,2560]{1,0:T(8,128)(2,1)S(1)} %get-tuple-element.61), channel_id=1, source_target_pairs={{0,24},{1,25},{2,26},{3,27},{4,28},{5,29},{6,30},{7,31},{8,0},{9,1... | collective-permute-start | bytes 737288 | tf_op jit(solution)/shard_map/third/ppermute | solution.py:31
  93.6 7.6 %collective-permute-start.16 = (bf16[80,640]{1,0:T(8,128)(2,1)S(1)}, bf16[80,640]{1,0:T(8,128)(2,1)S(1)}, u32[]{:S(2)}, u32[]{:S(2)}) collective-permute-start(bf16[80,640]{1,0:T(8,128)(2,1)S(1)} %get-tuple-element.62), channel_id=1, source_target_pairs={{0,64},{32,96},{64,128},{96,160},{128,192},{160,224},{192,0},{224,... | collective-permute-start | bytes 307208 | tf_op jit(solution)/shard_map/shares/ppermute | solution.py:54
  101.2 2.1 %collective-permute-done.16.refs_3_.refs_0_ = bf16[80,640]{1,0:T(8,128)(2,1)S(1)} collective-permute-done((bf16[80,640]{1,0:T(8,128)(2,1)S(1)}, bf16[80,640]{1,0:T(8,128)(2,1)S(1)}, u32[]{:S(2)}, u32[]{:S(2)}) %collective-permute-start.16) | collective-permute-done | bytes 102432 | tf_op jit(solution)/shard_map/shares/ppermute | solution.py:54
  103.2 1.2 collective-permute-start.18
  104.5 2.3 %pair_early.1 = (f32[640,480]{1,0:T(8,128)S(1)}, bf16[640,2560]{1,0:T(8,128)(2,1)S(1)}) custom-call(bf16[640,2560]{1,0:T(8,128)(2,1)S(1)} %get-tuple-element.56.acat, bf16[160,2560]{1,0:T(8,128)(2,1)S(1)} %collective-permute-done.10.refs_0_.refs_1_, bf16[160,2560]{1,0:T(8,128)(2,1)S(1)} %collective-permute-done.11.refs_1_.refs_0_, ...), custom_call_target="tpu_custom_call" | custom-call | flops 1000 | bytes 1000 | tf_op jit(solution)/shard_map/pair_early/pallas_call | solution.py:90
  106.8 3.0 %collective-permute-done.17.refs_4_.refs_1_ = bf16[80,640]{1,0:T(8,128)(2,1)S(1)} collective-permute-done((bf16[80,640]{1,0:T(8,128)(2,1)S(1)}, bf16[80,640]{1,0:T(8,128)(2,1)S(1)}, u32[]{:S(2)}, u32[]{:S(2)}) %collective-permute-start.17) | collective-permute-done | bytes 102432 | tf_op jit(solution)/shard_map/shares/ppermute | solution.py:54
  109.8 1.5 pair_late.1
  111.4 4.8 %collective-permute-start.19 = (bf16[320,640]{1,0:T(8,128)(2,1)S(1)}, bf16[320,640]{1,0:T(8,128)(2,1)S(1)}, u32[]{:S(2)}, u32[]{:S(2)}) collective-permute-start(bf16[320,640]{1,0:T(8,128)(2,1)S(1)} %get-tuple-element.66), channel_id=1, source_target_pairs={{0,32},{32,0},{64,96},{96,64},{128,160},{160,128},{192,224},{224,1... | collective-permute-start | bytes 1228808 | tf_op jit(solution)/shard_map/core/ppermute | solution.py:50
  116.1 1.4 collective-permute-done.19.got_in
  117.8 2.5 %collective-permute-start.20 = (bf16[80,640]{1,0:T(8,128)(2,1)S(1)}, bf16[80,640]{1,0:T(8,128)(2,1)S(1)}, u32[]{:S(2)}, u32[]{:S(2)}) collective-permute-start(bf16[80,640]{1,0:T(8,128)(2,1)S(1)} %get-tuple-element.68), channel_id=1, source_target_pairs={{0,64},{32,96},{64,128},{96,160},{128,192},{160,224},{192,0},{224,... | collective-permute-start | bytes 307208 | tf_op jit(solution)/shard_map/shares/ppermute | solution.py:54
  120.4 3.4 %collective-permute-start.22 = (bf16[80,640]{1,0:T(8,128)(2,1)S(1)}, bf16[80,640]{1,0:T(8,128)(2,1)S(1)}, u32[]{:S(2)}, u32[]{:S(2)}) collective-permute-start(bf16[80,640]{1,0:T(8,128)(2,1)S(1)} %get-tuple-element.70), channel_id=1, source_target_pairs={{0,192},{32,224},{64,0},{96,32},{128,64},{160,96},{192,128},{224,1... | collective-permute-start | bytes 307208 | tf_op jit(solution)/shard_map/shares/ppermute | solution.py:54
  124.1 4.8 %collective-permute-done.21.refs_4_ = bf16[80,640]{1,0:T(8,128)(2,1)S(1)} collective-permute-done((bf16[80,640]{1,0:T(8,128)(2,1)S(1)}, bf16[80,640]{1,0:T(8,128)(2,1)S(1)}, u32[]{:S(2)}, u32[]{:S(2)}) %collective-permute-start.21) | collective-permute-done | bytes 102432 | tf_op jit(solution)/shard_map/shares/ppermute | solution.py:54
  128.9 1.8 amplitude.1.refs_0_
  130.7 2.2 %collective-permute-start.25 = (bf16[80,1280]{1,0:T(8,128)(2,1)S(1)}, bf16[80,1280]{1,0:T(8,128)(2,1)S(1)}, u32[]{:S(2)}, u32[]{:S(2)}) collective-permute-start(bf16[80,1280]{1,0:T(8,128)(2,1)S(1)} %amplitude.1.refs_0_), channel_id=1, source_target_pairs={{0,192},{32,224},{64,0},{96,32},{128,64},{160,96},{192,128},{224,1... | collective-permute-start | bytes 614408 | tf_op jit(solution)/shard_map/spread/ppermute | solution.py:54
  132.8 5.1 %collective-permute-start.24 = (bf16[80,1280]{1,0:T(8,128)(2,1)S(1)}, bf16[80,1280]{1,0:T(8,128)(2,1)S(1)}, u32[]{:S(2)}, u32[]{:S(2)}) collective-permute-start(bf16[80,1280]{1,0:T(8,128)(2,1)S(1)} %amplitude.1.refs_0_), channel_id=1, source_target_pairs={{0,128},{32,160},{64,192},{96,224},{128,0},{160,32},{192,64},{224,... | collective-permute-start | bytes 614408 | tf_op jit(solution)/shard_map/spread/ppermute | solution.py:54
  138.0 2.9 %collective-permute-done.25.refs_3_ = bf16[80,1280]{1,0:T(8,128)(2,1)S(1)} collective-permute-done((bf16[80,1280]{1,0:T(8,128)(2,1)S(1)}, bf16[80,1280]{1,0:T(8,128)(2,1)S(1)}, u32[]{:S(2)}, u32[]{:S(2)}) %collective-permute-start.25) | collective-permute-done | bytes 204832 | tf_op jit(solution)/shard_map/spread/ppermute | solution.py:54
  140.8 3.7 %collective-permute-done.24.refs_2_ = bf16[80,1280]{1,0:T(8,128)(2,1)S(1)} collective-permute-done((bf16[80,1280]{1,0:T(8,128)(2,1)S(1)}, bf16[80,1280]{1,0:T(8,128)(2,1)S(1)}, u32[]{:S(2)}, u32[]{:S(2)}) %collective-permute-start.24) | collective-permute-done | bytes 204832 | tf_op jit(solution)/shard_map/spread/ppermute | solution.py:54
  144.6 7.7 %collective-permute-done.23.refs_1_ = bf16[80,1280]{1,0:T(8,128)(2,1)S(1)} collective-permute-done((bf16[80,1280]{1,0:T(8,128)(2,1)S(1)}, bf16[80,1280]{1,0:T(8,128)(2,1)S(1)}, u32[]{:S(2)}, u32[]{:S(2)}) %collective-permute-start.23) | collective-permute-done | bytes 204832 | tf_op jit(solution)/shard_map/spread/ppermute | solution.py:54
  153.2 2.0 %collective-permute-done.26.refs_4_ = bf16[320,1280]{1,0:T(8,128)(2,1)S(1)} collective-permute-done((bf16[320,1280]{1,0:T(8,128)(2,1)S(1)}, bf16[320,1280]{1,0:T(8,128)(2,1)S(1)}, u32[]{:S(2)}, u32[]{:S(2)}) %collective-permute-start.26) | collective-permute-done | bytes 819232 | tf_op jit(solution)/shard_map/other/ppermute | solution.py:50
  155.2 5.7 %density_first.1 = (bf16[80,2560]{1,0:T(8,128)(2,1)S(1)}, bf16[80,2560]{1,0:T(8,128)(2,1)S(1)}, bf16[80,2560]{1,0:T(8,128)(2,1)S(1)}, bf16[80,2560]{1,0:T(8,128)(2,1)S(1)}, bf16[640,1280]{1,0:T(8,128)(2,1)S(1)}) custom-call(bf16[80,1280]{1,0:T(8,128)(2,1)S(1)} %amplitude.1.refs_0_, bf16[80,1280]{1,0:T(8,128)(2,1)S(1)} %collective-permute-done.23.refs_1_, ...), custom_call_target="tpu_custom_call" | custom-call | flops 1000 | bytes 1000 | tf_op jit(solution)/shard_map/density_first/pallas_call | solution.py:90
  160.9 5.6 %collective-permute-start.28 = (bf16[80,2560]{1,0:T(8,128)(2,1)S(1)}, bf16[80,2560]{1,0:T(8,128)(2,1)S(1)}, u32[]{:S(2)}, u32[]{:S(2)}) collective-permute-start(bf16[80,2560]{1,0:T(8,128)(2,1)S(1)} %get-tuple-element.75), channel_id=1, source_target_pairs={{0,1},{1,0},{2,3},{3,2},{4,5},{5,4},{6,7},{7,6},{8,9},{9,8},{10,11... | collective-permute-start | bytes 1228808 | tf_op jit(solution)/shard_map/out/ppermute | solution.py:46
  166.6 1.4 collective-permute-start.29
  167.9 3.7 %collective-permute-done.27.from_x = bf16[80,2560]{1,0:T(8,128)(2,1)S(1)} collective-permute-done((bf16[80,2560]{1,0:T(8,128)(2,1)S(1)}, bf16[80,2560]{1,0:T(8,128)(2,1)S(1)}, u32[]{:S(2)}, u32[]{:S(2)}) %collective-permute-start.27) | collective-permute-done | bytes 409632 | tf_op jit(solution)/shard_map/out/ppermute | solution.py:41
  171.6 4.3 %collective-permute-done.28.from_z = bf16[80,2560]{1,0:T(8,128)(2,1)S(1)} collective-permute-done((bf16[80,2560]{1,0:T(8,128)(2,1)S(1)}, bf16[80,2560]{1,0:T(8,128)(2,1)S(1)}, u32[]{:S(2)}, u32[]{:S(2)}) %collective-permute-start.28) | collective-permute-done | bytes 409632 | tf_op jit(solution)/shard_map/out/ppermute | solution.py:46
  175.9 3.6 %density_second.1 = (bf16[80,2560]{1,0:T(8,128)(2,1)S(1)}, bf16[80,2560]{1,0:T(8,128)(2,1)S(1)}, f32[160,2560]{1,0:T(8,128)S(1)}) custom-call(bf16[640,1280]{1,0:T(8,128)(2,1)S(1)} %get-tuple-element.73.tcat, bf16[640,2560]{1,0:T(8,128)(2,1)S(1)} %get-tuple-element.71.refs_5_.b1, bf16[640,2560]{1,0:T(8,128)(2,1)S(1)} %get-tuple-element.72.refs_6_.b2, ...), custom_call_target="tpu_custom_call" | custom-call | flops 1000 | bytes 1000 | tf_op jit(solution)/shard_map/density_second/pallas_call | solution.py:90
  179.6 1.3 collective-permute-start.30
  182.0 2.7 %collective-permute-done.32.z2 = bf16[80,2560]{1,0:T(8,128)(2,1)S(1)} collective-permute-done((bf16[80,2560]{1,0:T(8,128)(2,1)S(1)}, bf16[80,2560]{1,0:T(8,128)(2,1)S(1)}, u32[]{:S(2)}, u32[]{:S(2)}) %collective-permute-start.32) | collective-permute-done | bytes 409632 | tf_op jit(solution)/shard_map/out/ppermute | solution.py:46
  184.7 8.8 %collective-permute-done.30.z1 = bf16[80,2560]{1,0:T(8,128)(2,1)S(1)} collective-permute-done((bf16[80,2560]{1,0:T(8,128)(2,1)S(1)}, bf16[80,2560]{1,0:T(8,128)(2,1)S(1)}, u32[]{:S(2)}, u32[]{:S(2)}) %collective-permute-start.30) | collective-permute-done | bytes 409632 | tf_op jit(solution)/shard_map/out/ppermute | solution.py:46
  193.5 2.0 %total.1 = bf16[160,2560]{1,0:T(8,128)(2,1)} custom-call(f32[160,2560]{1,0:T(8,128)S(1)} %get-tuple-element.76.own, bf16[80,2560]{1,0:T(8,128)(2,1)S(1)} %collective-permute-done.29.x1, bf16[80,2560]{1,0:T(8,128)(2,1)S(1)} %collective-permute-done.30.z1, bf16[80,2560]{1,0:T(8,128)(2,1)S(1)} %collective-permute-done.31.x2, ...), custom_call_target="tpu_custom_call" | custom-call | flops 1000 | bytes 1000 | tf_op jit(solution)/shard_map/total/pallas_call | solution.py:90
  (40 shorter events, 7.4 us)
Async XLA Ops:
  21.0 17.0 %collective-permute-start = (bf16[320,512]{1,0:T(8,128)(2,1)}, bf16[320,512]{1,0:T(8,128)(2,1)S(1)}, u32[]{:S(2)}, u32[]{:S(2)}) collective-permute-start(bf16[320,512]{1,0:T(8,128)(2,1)} %get-tuple-element.43), channel_id=1, source_target_pairs={{0,32},{32,64},{64,96},{96,128},{128,160},{160,192},{192,224},{1,3... | collective-permute-start | bytes 983048 | tf_op jit(solution)/shard_map/ppermute | solution.py:519
  27.3 13.1 %collective-permute-start.1 = (bf16[320,512]{1,0:T(8,128)(2,1)}, bf16[320,512]{1,0:T(8,128)(2,1)S(1)}, u32[]{:S(2)}, u32[]{:S(2)}) collective-permute-start(bf16[320,512]{1,0:T(8,128)(2,1)} %get-tuple-element.44), channel_id=1, source_target_pairs={{32,0},{64,32},{96,64},{128,96},{160,128},{192,160},{224,192},{33,... | collective-permute-start | bytes 983048 | tf_op jit(solution)/shard_map/ppermute | solution.py:520
  40.4 7.0 %copy-start.2 = (f32[5120]{0:T(1024)S(1)}, f32[5120]{0:T(1024)}, u32[]{:S(2)}) copy-start(f32[5120]{0:T(1024)} %param.9) | copy-start | bytes 61444
  41.4 16.9 %collective-permute-start.3 = (bf16[160,2560]{1,0:T(8,128)(2,1)S(1)}, bf16[160,2560]{1,0:T(8,128)(2,1)}, u32[]{:S(2)}, u32[]{:S(2)}) collective-permute-start(bf16[160,2560]{1,0:T(8,128)(2,1)S(1)} %get-tuple-element.49.refs_0_), channel_id=1, source_target_pairs={{0,1},{1,0},{2,3},{3,2},{4,5},{5,4},{6,7},{7,6},{8,9},{9,8},{10,11... | collective-permute-start | bytes 2457608 | tf_op jit(solution)/shard_map/first/ppermute | solution.py:46
  41.5 16.8 %collective-permute-start.2 = (bf16[160,2560]{1,0:T(8,128)(2,1)S(1)}, bf16[160,2560]{1,0:T(8,128)(2,1)}, u32[]{:S(2)}, u32[]{:S(2)}) collective-permute-start(bf16[160,2560]{1,0:T(8,128)(2,1)S(1)} %get-tuple-element.49.refs_0_), channel_id=1, source_target_pairs={{0,2},{1,3},{2,0},{3,1},{4,6},{5,7},{6,4},{7,5},{8,10},{9,11},{10,... | collective-permute-start | bytes 2457608 | tf_op jit(solution)/shard_map/first/ppermute | solution.py:41
  42.8 18.1 %collective-permute-start.6 = (bf16[160,2560]{1,0:T(8,128)(2,1)S(1)}, bf16[160,2560]{1,0:T(8,128)(2,1)}, u32[]{:S(2)}, u32[]{:S(2)}) collective-permute-start(bf16[160,2560]{1,0:T(8,128)(2,1)S(1)} %get-tuple-element.50.refs_5_), channel_id=1, source_target_pairs={{0,6},{1,7},{2,4},{3,5},{4,2},{5,3},{6,0},{7,1},{8,14},{9,15},{10,... | collective-permute-start | bytes 2457608 | tf_op jit(solution)/shard_map/first/ppermute | solution.py:36
  44.6 17.6 %collective-permute-start.5 = (bf16[160,2560]{1,0:T(8,128)(2,1)S(1)}, bf16[160,2560]{1,0:T(8,128)(2,1)S(1)}, u32[]{:S(2)}, u32[]{:S(2)}) collective-permute-start(bf16[160,2560]{1,0:T(8,128)(2,1)S(1)} %get-tuple-element.50.refs_5_), channel_id=1, source_target_pairs={{0,24},{1,25},{2,26},{3,27},{4,28},{5,29},{6,30},{7,31},{8,0},{9,1... | collective-permute-start | bytes 2457608 | tf_op jit(solution)/shard_map/first/ppermute | solution.py:31
  47.4 18.3 %collective-permute-start.4 = (bf16[160,2560]{1,0:T(8,128)(2,1)S(1)}, bf16[160,2560]{1,0:T(8,128)(2,1)}, u32[]{:S(2)}, u32[]{:S(2)}) collective-permute-start(bf16[160,2560]{1,0:T(8,128)(2,1)S(1)} %get-tuple-element.50.refs_5_), channel_id=1, source_target_pairs={{0,8},{1,9},{2,10},{3,11},{4,12},{5,13},{6,14},{7,15},{8,16},{9,17... | collective-permute-start | bytes 2457608 | tf_op jit(solution)/shard_map/first/ppermute | solution.py:31
  66.8 9.7 %collective-permute-start.7 = (bf16[80,2560]{1,0:T(8,128)(2,1)S(1)}, bf16[80,2560]{1,0:T(8,128)(2,1)S(1)}, u32[]{:S(2)}, u32[]{:S(2)}) collective-permute-start(bf16[80,2560]{1,0:T(8,128)(2,1)S(1)} %get-tuple-element.51), channel_id=1, source_target_pairs={{0,2},{1,3},{2,0},{3,1},{4,6},{5,7},{6,4},{7,5},{8,10},{9,11},{10,... | collective-permute-start | bytes 1228808 | tf_op jit(solution)/shard_map/second/ppermute | solution.py:41
  67.2 9.9 %collective-permute-start.8 = (bf16[80,2560]{1,0:T(8,128)(2,1)S(1)}, bf16[80,2560]{1,0:T(8,128)(2,1)S(1)}, u32[]{:S(2)}, u32[]{:S(2)}) collective-permute-start(bf16[80,2560]{1,0:T(8,128)(2,1)S(1)} %get-tuple-element.52), channel_id=1, source_target_pairs={{0,1},{1,0},{2,3},{3,2},{4,5},{5,4},{6,7},{7,6},{8,9},{9,8},{10,11... | collective-permute-start | bytes 1228808 | tf_op jit(solution)/shard_map/second/ppermute | solution.py:46
  67.2 19.8 %collective-permute-start.10 = (bf16[160,2560]{1,0:T(8,128)(2,1)}, bf16[160,2560]{1,0:T(8,128)(2,1)S(1)}, u32[]{:S(2)}, u32[]{:S(2)}) collective-permute-start(bf16[160,2560]{1,0:T(8,128)(2,1)} %collective-permute-done.6.refs_4_.refs_8_), channel_id=1, source_target_pairs={{0,8},{1,9},{2,10},{3,11},{4,12},{5,13},{6,14},{7,15},{8,16},{9,17... | collective-permute-start | bytes 2457608 | tf_op jit(solution)/shard_map/second/ppermute | solution.py:31
  67.2 19.8 %collective-permute-start.12 = (bf16[160,2560]{1,0:T(8,128)(2,1)S(1)}, bf16[160,2560]{1,0:T(8,128)(2,1)S(1)}, u32[]{:S(2)}, u32[]{:S(2)}) collective-permute-start(bf16[160,2560]{1,0:T(8,128)(2,1)S(1)} %collective-permute-done.5.refs_3_.refs_7_), channel_id=1, source_target_pairs={{0,6},{1,7},{2,4},{3,5},{4,2},{5,3},{6,0},{7,1},{8,14},{9,15},{10,... | collective-permute-start | bytes 2457608 | tf_op jit(solution)/shard_map/second/ppermute | solution.py:36
  68.1 19.3 %collective-permute-start.11 = (bf16[160,2560]{1,0:T(8,128)(2,1)S(1)}, bf16[160,2560]{1,0:T(8,128)(2,1)S(1)}, u32[]{:S(2)}, u32[]{:S(2)}) collective-permute-start(bf16[160,2560]{1,0:T(8,128)(2,1)S(1)} %collective-permute-done.5.refs_3_.refs_7_), channel_id=1, source_target_pairs={{0,24},{1,25},{2,26},{3,27},{4,28},{5,29},{6,30},{7,31},{8,0},{9,1... | collective-permute-start | bytes 2457608 | tf_op jit(solution)/shard_map/second/ppermute | solution.py:31
  82.0 1.8 collective-permute-start.9
  88.2 21.6 %collective-permute-start.13 = (bf16[64,2560]{1,0:T(8,128)(2,1)S(1)}, bf16[64,2560]{1,0:T(8,128)(2,1)S(1)}, u32[]{:S(2)}, u32[]{:S(2)}) collective-permute-start(bf16[64,2560]{1,0:T(8,128)(2,1)S(1)} %get-tuple-element.59), channel_id=1, source_target_pairs={{0,6},{1,7},{2,4},{3,5},{4,2},{5,3},{6,0},{7,1},{8,14},{9,15},{10,... | collective-permute-start | bytes 983048 | tf_op jit(solution)/shard_map/third/ppermute | solution.py:36
  90.5 19.3 %collective-permute-start.14 = (bf16[48,2560]{1,0:T(8,128)(2,1)S(1)}, bf16[48,2560]{1,0:T(8,128)(2,1)S(1)}, u32[]{:S(2)}, u32[]{:S(2)}) collective-permute-start(bf16[48,2560]{1,0:T(8,128)(2,1)S(1)} %get-tuple-element.60), channel_id=1, source_target_pairs={{0,8},{1,9},{2,10},{3,11},{4,12},{5,13},{6,14},{7,15},{8,16},{9,17... | collective-permute-start | bytes 737288 | tf_op jit(solution)/shard_map/third/ppermute | solution.py:31
  90.5 19.3 %collective-permute-start.15 = (bf16[48,2560]{1,0:T(8,128)(2,1)S(1)}, bf16[48,2560]{1,0:T(8,128)(2,1)S(1)}, u32[]{:S(2)}, u32[]{:S(2)}) collective-permute-start(bf16[48,2560]{1,0:T(8,128)(2,1)S(1)} %get-tuple-element.61), channel_id=1, source_target_pairs={{0,24},{1,25},{2,26},{3,27},{4,28},{5,29},{6,30},{7,31},{8,0},{9,1... | collective-permute-start | bytes 737288 | tf_op jit(solution)/shard_map/third/ppermute | solution.py:31
  93.6 9.6 %collective-permute-start.16 = (bf16[80,640]{1,0:T(8,128)(2,1)S(1)}, bf16[80,640]{1,0:T(8,128)(2,1)S(1)}, u32[]{:S(2)}, u32[]{:S(2)}) collective-permute-start(bf16[80,640]{1,0:T(8,128)(2,1)S(1)} %get-tuple-element.62), channel_id=1, source_target_pairs={{0,64},{32,96},{64,128},{96,160},{128,192},{160,224},{192,0},{224,... | collective-permute-start | bytes 307208 | tf_op jit(solution)/shard_map/shares/ppermute | solution.py:54
  101.2 8.6 %collective-permute-start.17 = (bf16[80,640]{1,0:T(8,128)(2,1)S(1)}, bf16[80,640]{1,0:T(8,128)(2,1)S(1)}, u32[]{:S(2)}, u32[]{:S(2)}) collective-permute-start(bf16[80,640]{1,0:T(8,128)(2,1)S(1)} %get-tuple-element.63), channel_id=1, source_target_pairs={{0,128},{32,160},{64,192},{96,224},{128,0},{160,32},{192,64},{224,... | collective-permute-start | bytes 307208 | tf_op jit(solution)/shard_map/shares/ppermute | solution.py:54
  103.2 6.6 %collective-permute-start.18 = (bf16[80,640]{1,0:T(8,128)(2,1)S(1)}, bf16[80,640]{1,0:T(8,128)(2,1)S(1)}, u32[]{:S(2)}, u32[]{:S(2)}) collective-permute-start(bf16[80,640]{1,0:T(8,128)(2,1)S(1)} %get-tuple-element.64), channel_id=1, source_target_pairs={{0,192},{32,224},{64,0},{96,32},{128,64},{160,96},{192,128},{224,1... | collective-permute-start | bytes 307208 | tf_op jit(solution)/shard_map/shares/ppermute | solution.py:54
  109.8 19.1 %copy-start = (f32[1000]{0:T(1024)S(1)}, f32[1000]{0:T(1024)}, u32[]{:S(2)}) copy-start(f32[1000]{0:T(1024)} %occ.1) | copy-start | bytes 12004
  109.8 19.0 %copy-start.1 = (s32[2]{0:T(128)S(1)}, s32[2]{0:T(128)}, u32[]{:S(2)}) copy-start(s32[2]{0:T(128)} %chosen.1) | copy-start | bytes 28
  111.4 6.1 %collective-permute-start.19 = (bf16[320,640]{1,0:T(8,128)(2,1)S(1)}, bf16[320,640]{1,0:T(8,128)(2,1)S(1)}, u32[]{:S(2)}, u32[]{:S(2)}) collective-permute-start(bf16[320,640]{1,0:T(8,128)(2,1)S(1)} %get-tuple-element.66), channel_id=1, source_target_pairs={{0,32},{32,0},{64,96},{96,64},{128,160},{160,128},{192,224},{224,1... | collective-permute-start | bytes 1228808 | tf_op jit(solution)/shard_map/core/ppermute | solution.py:50
  117.8 6.3 %collective-permute-start.20 = (bf16[80,640]{1,0:T(8,128)(2,1)S(1)}, bf16[80,640]{1,0:T(8,128)(2,1)S(1)}, u32[]{:S(2)}, u32[]{:S(2)}) collective-permute-start(bf16[80,640]{1,0:T(8,128)(2,1)S(1)} %get-tuple-element.68), channel_id=1, source_target_pairs={{0,64},{32,96},{64,128},{96,160},{128,192},{160,224},{192,0},{224,... | collective-permute-start | bytes 307208 | tf_op jit(solution)/shard_map/shares/ppermute | solution.py:54
  120.4 8.5 %collective-permute-start.21 = (bf16[80,640]{1,0:T(8,128)(2,1)S(1)}, bf16[80,640]{1,0:T(8,128)(2,1)S(1)}, u32[]{:S(2)}, u32[]{:S(2)}) collective-permute-start(bf16[80,640]{1,0:T(8,128)(2,1)S(1)} %get-tuple-element.69), channel_id=1, source_target_pairs={{0,128},{32,160},{64,192},{96,224},{128,0},{160,32},{192,64},{224,... | collective-permute-start | bytes 307208 | tf_op jit(solution)/shard_map/shares/ppermute | solution.py:54
  120.4 8.5 %collective-permute-start.22 = (bf16[80,640]{1,0:T(8,128)(2,1)S(1)}, bf16[80,640]{1,0:T(8,128)(2,1)S(1)}, u32[]{:S(2)}, u32[]{:S(2)}) collective-permute-start(bf16[80,640]{1,0:T(8,128)(2,1)S(1)} %get-tuple-element.70), channel_id=1, source_target_pairs={{0,192},{32,224},{64,0},{96,32},{128,64},{160,96},{192,128},{224,1... | collective-permute-start | bytes 307208 | tf_op jit(solution)/shard_map/shares/ppermute | solution.py:54
  130.7 10.2 %collective-permute-start.25 = (bf16[80,1280]{1,0:T(8,128)(2,1)S(1)}, bf16[80,1280]{1,0:T(8,128)(2,1)S(1)}, u32[]{:S(2)}, u32[]{:S(2)}) collective-permute-start(bf16[80,1280]{1,0:T(8,128)(2,1)S(1)} %amplitude.1.refs_0_), channel_id=1, source_target_pairs={{0,192},{32,224},{64,0},{96,32},{128,64},{160,96},{192,128},{224,1... | collective-permute-start | bytes 614408 | tf_op jit(solution)/shard_map/spread/ppermute | solution.py:54
  132.8 11.7 %collective-permute-start.24 = (bf16[80,1280]{1,0:T(8,128)(2,1)S(1)}, bf16[80,1280]{1,0:T(8,128)(2,1)S(1)}, u32[]{:S(2)}, u32[]{:S(2)}) collective-permute-start(bf16[80,1280]{1,0:T(8,128)(2,1)S(1)} %amplitude.1.refs_0_), channel_id=1, source_target_pairs={{0,128},{32,160},{64,192},{96,224},{128,0},{160,32},{192,64},{224,... | collective-permute-start | bytes 614408 | tf_op jit(solution)/shard_map/spread/ppermute | solution.py:54
  138.0 14.3 %collective-permute-start.23 = (bf16[80,1280]{1,0:T(8,128)(2,1)S(1)}, bf16[80,1280]{1,0:T(8,128)(2,1)S(1)}, u32[]{:S(2)}, u32[]{:S(2)}) collective-permute-start(bf16[80,1280]{1,0:T(8,128)(2,1)S(1)} %amplitude.1.refs_0_), channel_id=1, source_target_pairs={{0,64},{32,96},{64,128},{96,160},{128,192},{160,224},{192,0},{224,... | collective-permute-start | bytes 614408 | tf_op jit(solution)/shard_map/spread/ppermute | solution.py:54
  152.4 2.8 %collective-permute-start.26 = (bf16[320,1280]{1,0:T(8,128)(2,1)S(1)}, bf16[320,1280]{1,0:T(8,128)(2,1)S(1)}, u32[]{:S(2)}, u32[]{:S(2)}) collective-permute-start(bf16[320,1280]{1,0:T(8,128)(2,1)S(1)} %pad_maximum_fusion), channel_id=1, source_target_pairs={{0,32},{32,0},{64,96},{96,64},{128,160},{160,128},{192,224},{224,1... | collective-permute-start | bytes 2457608 | tf_op jit(solution)/shard_map/other/ppermute | solution.py:50
  160.8 10.8 %collective-permute-start.27 = (bf16[80,2560]{1,0:T(8,128)(2,1)S(1)}, bf16[80,2560]{1,0:T(8,128)(2,1)S(1)}, u32[]{:S(2)}, u32[]{:S(2)}) collective-permute-start(bf16[80,2560]{1,0:T(8,128)(2,1)S(1)} %get-tuple-element.74), channel_id=1, source_target_pairs={{0,2},{1,3},{2,0},{3,1},{4,6},{5,7},{6,4},{7,5},{8,10},{9,11},{10,... | collective-permute-start | bytes 1228808 | tf_op jit(solution)/shard_map/out/ppermute | solution.py:41
  160.9 15.0 %collective-permute-start.28 = (bf16[80,2560]{1,0:T(8,128)(2,1)S(1)}, bf16[80,2560]{1,0:T(8,128)(2,1)S(1)}, u32[]{:S(2)}, u32[]{:S(2)}) collective-permute-start(bf16[80,2560]{1,0:T(8,128)(2,1)S(1)} %get-tuple-element.75), channel_id=1, source_target_pairs={{0,1},{1,0},{2,3},{3,2},{4,5},{5,4},{6,7},{7,6},{8,9},{9,8},{10,11... | collective-permute-start | bytes 1228808 | tf_op jit(solution)/shard_map/out/ppermute | solution.py:46
  166.6 15.5 %collective-permute-start.29 = (bf16[80,2560]{1,0:T(8,128)(2,1)S(1)}, bf16[80,2560]{1,0:T(8,128)(2,1)S(1)}, u32[]{:S(2)}, u32[]{:S(2)}) collective-permute-start(bf16[80,2560]{1,0:T(8,128)(2,1)S(1)} %get-tuple-element.77), channel_id=1, source_target_pairs={{0,2},{1,3},{2,0},{3,1},{4,6},{5,7},{6,4},{7,5},{8,10},{9,11},{10,... | collective-permute-start | bytes 1228808 | tf_op jit(solution)/shard_map/out/ppermute | solution.py:41
  167.9 16.8 %collective-permute-start.32 = (bf16[80,2560]{1,0:T(8,128)(2,1)S(1)}, bf16[80,2560]{1,0:T(8,128)(2,1)S(1)}, u32[]{:S(2)}, u32[]{:S(2)}) collective-permute-start(bf16[80,2560]{1,0:T(8,128)(2,1)S(1)} %get-tuple-element.80), channel_id=1, source_target_pairs={{0,1},{1,0},{2,3},{3,2},{4,5},{5,4},{6,7},{7,6},{8,9},{9,8},{10,11... | collective-permute-start | bytes 1228808 | tf_op jit(solution)/shard_map/out/ppermute | solution.py:46
  179.6 13.9 %collective-permute-start.30 = (bf16[80,2560]{1,0:T(8,128)(2,1)S(1)}, bf16[80,2560]{1,0:T(8,128)(2,1)S(1)}, u32[]{:S(2)}, u32[]{:S(2)}) collective-permute-start(bf16[80,2560]{1,0:T(8,128)(2,1)S(1)} %get-tuple-element.78), channel_id=1, source_target_pairs={{0,1},{1,0},{2,3},{3,2},{4,5},{5,4},{6,7},{7,6},{8,9},{9,8},{10,11... | collective-permute-start | bytes 1228808 | tf_op jit(solution)/shard_map/out/ppermute | solution.py:46
  180.9 12.6 %collective-permute-start.31 = (bf16[80,2560]{1,0:T(8,128)(2,1)S(1)}, bf16[80,2560]{1,0:T(8,128)(2,1)S(1)}, u32[]{:S(2)}, u32[]{:S(2)}) collective-permute-start(bf16[80,2560]{1,0:T(8,128)(2,1)S(1)} %get-tuple-element.79), channel_id=1, source_target_pairs={{0,2},{1,3},{2,0},{3,1},{4,6},{5,7},{6,4},{7,5},{8,10},{9,11},{10,... | collective-permute-start | bytes 1228808 | tf_op jit(solution)/shard_map/out/ppermute | solution.py:41

commit v5 on v4

--- a/solution.py
+++ b/solution.py
@@ -104,61 +104,49 @@
 EDGE = (0, 1, 8, 9)
 
 
-def fit_inner_kernel(index, own_in, tiles_in, a, b, own, edge, inner, own_sem, sems):
+def fit_inner_kernel(index, own_in, tiles_in, a, b, own, edge, tiles, weights, own_sem, sems):
     own_copies = [
         pltpu.make_async_copy(
             own_in.at[pl.ds(i * ROWS, ROWS)], own.at[pl.ds(i * ROWS, ROWS)], own_sem.at[i]
         )
         for i in range(2)
     ]
-    where = {p: inner.at[n] for n, p in enumerate(INNER)}
-    where |= {p: edge.at[n] for n, p in enumerate(EDGE)}
-    depth = BAND * TILE
-    copies = {
-        p: [
-            pltpu.make_async_copy(
-                tiles_in.at[pl.ds((2 * p + q) * depth, depth)],
-                where[p].at[pl.ds(q * TILE, depth), pl.ds(q * TILE, TILE)],
-                sems.at[p, q],
-            )
-            for q in range(2)
-        ]
-        for p in INNER + EDGE
-    }
-    order = INNER + EDGE
-    for c in copies[order[0]] + own_copies:
+    copies = {}
+    for p in INNER + EDGE:
+        part = pl.ds(p * 2 * BAND, 2 * BAND)
+        copies[p] = pltpu.make_async_copy(tiles_in.at[part], tiles.at[part], sems.at[p])
+    copies[INNER[0]].start()
+    for c in own_copies:
         c.start()
-    for p in order[1:]:
-        for c in copies[p]:
-            c.start()
+    for p in (INNER + EDGE)[1:]:
+        copies[p].start()
     zero = jnp.zeros((TILE, TILE), bf16)
-    for p in order:
-        where[p][:TILE, TILE:] = zero
-        where[p][depth:, :TILE] = zero
-
-    def ready(p):
-        for c in copies[p]:
-            c.wait()
+
+    def build(p, out):
+        out[:TILE, TILE:] = zero
+        out[BAND * TILE :, :TILE] = zero
         for q in range(2):
             for o in range(BAND):
+                slot = p * 2 * BAND + q * BAND + o
                 at = (q + o) * TILE
-
-                @pl.when(index[1, p * 2 * BAND + q * BAND + o] == 0)
-                def _():
-                    where[p][at : at + TILE, q * TILE : (q + 1) * TILE] = zero
-
-    for n, p in enumerate(INNER):
-        ready(p)
-        if n == 0:
+                out[at : at + TILE, q * TILE : (q + 1) * TILE] = jnp.where(
+                    index[1, slot] == 1, tiles[slot], zero
+                )
+
+    for p in INNER:
+        copies[p].wait()
+        if p == INNER[0]:
             for c in own_copies:
                 c.wait()
+        build(p, weights)
         window = own[:, (2 * p - HB) * TILE : (2 * p + HB + 2) * TILE]
-        fitted = jnp.dot(window, inner[n], preferred_element_type=f32).astype(bf16)
+        fitted = jnp.dot(window, weights[...], preferred_element_type=f32).astype(bf16)
         columns = slice(p * 2 * TILE, (p + 1) * 2 * TILE)
         a[:, columns] = fitted[:ROWS]
         b[:, columns] = fitted[ROWS:]
-    for p in EDGE:
-        ready(p)
+    for n, p in enumerate(EDGE):
+        copies[p].wait()
+        build(p, edge.at[n])
 
 
 def fit_edge_kernel(left, right, own, edge, _, __, a, b, ext):
@@ -179,9 +167,9 @@
     banded = ((BAND + 1) * TILE, 2 * TILE)
     a, b, own, edge = call(
         fit_inner_kernel,
-        [(index, SMEM), (own, ANY), (tiles.reshape(-1, TILE), ANY)],
+        [(index, SMEM), (own, ANY), (tiles, ANY)],
         [vmem((ROWS, AUX)), vmem((ROWS, AUX)), vmem((2 * ROWS, AUX)), vmem((4, *banded))],
-        [pltpu.VMEM((6, *banded), bf16), DMA((2,)), DMA((10, 2))],
+        [pltpu.VMEM(tiles.shape, bf16), pltpu.VMEM(banded, bf16), DMA((2,)), DMA((10,))],
         name="fit_inner",
         mib=56,
     )
@@ -195,14 +183,28 @@
     )
 
 
-def cut(parts, after=(), name=None, mib=40):
-    parts = [(*p, 0, AUX)[:5] for p in parts]
-
+def ends_kernel(own, last, first, sems):
+    copies = [
+        pltpu.make_async_copy(own.at[:, pl.ds(AUX - HALO, HALO)], last, sems.at[0]),
+        pltpu.make_async_copy(own.at[:, pl.ds(0, HALO)], first, sems.at[1]),
+    ]
+    for c in copies:
+        c.start()
+    for c in copies:
+        c.wait()
+
+
+def ends(own):
+    outs = [vmem((2 * ROWS, HALO))] * 2
+    return call(ends_kernel, [(own, ANY)], outs, [DMA((2,))], name="ends", mib=60)
+
+
+def cut(parts, after=(), name=None):
     def kernel(*refs):
         ins, outs, sems = refs[: len(parts)], refs[-1 - len(parts) : -1], refs[-1]
         copies = [
-            pltpu.make_async_copy(i.at[pl.ds(r, n), pl.ds(c, m)], o, sems.at[j])
-            for j, (i, o, (_, r, n, c, m)) in enumerate(zip(ins, outs, parts))
+            pltpu.make_async_copy(i.at[pl.ds(r, n)], o, sems.at[j])
+            for j, (i, o, (_, r, n)) in enumerate(zip(ins, outs, parts))
         ]
         for c in copies:
             c.start()
@@ -213,9 +215,9 @@
         kernel,
         in_specs=[ANY] * (len(parts) + len(after)),
         out_specs=[ANY] * len(parts),
-        out_shape=[hbm((n, m)) for _, _, n, _, m in parts],
+        out_shape=[hbm((n, AUX)) for _, _, n in parts],
         scratch_shapes=[DMA((len(parts),))],
-        compiler_params=params(mib),
+        compiler_params=params(),
         cost_estimate=cost(),
         name=name,
     )(*[p[0] for p in parts], *after)
@@ -421,9 +423,11 @@
     high, core = position()[:2]
     copies = []
     for k in range(4):
-        at = ((high - k + 4) % 4) * SHARE
-        here = pl.multiple_of(core * (2 * ROWS) + at, SHARE)
-        there = pl.multiple_of((1 - core) * (2 * ROWS) + at, SHARE)
+        share = (high - k + 4) % 4
+        of_0 = jnp.where(share < 2, share, 8 - 2 * share)
+        of_1 = jnp.where(share == 0, 3, share + 4)
+        here = pl.multiple_of(jnp.where(core == 0, of_0, of_1) * SHARE, SHARE)
+        there = pl.multiple_of(jnp.where(core == 0, of_1, of_0) * SHARE, SHARE)
         away = other.at[pl.ds(k * SHARE, SHARE)]
         copies += [
             pltpu.make_async_copy(mine[k], tcat.at[pl.ds(here, SHARE)], sems.at[k, 0]),
@@ -435,13 +439,9 @@
         c.wait()
     for half in range(2):
         columns = slice(half * K2, (half + 1) * K2)
-        value = product(tcat, b1, b2, slice(3 * ROWS, 4 * ROWS), half).astype(bf16)
-        d1[:, columns] = value[:HALF]
-        d2[:, columns] = value[HALF:]
-        rows = slice(ROWS, ROWS + HALF)
-        x1[:, columns] = product(tcat, b1, b2, rows, half).astype(bf16)
-        rows = slice(2 * ROWS + HALF, 3 * ROWS)
-        z2[:, columns] = product(tcat, b1, b2, rows, half).astype(bf16)
+        value = product(tcat, b1, b2, slice(2 * ROWS, 4 * ROWS), half).astype(bf16)
+        for i, out in enumerate((x1, z2, d1, d2)):
+            out[:, columns] = value[i * HALF : (i + 1) * HALF]
 
 
 def density_first(mine, other, b1, b2):
@@ -463,13 +463,15 @@
         c.start()
     for half in range(2):
         columns = slice(half * K2, (half + 1) * K2)
-        value = product(tcat, b1, b2, slice(ROWS + HALF, 2 * ROWS + HALF), half)
+        value = product(tcat, b1, b2, slice(0, 2 * ROWS), half)
         if half == 0:
             for c in copies:
                 c.wait()
-        x2[:, columns] = (value[:HALF] + got_z[:, columns].astype(f32)).astype(bf16)
-        z1[:, columns] = (value[HALF:] + got_x[:, columns].astype(f32)).astype(bf16)
-        own[:, columns] = product(tcat, b1, b2, slice(0, ROWS), half)
+        x = value[ROWS : ROWS + HALF] + got_z[:, columns].astype(f32)
+        z = value[ROWS + HALF :] + got_x[:, columns].astype(f32)
+        x2[:, columns] = x.astype(bf16)
+        z1[:, columns] = z.astype(bf16)
+        own[:, columns] = value[:ROWS]
 
 
 def density_second(tcat, b1, b2, from_x, from_z):
@@ -511,11 +513,7 @@
     vir = vir_energy.reshape(-1, ROWS)
     up = [(g, g + 1) for g in range(7)]
     down = [(g + 1, g) for g in range(7)]
-    last, first = cut(
-        [(window, 0, 2 * ROWS, AUX - HALO, HALO), (window, 0, 2 * ROWS, 0, HALO)],
-        name="cut_halo",
-        mib=60,
-    )
+    last, first = ends(window)
     left = lax.ppermute(last, "grp", up)
     right = lax.ppermute(first, "grp", down)
     a, b = fit(tile_index.T, window, tiles, left, right)
@@ -559,7 +557,7 @@
         c2 = send_y(c2, 1)
         c3 = send_y(c3, -1)
     early, b_second = pair_early(acat, (bom, b2, bop))
-    keep, send, b_second = pair_late(acat, early, b_second, (c1, c2, c3), arrived)
+    keep, send, b_second = pair_late(acat, early, b_second, (c1, c2, c3), arrived[1:2])
     own2, *s = core_total(keep, send)
     arrived += shares(s)
     mine = spread(amplitude(vir, occ_energy, pair_index, own, own2, arrived))

time: 196 us -> 174 us (0.89)
  Pallas kernels: 55 us -> 33.9 us
    pallas_call x3 -> x2, Pallas kernels: 22.9 us -> 1.9 us  [cut(): pl.pallas_call(kernel, in_specs=[ANY] * (len(parts) + len(after)), out_sp...]
    ppermute x5, waiting for transfers between devices: 27.2 us -> 20.1 us  [send_z(): return lax.ppermute(v, 'blk', pairs)]
    ppermute x5, waiting for transfers between devices: 9.58 us -> 15.3 us  [send_inner(): return lax.ppermute(v, 'blk', pairs)]
    ppermute x5, starting transfers between devices: 6.99 us -> 3.11 us  [send_z(): return lax.ppermute(v, 'blk', pairs)]
    ppermute x9, starting transfers between devices: 22.1 us -> 25.1 us  [send_high(): return lax.ppermute(v, 'grp', [(g, (g + 2 * step) % 8) for g in range(8)])]
    ppermute x9, waiting for transfers between devices: 24.5 us -> 26.5 us  [send_high(): return lax.ppermute(v, 'grp', [(g, (g + 2 * step) % 8) for g in range(8)])]
    pallas_call x11 -> x12, Pallas kernels: 32.1 us -> 32 us  [call(): pl.pallas_call(kernel, in_specs=[spec for _, spec in args], out_specs=[VM...]
  transfers between devices with their start and end apart: 33 -> 33, of which waited for: 23 -> 20; matrix products, arithmetic and copies ran while one was open for 0% -> 0% of each run, Pallas kernels for 10% -> 11%
where the time goes in v5:
time: 174 us
  waiting for transfers between devices  78.8 us (45%)
  starting transfers between devices  60.5 us (35%)
  Pallas kernels  33.9 us (19%)
    pallas_call x12, Pallas kernels, call(): pl.pallas_call(kernel, in_specs=[spec for _, spec in args], out_specs=[VM...  32 us
    ppermute x9, waiting for transfers between devices, send_high(): return lax.ppermute(v, 'grp', [(g, (g + 2 * step) % 8) for g in range(8)])  26.5 us
    ppermute x9, starting transfers between devices, send_high(): return lax.ppermute(v, 'grp', [(g, (g + 2 * step) % 8) for g in range(8)])  25.1 us
    ppermute x5, waiting for transfers between devices, send_z(): return lax.ppermute(v, 'blk', pairs)  20.1 us
    ppermute x5, waiting for transfers between devices, send_inner(): return lax.ppermute(v, 'blk', pairs)  15.3 us
    ppermute x6, starting transfers between devices, send_y(): return lax.ppermute(v, 'blk', pairs)  8.44 us
    ppermute x6, waiting for transfers between devices, send_y(): return lax.ppermute(v, 'blk', pairs)  8.09 us
    ppermute x3, starting transfers between devices, send_core(): return lax.ppermute(v, 'grp', [(g, g ^ 1) for g in range(8)])  6.45 us
  transfers between devices with their start and end apart: 33, of which 20 were waited for; matrix products, arithmetic and copies ran while one was open for 0% of the time, Pallas kernels for 11%

profile of v5, /device:TPU:1, one launch (start us, length us, event | category | flops | bytes accessed | tf_op | source)
XLA Modules:
  0.0 173.8 jit_solution(14847760841213409969)
XLA Ops:
  0.0 1.1 ends.1
  1.1 6.3 %collective-permute-start = (bf16[320,512]{1,0:T(8,128)(2,1)S(1)}, bf16[320,512]{1,0:T(8,128)(2,1)S(1)}, u32[]{:S(2)}, u32[]{:S(2)}) collective-permute-start(bf16[320,512]{1,0:T(8,128)(2,1)S(1)} %get-tuple-element.43), channel_id=1, source_target_pairs={{0,32},{32,64},{64,96},{96,128},{128,160},{160,192},{192,224},{1,3... | collective-permute-start | bytes 983048 | tf_op jit(solution)/shard_map/ppermute | solution.py:517
  7.4 1.9 %collective-permute-start.1 = (bf16[320,512]{1,0:T(8,128)(2,1)S(1)}, bf16[320,512]{1,0:T(8,128)(2,1)S(1)}, u32[]{:S(2)}, u32[]{:S(2)}) collective-permute-start(bf16[320,512]{1,0:T(8,128)(2,1)S(1)} %get-tuple-element.44), channel_id=1, source_target_pairs={{32,0},{64,32},{96,64},{128,96},{160,128},{192,160},{224,192},{33,... | collective-permute-start | bytes 983048 | tf_op jit(solution)/shard_map/ppermute | solution.py:518
  9.3 8.0 %fit_inner.1 = (bf16[160,2560]{1,0:T(8,128)(2,1)S(1)}, bf16[160,2560]{1,0:T(8,128)(2,1)S(1)}, bf16[320,2560]{1,0:T(8,128)(2,1)S(1)}, bf16[4,1280,256]{2,1,0:T(8,128)(2,1)S(1)}) custom-call(s32[2,180]{1,0:T(2,128)} %bitcast.4, bf16[320,2560]{1,0:T(8,128)(2,1)} %bitcast.3, bf16[180,128,128]{2,1,0:T(8,128)(2,1)} %tiles_in.1), custom_call_target="tpu_custom_call" | custom-call | flops 1000 | bytes 1000 | tf_op jit(solution)/shard_map/fit_inner/pallas_call | solution.py:90
  17.3 3.0 %collective-permute-done.1.right = bf16[320,512]{1,0:T(8,128)(2,1)S(1)} collective-permute-done((bf16[320,512]{1,0:T(8,128)(2,1)S(1)}, bf16[320,512]{1,0:T(8,128)(2,1)S(1)}, u32[]{:S(2)}, u32[]{:S(2)}) %collective-permute-start.1) | collective-permute-done | bytes 327712 | tf_op jit(solution)/shard_map/ppermute | solution.py:518
  21.4 1.3 collective-permute-start.2
  22.7 1.8 %collective-permute-start.6 = (bf16[160,2560]{1,0:T(8,128)(2,1)S(1)}, bf16[160,2560]{1,0:T(8,128)(2,1)}, u32[]{:S(2)}, u32[]{:S(2)}) collective-permute-start(bf16[160,2560]{1,0:T(8,128)(2,1)S(1)} %get-tuple-element.50.refs_5_), channel_id=1, source_target_pairs={{0,6},{1,7},{2,4},{3,5},{4,2},{5,3},{6,0},{7,1},{8,14},{9,15},{10,... | collective-permute-start | bytes 2457608 | tf_op jit(solution)/shard_map/first/ppermute | solution.py:36
  24.5 2.7 %collective-permute-start.5 = (bf16[160,2560]{1,0:T(8,128)(2,1)S(1)}, bf16[160,2560]{1,0:T(8,128)(2,1)S(1)}, u32[]{:S(2)}, u32[]{:S(2)}) collective-permute-start(bf16[160,2560]{1,0:T(8,128)(2,1)S(1)} %get-tuple-element.50.refs_5_), channel_id=1, source_target_pairs={{0,24},{1,25},{2,26},{3,27},{4,28},{5,29},{6,30},{7,31},{8,0},{9,1... | collective-permute-start | bytes 2457608 | tf_op jit(solution)/shard_map/first/ppermute | solution.py:31
  27.4 10.8 %collective-permute-done.3.refs_0_.refs_2_ = bf16[160,2560]{1,0:T(8,128)(2,1)} collective-permute-done((bf16[160,2560]{1,0:T(8,128)(2,1)S(1)}, bf16[160,2560]{1,0:T(8,128)(2,1)}, u32[]{:S(2)}, u32[]{:S(2)}) %collective-permute-start.3) | collective-permute-done | bytes 819232 | tf_op jit(solution)/shard_map/first/ppermute | solution.py:46
  38.2 2.1 %collective-permute-done.6.refs_4_.refs_8_ = bf16[160,2560]{1,0:T(8,128)(2,1)} collective-permute-done((bf16[160,2560]{1,0:T(8,128)(2,1)S(1)}, bf16[160,2560]{1,0:T(8,128)(2,1)}, u32[]{:S(2)}, u32[]{:S(2)}) %collective-permute-start.6) | collective-permute-done | bytes 819232 | tf_op jit(solution)/shard_map/first/ppermute | solution.py:36
  40.3 1.3 collective-permute-done.5.refs_3_.refs_7_
  41.6 3.5 %collective-permute-done.4.refs_2_.refs_6_ = bf16[160,2560]{1,0:T(8,128)(2,1)} collective-permute-done((bf16[160,2560]{1,0:T(8,128)(2,1)S(1)}, bf16[160,2560]{1,0:T(8,128)(2,1)}, u32[]{:S(2)}, u32[]{:S(2)}) %collective-permute-start.4) | collective-permute-done | bytes 819232 | tf_op jit(solution)/shard_map/first/ppermute | solution.py:31
  45.1 1.1 cut_a.1
  47.5 2.6 %collective-permute-start.11 = (bf16[160,2560]{1,0:T(8,128)(2,1)S(1)}, bf16[160,2560]{1,0:T(8,128)(2,1)S(1)}, u32[]{:S(2)}, u32[]{:S(2)}) collective-permute-start(bf16[160,2560]{1,0:T(8,128)(2,1)S(1)} %collective-permute-done.5.refs_3_.refs_7_), channel_id=1, source_target_pairs={{0,24},{1,25},{2,26},{3,27},{4,28},{5,29},{6,30},{7,31},{8,0},{9,1... | collective-permute-start | bytes 2457608 | tf_op jit(solution)/shard_map/second/ppermute | solution.py:31
  50.1 5.4 %collective-permute-done.7.refs_3_ = bf16[80,2560]{1,0:T(8,128)(2,1)S(1)} collective-permute-done((bf16[80,2560]{1,0:T(8,128)(2,1)S(1)}, bf16[80,2560]{1,0:T(8,128)(2,1)S(1)}, u32[]{:S(2)}, u32[]{:S(2)}) %collective-permute-start.7) | collective-permute-done | bytes 409632 | tf_op jit(solution)/shard_map/second/ppermute | solution.py:41
  56.0 4.8 %pair_first.1 = (f32[320,640]{1,0:T(8,128)S(1)}, bf16[320,640]{1,0:T(8,128)(2,1)S(1)}, bf16[640,2560]{1,0:T(8,128)(2,1)S(1)}, bf16[640,2560]{1,0:T(8,128)(2,1)S(1)}) custom-call(bf16[160,2560]{1,0:T(8,128)(2,1)S(1)} %get-tuple-element.49.refs_0_, bf16[160,2560]{1,0:T(8,128)(2,1)} %collective-permute-done.2.refs_1_, ...), custom_call_target="tpu_custom_call" | custom-call | flops 1000 | bytes 1000 | tf_op jit(solution)/shard_map/pair_first/pallas_call | solution.py:90
  60.9 1.7 collective-permute-done.9.got_in
  63.0 2.9 %collective-permute-done.10.refs_0_.refs_1_ = bf16[160,2560]{1,0:T(8,128)(2,1)S(1)} collective-permute-done((bf16[160,2560]{1,0:T(8,128)(2,1)}, bf16[160,2560]{1,0:T(8,128)(2,1)S(1)}, u32[]{:S(2)}, u32[]{:S(2)}) %collective-permute-start.10) | collective-permute-done | bytes 819232 | tf_op jit(solution)/shard_map/second/ppermute | solution.py:31
  67.1 2.3 %collective-permute-start.13 = (bf16[64,2560]{1,0:T(8,128)(2,1)S(1)}, bf16[64,2560]{1,0:T(8,128)(2,1)S(1)}, u32[]{:S(2)}, u32[]{:S(2)}) collective-permute-start(bf16[64,2560]{1,0:T(8,128)(2,1)S(1)} %get-tuple-element.59), channel_id=1, source_target_pairs={{0,6},{1,7},{2,4},{3,5},{4,2},{5,3},{6,0},{7,1},{8,14},{9,15},{10,... | collective-permute-start | bytes 983048 | tf_op jit(solution)/shard_map/third/ppermute | solution.py:36
  69.4 3.1 %collective-permute-start.15 = (bf16[48,2560]{1,0:T(8,128)(2,1)S(1)}, bf16[48,2560]{1,0:T(8,128)(2,1)S(1)}, u32[]{:S(2)}, u32[]{:S(2)}) collective-permute-start(bf16[48,2560]{1,0:T(8,128)(2,1)S(1)} %get-tuple-element.61), channel_id=1, source_target_pairs={{0,24},{1,25},{2,26},{3,27},{4,28},{5,29},{6,30},{7,31},{8,0},{9,1... | collective-permute-start | bytes 737288 | tf_op jit(solution)/shard_map/third/ppermute | solution.py:31
  72.5 7.2 %collective-permute-start.16 = (bf16[80,640]{1,0:T(8,128)(2,1)S(1)}, bf16[80,640]{1,0:T(8,128)(2,1)S(1)}, u32[]{:S(2)}, u32[]{:S(2)}) collective-permute-start(bf16[80,640]{1,0:T(8,128)(2,1)S(1)} %get-tuple-element.62), channel_id=1, source_target_pairs={{0,128},{32,160},{64,192},{96,224},{128,0},{160,32},{192,64},{224,... | collective-permute-start | bytes 307208 | tf_op jit(solution)/shard_map/shares/ppermute | solution.py:54
  79.7 2.3 %pair_early.1 = (f32[640,480]{1,0:T(8,128)S(1)}, bf16[640,2560]{1,0:T(8,128)(2,1)S(1)}) custom-call(bf16[640,2560]{1,0:T(8,128)(2,1)S(1)} %get-tuple-element.56.acat, bf16[160,2560]{1,0:T(8,128)(2,1)S(1)} %collective-permute-done.10.refs_0_.refs_1_, bf16[160,2560]{1,0:T(8,128)(2,1)S(1)} %collective-permute-done.11.refs_1_.refs_0_, ...), custom_call_target="tpu_custom_call" | custom-call | flops 1000 | bytes 1000 | tf_op jit(solution)/shard_map/pair_early/pallas_call | solution.py:90
  82.1 1.5 pair_late.1
  83.6 5.8 %collective-permute-start.17 = (bf16[320,640]{1,0:T(8,128)(2,1)S(1)}, bf16[320,640]{1,0:T(8,128)(2,1)S(1)}, u32[]{:S(2)}, u32[]{:S(2)}) collective-permute-start(bf16[320,640]{1,0:T(8,128)(2,1)S(1)} %get-tuple-element.64), channel_id=1, source_target_pairs={{0,32},{32,0},{64,96},{96,64},{128,160},{160,128},{192,224},{224,1... | collective-permute-start | bytes 1228808 | tf_op jit(solution)/shard_map/core/ppermute | solution.py:50
  89.4 2.5 %collective-permute-start.18 = (bf16[80,640]{1,0:T(8,128)(2,1)S(1)}, bf16[80,640]{1,0:T(8,128)(2,1)S(1)}, u32[]{:S(2)}, u32[]{:S(2)}) collective-permute-start(bf16[80,640]{1,0:T(8,128)(2,1)S(1)} %get-tuple-element.66), channel_id=1, source_target_pairs={{0,64},{32,96},{64,128},{96,160},{128,192},{160,224},{192,0},{224,... | collective-permute-start | bytes 307208 | tf_op jit(solution)/shard_map/shares/ppermute | solution.py:54
  91.8 1.1 collective-permute-start.19
  93.3 1.9 %collective-permute-start.20 = (bf16[80,640]{1,0:T(8,128)(2,1)S(1)}, bf16[80,640]{1,0:T(8,128)(2,1)S(1)}, u32[]{:S(2)}, u32[]{:S(2)}) collective-permute-start(bf16[80,640]{1,0:T(8,128)(2,1)S(1)} %get-tuple-element.68), channel_id=1, source_target_pairs={{0,64},{32,96},{64,128},{96,160},{128,192},{160,224},{192,0},{224,... | collective-permute-start | bytes 307208 | tf_op jit(solution)/shard_map/shares/ppermute | solution.py:54
  95.2 3.4 %collective-permute-start.21 = (bf16[80,640]{1,0:T(8,128)(2,1)S(1)}, bf16[80,640]{1,0:T(8,128)(2,1)S(1)}, u32[]{:S(2)}, u32[]{:S(2)}) collective-permute-start(bf16[80,640]{1,0:T(8,128)(2,1)S(1)} %get-tuple-element.69), channel_id=1, source_target_pairs={{0,128},{32,160},{64,192},{96,224},{128,0},{160,32},{192,64},{224,... | collective-permute-start | bytes 307208 | tf_op jit(solution)/shard_map/shares/ppermute | solution.py:54
  98.6 3.5 %collective-permute-start.22 = (bf16[80,640]{1,0:T(8,128)(2,1)S(1)}, bf16[80,640]{1,0:T(8,128)(2,1)S(1)}, u32[]{:S(2)}, u32[]{:S(2)}) collective-permute-start(bf16[80,640]{1,0:T(8,128)(2,1)S(1)} %get-tuple-element.70), channel_id=1, source_target_pairs={{0,192},{32,224},{64,0},{96,32},{128,64},{160,96},{192,128},{224,1... | collective-permute-start | bytes 307208 | tf_op jit(solution)/shard_map/shares/ppermute | solution.py:54
  102.9 3.6 %collective-permute-done.21.refs_4_ = bf16[80,640]{1,0:T(8,128)(2,1)S(1)} collective-permute-done((bf16[80,640]{1,0:T(8,128)(2,1)S(1)}, bf16[80,640]{1,0:T(8,128)(2,1)S(1)}, u32[]{:S(2)}, u32[]{:S(2)}) %collective-permute-start.21) | collective-permute-done | bytes 102432 | tf_op jit(solution)/shard_map/shares/ppermute | solution.py:54
  106.5 4.1 %collective-permute-done.22.refs_5_ = bf16[80,640]{1,0:T(8,128)(2,1)S(1)} collective-permute-done((bf16[80,640]{1,0:T(8,128)(2,1)S(1)}, bf16[80,640]{1,0:T(8,128)(2,1)S(1)}, u32[]{:S(2)}, u32[]{:S(2)}) %collective-permute-start.22) | collective-permute-done | bytes 102432 | tf_op jit(solution)/shard_map/shares/ppermute | solution.py:54
  110.6 1.8 %amplitude.1.refs_0_ = bf16[80,1280]{1,0:T(8,128)(2,1)S(1)} custom-call(f32[32,160]{1,0:T(8,128)S(1)} %reshape.6.refs_5_.vir, f32[1000]{0:T(1024)S(1)} %copy-done, s32[2]{0:T(128)S(1)} %copy-done.1, f32[80,640]{1,0:T(8,128)S(1)} %get-tuple-element.55.refs_3_.own1, f32[80,640]{1,0:T(8,128)S(1)} %get-tuple-element.65.own2, ...), custom_call_target="tpu_custom_call" | custom-call | flops 1000 | bytes 1000 | tf_op jit(solution)/shard_map/amplitude/pallas_call | solution.py:90
  112.4 2.0 %collective-permute-start.25 = (bf16[80,1280]{1,0:T(8,128)(2,1)S(1)}, bf16[80,1280]{1,0:T(8,128)(2,1)S(1)}, u32[]{:S(2)}, u32[]{:S(2)}) collective-permute-start(bf16[80,1280]{1,0:T(8,128)(2,1)S(1)} %amplitude.1.refs_0_), channel_id=1, source_target_pairs={{0,192},{32,224},{64,0},{96,32},{128,64},{160,96},{192,128},{224,1... | collective-permute-start | bytes 614408 | tf_op jit(solution)/shard_map/spread/ppermute | solution.py:54
  114.4 3.1 %collective-permute-start.24 = (bf16[80,1280]{1,0:T(8,128)(2,1)S(1)}, bf16[80,1280]{1,0:T(8,128)(2,1)S(1)}, u32[]{:S(2)}, u32[]{:S(2)}) collective-permute-start(bf16[80,1280]{1,0:T(8,128)(2,1)S(1)} %amplitude.1.refs_0_), channel_id=1, source_target_pairs={{0,128},{32,160},{64,192},{96,224},{128,0},{160,32},{192,64},{224,... | collective-permute-start | bytes 614408 | tf_op jit(solution)/shard_map/spread/ppermute | solution.py:54
  117.9 12.9 %collective-permute-done.25.refs_3_ = bf16[80,1280]{1,0:T(8,128)(2,1)S(1)} collective-permute-done((bf16[80,1280]{1,0:T(8,128)(2,1)S(1)}, bf16[80,1280]{1,0:T(8,128)(2,1)S(1)}, u32[]{:S(2)}, u32[]{:S(2)}) %collective-permute-start.25) | collective-permute-done | bytes 204832 | tf_op jit(solution)/shard_map/spread/ppermute | solution.py:54
  130.8 2.7 %collective-permute-done.24.refs_2_ = bf16[80,1280]{1,0:T(8,128)(2,1)S(1)} collective-permute-done((bf16[80,1280]{1,0:T(8,128)(2,1)S(1)}, bf16[80,1280]{1,0:T(8,128)(2,1)S(1)}, u32[]{:S(2)}, u32[]{:S(2)}) %collective-permute-start.24) | collective-permute-done | bytes 204832 | tf_op jit(solution)/shard_map/spread/ppermute | solution.py:54
  133.5 2.3 %collective-permute-done.23.refs_1_ = bf16[80,1280]{1,0:T(8,128)(2,1)S(1)} collective-permute-done((bf16[80,1280]{1,0:T(8,128)(2,1)S(1)}, bf16[80,1280]{1,0:T(8,128)(2,1)S(1)}, u32[]{:S(2)}, u32[]{:S(2)}) %collective-permute-start.23) | collective-permute-done | bytes 204832 | tf_op jit(solution)/shard_map/spread/ppermute | solution.py:54
  136.5 2.0 %collective-permute-done.26.refs_4_ = bf16[320,1280]{1,0:T(8,128)(2,1)S(1)} collective-permute-done((bf16[320,1280]{1,0:T(8,128)(2,1)S(1)}, bf16[320,1280]{1,0:T(8,128)(2,1)S(1)}, u32[]{:S(2)}, u32[]{:S(2)}) %collective-permute-start.26) | collective-permute-done | bytes 819232 | tf_op jit(solution)/shard_map/other/ppermute | solution.py:50
  138.4 4.9 %density_first.1 = (bf16[80,2560]{1,0:T(8,128)(2,1)S(1)}, bf16[80,2560]{1,0:T(8,128)(2,1)S(1)}, bf16[80,2560]{1,0:T(8,128)(2,1)S(1)}, bf16[80,2560]{1,0:T(8,128)(2,1)S(1)}, bf16[640,1280]{1,0:T(8,128)(2,1)S(1)}) custom-call(bf16[80,1280]{1,0:T(8,128)(2,1)S(1)} %amplitude.1.refs_0_, bf16[80,1280]{1,0:T(8,128)(2,1)S(1)} %collective-permute-done.23.refs_1_, ...), custom_call_target="tpu_custom_call" | custom-call | flops 1000 | bytes 1000 | tf_op jit(solution)/shard_map/density_first/pallas_call | solution.py:90
  143.4 1.5 collective-permute-start.28
  144.9 1.4 collective-permute-start.29
  146.3 7.7 %collective-permute-done.27.from_x = bf16[80,2560]{1,0:T(8,128)(2,1)S(1)} collective-permute-done((bf16[80,2560]{1,0:T(8,128)(2,1)S(1)}, bf16[80,2560]{1,0:T(8,128)(2,1)S(1)}, u32[]{:S(2)}, u32[]{:S(2)}) %collective-permute-start.27) | collective-permute-done | bytes 409632 | tf_op jit(solution)/shard_map/out/ppermute | solution.py:41
  154.1 3.9 %density_second.1 = (bf16[80,2560]{1,0:T(8,128)(2,1)S(1)}, bf16[80,2560]{1,0:T(8,128)(2,1)S(1)}, f32[160,2560]{1,0:T(8,128)S(1)}) custom-call(bf16[640,1280]{1,0:T(8,128)(2,1)S(1)} %get-tuple-element.73.tcat, bf16[640,2560]{1,0:T(8,128)(2,1)S(1)} %get-tuple-element.71.refs_5_.b1, bf16[640,2560]{1,0:T(8,128)(2,1)S(1)} %get-tuple-element.72.refs_6_.b2, ...), custom_call_target="tpu_custom_call" | custom-call | flops 1000 | bytes 1000 | tf_op jit(solution)/shard_map/density_second/pallas_call | solution.py:90
  158.0 1.5 collective-permute-start.30
  159.5 1.1 collective-permute-start.31
  160.6 2.2 %collective-permute-done.29.x1 = bf16[80,2560]{1,0:T(8,128)(2,1)S(1)} collective-permute-done((bf16[80,2560]{1,0:T(8,128)(2,1)S(1)}, bf16[80,2560]{1,0:T(8,128)(2,1)S(1)}, u32[]{:S(2)}, u32[]{:S(2)}) %collective-permute-start.29) | collective-permute-done | bytes 409632 | tf_op jit(solution)/shard_map/out/ppermute | solution.py:41
  162.9 8.7 %collective-permute-done.30.z1 = bf16[80,2560]{1,0:T(8,128)(2,1)S(1)} collective-permute-done((bf16[80,2560]{1,0:T(8,128)(2,1)S(1)}, bf16[80,2560]{1,0:T(8,128)(2,1)S(1)}, u32[]{:S(2)}, u32[]{:S(2)}) %collective-permute-start.30) | collective-permute-done | bytes 409632 | tf_op jit(solution)/shard_map/out/ppermute | solution.py:46
  171.6 2.0 %total.1 = bf16[160,2560]{1,0:T(8,128)(2,1)} custom-call(f32[160,2560]{1,0:T(8,128)S(1)} %get-tuple-element.76.own, bf16[80,2560]{1,0:T(8,128)(2,1)S(1)} %collective-permute-done.29.x1, bf16[80,2560]{1,0:T(8,128)(2,1)S(1)} %collective-permute-done.30.z1, bf16[80,2560]{1,0:T(8,128)(2,1)S(1)} %collective-permute-done.31.x2, ...), custom_call_target="tpu_custom_call" | custom-call | flops 1000 | bytes 1000 | tf_op jit(solution)/shard_map/total/pallas_call | solution.py:90
  (40 shorter events, 6.9 us)
Async XLA Ops:
  1.1 16.2 %collective-permute-start = (bf16[320,512]{1,0:T(8,128)(2,1)S(1)}, bf16[320,512]{1,0:T(8,128)(2,1)S(1)}, u32[]{:S(2)}, u32[]{:S(2)}) collective-permute-start(bf16[320,512]{1,0:T(8,128)(2,1)S(1)} %get-tuple-element.43), channel_id=1, source_target_pairs={{0,32},{32,64},{64,96},{96,128},{128,160},{160,192},{192,224},{1,3... | collective-permute-start | bytes 983048 | tf_op jit(solution)/shard_map/ppermute | solution.py:517
  7.4 12.9 %collective-permute-start.1 = (bf16[320,512]{1,0:T(8,128)(2,1)S(1)}, bf16[320,512]{1,0:T(8,128)(2,1)S(1)}, u32[]{:S(2)}, u32[]{:S(2)}) collective-permute-start(bf16[320,512]{1,0:T(8,128)(2,1)S(1)} %get-tuple-element.44), channel_id=1, source_target_pairs={{32,0},{64,32},{96,64},{128,96},{160,128},{192,160},{224,192},{33,... | collective-permute-start | bytes 983048 | tf_op jit(solution)/shard_map/ppermute | solution.py:518
  20.3 7.0 %copy-start.2 = (f32[5120]{0:T(1024)S(1)}, f32[5120]{0:T(1024)}, u32[]{:S(2)}) copy-start(f32[5120]{0:T(1024)} %param.9) | copy-start | bytes 61444
  21.3 16.8 %collective-permute-start.3 = (bf16[160,2560]{1,0:T(8,128)(2,1)S(1)}, bf16[160,2560]{1,0:T(8,128)(2,1)}, u32[]{:S(2)}, u32[]{:S(2)}) collective-permute-start(bf16[160,2560]{1,0:T(8,128)(2,1)S(1)} %get-tuple-element.49.refs_0_), channel_id=1, source_target_pairs={{0,1},{1,0},{2,3},{3,2},{4,5},{5,4},{6,7},{7,6},{8,9},{9,8},{10,11... | collective-permute-start | bytes 2457608 | tf_op jit(solution)/shard_map/first/ppermute | solution.py:46
  21.4 16.7 %collective-permute-start.2 = (bf16[160,2560]{1,0:T(8,128)(2,1)S(1)}, bf16[160,2560]{1,0:T(8,128)(2,1)}, u32[]{:S(2)}, u32[]{:S(2)}) collective-permute-start(bf16[160,2560]{1,0:T(8,128)(2,1)S(1)} %get-tuple-element.49.refs_0_), channel_id=1, source_target_pairs={{0,2},{1,3},{2,0},{3,1},{4,6},{5,7},{6,4},{7,5},{8,10},{9,11},{10,... | collective-permute-start | bytes 2457608 | tf_op jit(solution)/shard_map/first/ppermute | solution.py:41
  22.7 17.5 %collective-permute-start.6 = (bf16[160,2560]{1,0:T(8,128)(2,1)S(1)}, bf16[160,2560]{1,0:T(8,128)(2,1)}, u32[]{:S(2)}, u32[]{:S(2)}) collective-permute-start(bf16[160,2560]{1,0:T(8,128)(2,1)S(1)} %get-tuple-element.50.refs_5_), channel_id=1, source_target_pairs={{0,6},{1,7},{2,4},{3,5},{4,2},{5,3},{6,0},{7,1},{8,14},{9,15},{10,... | collective-permute-start | bytes 2457608 | tf_op jit(solution)/shard_map/first/ppermute | solution.py:36
  24.5 17.0 %collective-permute-start.5 = (bf16[160,2560]{1,0:T(8,128)(2,1)S(1)}, bf16[160,2560]{1,0:T(8,128)(2,1)S(1)}, u32[]{:S(2)}, u32[]{:S(2)}) collective-permute-start(bf16[160,2560]{1,0:T(8,128)(2,1)S(1)} %get-tuple-element.50.refs_5_), channel_id=1, source_target_pairs={{0,24},{1,25},{2,26},{3,27},{4,28},{5,29},{6,30},{7,31},{8,0},{9,1... | collective-permute-start | bytes 2457608 | tf_op jit(solution)/shard_map/first/ppermute | solution.py:31
  27.3 17.8 %collective-permute-start.4 = (bf16[160,2560]{1,0:T(8,128)(2,1)S(1)}, bf16[160,2560]{1,0:T(8,128)(2,1)}, u32[]{:S(2)}, u32[]{:S(2)}) collective-permute-start(bf16[160,2560]{1,0:T(8,128)(2,1)S(1)} %get-tuple-element.50.refs_5_), channel_id=1, source_target_pairs={{0,8},{1,9},{2,10},{3,11},{4,12},{5,13},{6,14},{7,15},{8,16},{9,17... | collective-permute-start | bytes 2457608 | tf_op jit(solution)/shard_map/first/ppermute | solution.py:31
  46.2 9.2 %collective-permute-start.7 = (bf16[80,2560]{1,0:T(8,128)(2,1)S(1)}, bf16[80,2560]{1,0:T(8,128)(2,1)S(1)}, u32[]{:S(2)}, u32[]{:S(2)}) collective-permute-start(bf16[80,2560]{1,0:T(8,128)(2,1)S(1)} %get-tuple-element.51), channel_id=1, source_target_pairs={{0,2},{1,3},{2,0},{3,1},{4,6},{5,7},{6,4},{7,5},{8,10},{9,11},{10,... | collective-permute-start | bytes 1228808 | tf_op jit(solution)/shard_map/second/ppermute | solution.py:41
  46.6 9.4 %collective-permute-start.8 = (bf16[80,2560]{1,0:T(8,128)(2,1)S(1)}, bf16[80,2560]{1,0:T(8,128)(2,1)S(1)}, u32[]{:S(2)}, u32[]{:S(2)}) collective-permute-start(bf16[80,2560]{1,0:T(8,128)(2,1)S(1)} %get-tuple-element.52), channel_id=1, source_target_pairs={{0,1},{1,0},{2,3},{3,2},{4,5},{5,4},{6,7},{7,6},{8,9},{9,8},{10,11... | collective-permute-start | bytes 1228808 | tf_op jit(solution)/shard_map/second/ppermute | solution.py:46
  46.6 19.3 %collective-permute-start.10 = (bf16[160,2560]{1,0:T(8,128)(2,1)}, bf16[160,2560]{1,0:T(8,128)(2,1)S(1)}, u32[]{:S(2)}, u32[]{:S(2)}) collective-permute-start(bf16[160,2560]{1,0:T(8,128)(2,1)} %collective-permute-done.6.refs_4_.refs_8_), channel_id=1, source_target_pairs={{0,8},{1,9},{2,10},{3,11},{4,12},{5,13},{6,14},{7,15},{8,16},{9,17... | collective-permute-start | bytes 2457608 | tf_op jit(solution)/shard_map/second/ppermute | solution.py:31
  46.6 19.3 %collective-permute-start.12 = (bf16[160,2560]{1,0:T(8,128)(2,1)S(1)}, bf16[160,2560]{1,0:T(8,128)(2,1)S(1)}, u32[]{:S(2)}, u32[]{:S(2)}) collective-permute-start(bf16[160,2560]{1,0:T(8,128)(2,1)S(1)} %collective-permute-done.5.refs_3_.refs_7_), channel_id=1, source_target_pairs={{0,6},{1,7},{2,4},{3,5},{4,2},{5,3},{6,0},{7,1},{8,14},{9,15},{10,... | collective-permute-start | bytes 2457608 | tf_op jit(solution)/shard_map/second/ppermute | solution.py:36
  47.5 18.8 %collective-permute-start.11 = (bf16[160,2560]{1,0:T(8,128)(2,1)S(1)}, bf16[160,2560]{1,0:T(8,128)(2,1)S(1)}, u32[]{:S(2)}, u32[]{:S(2)}) collective-permute-start(bf16[160,2560]{1,0:T(8,128)(2,1)S(1)} %collective-permute-done.5.refs_3_.refs_7_), channel_id=1, source_target_pairs={{0,24},{1,25},{2,26},{3,27},{4,28},{5,29},{6,30},{7,31},{8,0},{9,1... | collective-permute-start | bytes 2457608 | tf_op jit(solution)/shard_map/second/ppermute | solution.py:31
  60.8 1.8 %collective-permute-start.9 = (bf16[320,640]{1,0:T(8,128)(2,1)S(1)}, bf16[320,640]{1,0:T(8,128)(2,1)S(1)}, u32[]{:S(2)}, u32[]{:S(2)}) collective-permute-start(bf16[320,640]{1,0:T(8,128)(2,1)S(1)} %get-tuple-element.54), channel_id=1, source_target_pairs={{0,32},{32,0},{64,96},{96,64},{128,160},{160,128},{192,224},{224,1... | collective-permute-start | bytes 1228808 | tf_op jit(solution)/shard_map/core/ppermute | solution.py:50
  67.1 15.0 %collective-permute-start.13 = (bf16[64,2560]{1,0:T(8,128)(2,1)S(1)}, bf16[64,2560]{1,0:T(8,128)(2,1)S(1)}, u32[]{:S(2)}, u32[]{:S(2)}) collective-permute-start(bf16[64,2560]{1,0:T(8,128)(2,1)S(1)} %get-tuple-element.59), channel_id=1, source_target_pairs={{0,6},{1,7},{2,4},{3,5},{4,2},{5,3},{6,0},{7,1},{8,14},{9,15},{10,... | collective-permute-start | bytes 983048 | tf_op jit(solution)/shard_map/third/ppermute | solution.py:36
  69.4 12.6 %collective-permute-start.14 = (bf16[48,2560]{1,0:T(8,128)(2,1)S(1)}, bf16[48,2560]{1,0:T(8,128)(2,1)S(1)}, u32[]{:S(2)}, u32[]{:S(2)}) collective-permute-start(bf16[48,2560]{1,0:T(8,128)(2,1)S(1)} %get-tuple-element.60), channel_id=1, source_target_pairs={{0,8},{1,9},{2,10},{3,11},{4,12},{5,13},{6,14},{7,15},{8,16},{9,17... | collective-permute-start | bytes 737288 | tf_op jit(solution)/shard_map/third/ppermute | solution.py:31
  69.4 12.7 %collective-permute-start.15 = (bf16[48,2560]{1,0:T(8,128)(2,1)S(1)}, bf16[48,2560]{1,0:T(8,128)(2,1)S(1)}, u32[]{:S(2)}, u32[]{:S(2)}) collective-permute-start(bf16[48,2560]{1,0:T(8,128)(2,1)S(1)} %get-tuple-element.61), channel_id=1, source_target_pairs={{0,24},{1,25},{2,26},{3,27},{4,28},{5,29},{6,30},{7,31},{8,0},{9,1... | collective-permute-start | bytes 737288 | tf_op jit(solution)/shard_map/third/ppermute | solution.py:31
  72.5 9.5 %collective-permute-start.16 = (bf16[80,640]{1,0:T(8,128)(2,1)S(1)}, bf16[80,640]{1,0:T(8,128)(2,1)S(1)}, u32[]{:S(2)}, u32[]{:S(2)}) collective-permute-start(bf16[80,640]{1,0:T(8,128)(2,1)S(1)} %get-tuple-element.62), channel_id=1, source_target_pairs={{0,128},{32,160},{64,192},{96,224},{128,0},{160,32},{192,64},{224,... | collective-permute-start | bytes 307208 | tf_op jit(solution)/shard_map/shares/ppermute | solution.py:54
  82.0 28.6 %copy-start = (f32[1000]{0:T(1024)S(1)}, f32[1000]{0:T(1024)}, u32[]{:S(2)}) copy-start(f32[1000]{0:T(1024)} %occ.1) | copy-start | bytes 12004
  82.0 28.6 %copy-start.1 = (s32[2]{0:T(128)S(1)}, s32[2]{0:T(128)}, u32[]{:S(2)}) copy-start(s32[2]{0:T(128)} %chosen.1) | copy-start | bytes 28
  83.6 9.4 %collective-permute-start.17 = (bf16[320,640]{1,0:T(8,128)(2,1)S(1)}, bf16[320,640]{1,0:T(8,128)(2,1)S(1)}, u32[]{:S(2)}, u32[]{:S(2)}) collective-permute-start(bf16[320,640]{1,0:T(8,128)(2,1)S(1)} %get-tuple-element.64), channel_id=1, source_target_pairs={{0,32},{32,0},{64,96},{96,64},{128,160},{160,128},{192,224},{224,1... | collective-permute-start | bytes 1228808 | tf_op jit(solution)/shard_map/core/ppermute | solution.py:50
  89.4 12.7 %collective-permute-start.18 = (bf16[80,640]{1,0:T(8,128)(2,1)S(1)}, bf16[80,640]{1,0:T(8,128)(2,1)S(1)}, u32[]{:S(2)}, u32[]{:S(2)}) collective-permute-start(bf16[80,640]{1,0:T(8,128)(2,1)S(1)} %get-tuple-element.66), channel_id=1, source_target_pairs={{0,64},{32,96},{64,128},{96,160},{128,192},{160,224},{192,0},{224,... | collective-permute-start | bytes 307208 | tf_op jit(solution)/shard_map/shares/ppermute | solution.py:54
  91.8 10.3 %collective-permute-start.19 = (bf16[80,640]{1,0:T(8,128)(2,1)S(1)}, bf16[80,640]{1,0:T(8,128)(2,1)S(1)}, u32[]{:S(2)}, u32[]{:S(2)}) collective-permute-start(bf16[80,640]{1,0:T(8,128)(2,1)S(1)} %get-tuple-element.67), channel_id=1, source_target_pairs={{0,192},{32,224},{64,0},{96,32},{128,64},{160,96},{192,128},{224,1... | collective-permute-start | bytes 307208 | tf_op jit(solution)/shard_map/shares/ppermute | solution.py:54
  93.3 9.6 %collective-permute-start.20 = (bf16[80,640]{1,0:T(8,128)(2,1)S(1)}, bf16[80,640]{1,0:T(8,128)(2,1)S(1)}, u32[]{:S(2)}, u32[]{:S(2)}) collective-permute-start(bf16[80,640]{1,0:T(8,128)(2,1)S(1)} %get-tuple-element.68), channel_id=1, source_target_pairs={{0,64},{32,96},{64,128},{96,160},{128,192},{160,224},{192,0},{224,... | collective-permute-start | bytes 307208 | tf_op jit(solution)/shard_map/shares/ppermute | solution.py:54
  95.2 11.3 %collective-permute-start.21 = (bf16[80,640]{1,0:T(8,128)(2,1)S(1)}, bf16[80,640]{1,0:T(8,128)(2,1)S(1)}, u32[]{:S(2)}, u32[]{:S(2)}) collective-permute-start(bf16[80,640]{1,0:T(8,128)(2,1)S(1)} %get-tuple-element.69), channel_id=1, source_target_pairs={{0,128},{32,160},{64,192},{96,224},{128,0},{160,32},{192,64},{224,... | collective-permute-start | bytes 307208 | tf_op jit(solution)/shard_map/shares/ppermute | solution.py:54
  98.6 12.0 %collective-permute-start.22 = (bf16[80,640]{1,0:T(8,128)(2,1)S(1)}, bf16[80,640]{1,0:T(8,128)(2,1)S(1)}, u32[]{:S(2)}, u32[]{:S(2)}) collective-permute-start(bf16[80,640]{1,0:T(8,128)(2,1)S(1)} %get-tuple-element.70), channel_id=1, source_target_pairs={{0,192},{32,224},{64,0},{96,32},{128,64},{160,96},{192,128},{224,1... | collective-permute-start | bytes 307208 | tf_op jit(solution)/shard_map/shares/ppermute | solution.py:54
  112.4 18.4 %collective-permute-start.25 = (bf16[80,1280]{1,0:T(8,128)(2,1)S(1)}, bf16[80,1280]{1,0:T(8,128)(2,1)S(1)}, u32[]{:S(2)}, u32[]{:S(2)}) collective-permute-start(bf16[80,1280]{1,0:T(8,128)(2,1)S(1)} %amplitude.1.refs_0_), channel_id=1, source_target_pairs={{0,192},{32,224},{64,0},{96,32},{128,64},{160,96},{192,128},{224,1... | collective-permute-start | bytes 614408 | tf_op jit(solution)/shard_map/spread/ppermute | solution.py:54
  114.4 19.1 %collective-permute-start.24 = (bf16[80,1280]{1,0:T(8,128)(2,1)S(1)}, bf16[80,1280]{1,0:T(8,128)(2,1)S(1)}, u32[]{:S(2)}, u32[]{:S(2)}) collective-permute-start(bf16[80,1280]{1,0:T(8,128)(2,1)S(1)} %amplitude.1.refs_0_), channel_id=1, source_target_pairs={{0,128},{32,160},{64,192},{96,224},{128,0},{160,32},{192,64},{224,... | collective-permute-start | bytes 614408 | tf_op jit(solution)/shard_map/spread/ppermute | solution.py:54
  117.5 18.3 %collective-permute-start.23 = (bf16[80,1280]{1,0:T(8,128)(2,1)S(1)}, bf16[80,1280]{1,0:T(8,128)(2,1)S(1)}, u32[]{:S(2)}, u32[]{:S(2)}) collective-permute-start(bf16[80,1280]{1,0:T(8,128)(2,1)S(1)} %amplitude.1.refs_0_), channel_id=1, source_target_pairs={{0,64},{32,96},{64,128},{96,160},{128,192},{160,224},{192,0},{224,... | collective-permute-start | bytes 614408 | tf_op jit(solution)/shard_map/spread/ppermute | solution.py:54
  135.9 2.5 %collective-permute-start.26 = (bf16[320,1280]{1,0:T(8,128)(2,1)S(1)}, bf16[320,1280]{1,0:T(8,128)(2,1)S(1)}, u32[]{:S(2)}, u32[]{:S(2)}) collective-permute-start(bf16[320,1280]{1,0:T(8,128)(2,1)S(1)} %pad_maximum_fusion), channel_id=1, source_target_pairs={{0,32},{32,0},{64,96},{96,64},{128,160},{160,128},{192,224},{224,1... | collective-permute-start | bytes 2457608 | tf_op jit(solution)/shard_map/other/ppermute | solution.py:50
  143.3 10.8 %collective-permute-start.27 = (bf16[80,2560]{1,0:T(8,128)(2,1)S(1)}, bf16[80,2560]{1,0:T(8,128)(2,1)S(1)}, u32[]{:S(2)}, u32[]{:S(2)}) collective-permute-start(bf16[80,2560]{1,0:T(8,128)(2,1)S(1)} %get-tuple-element.74), channel_id=1, source_target_pairs={{0,2},{1,3},{2,0},{3,1},{4,6},{5,7},{6,4},{7,5},{8,10},{9,11},{10,... | collective-permute-start | bytes 1228808 | tf_op jit(solution)/shard_map/out/ppermute | solution.py:41
  143.4 10.7 %collective-permute-start.28 = (bf16[80,2560]{1,0:T(8,128)(2,1)S(1)}, bf16[80,2560]{1,0:T(8,128)(2,1)S(1)}, u32[]{:S(2)}, u32[]{:S(2)}) collective-permute-start(bf16[80,2560]{1,0:T(8,128)(2,1)S(1)} %get-tuple-element.75), channel_id=1, source_target_pairs={{0,1},{1,0},{2,3},{3,2},{4,5},{5,4},{6,7},{7,6},{8,9},{9,8},{10,11... | collective-permute-start | bytes 1228808 | tf_op jit(solution)/shard_map/out/ppermute | solution.py:46
  144.9 18.0 %collective-permute-start.29 = (bf16[80,2560]{1,0:T(8,128)(2,1)S(1)}, bf16[80,2560]{1,0:T(8,128)(2,1)S(1)}, u32[]{:S(2)}, u32[]{:S(2)}) collective-permute-start(bf16[80,2560]{1,0:T(8,128)(2,1)S(1)} %get-tuple-element.77), channel_id=1, source_target_pairs={{0,2},{1,3},{2,0},{3,1},{4,6},{5,7},{6,4},{7,5},{8,10},{9,11},{10,... | collective-permute-start | bytes 1228808 | tf_op jit(solution)/shard_map/out/ppermute | solution.py:41
  146.2 16.6 %collective-permute-start.32 = (bf16[80,2560]{1,0:T(8,128)(2,1)S(1)}, bf16[80,2560]{1,0:T(8,128)(2,1)S(1)}, u32[]{:S(2)}, u32[]{:S(2)}) collective-permute-start(bf16[80,2560]{1,0:T(8,128)(2,1)S(1)} %get-tuple-element.80), channel_id=1, source_target_pairs={{0,1},{1,0},{2,3},{3,2},{4,5},{5,4},{6,7},{7,6},{8,9},{9,8},{10,11... | collective-permute-start | bytes 1228808 | tf_op jit(solution)/shard_map/out/ppermute | solution.py:46
  158.0 13.6 %collective-permute-start.30 = (bf16[80,2560]{1,0:T(8,128)(2,1)S(1)}, bf16[80,2560]{1,0:T(8,128)(2,1)S(1)}, u32[]{:S(2)}, u32[]{:S(2)}) collective-permute-start(bf16[80,2560]{1,0:T(8,128)(2,1)S(1)} %get-tuple-element.78), channel_id=1, source_target_pairs={{0,1},{1,0},{2,3},{3,2},{4,5},{5,4},{6,7},{7,6},{8,9},{9,8},{10,11... | collective-permute-start | bytes 1228808 | tf_op jit(solution)/shard_map/out/ppermute | solution.py:46
  159.5 12.1 %collective-permute-start.31 = (bf16[80,2560]{1,0:T(8,128)(2,1)S(1)}, bf16[80,2560]{1,0:T(8,128)(2,1)S(1)}, u32[]{:S(2)}, u32[]{:S(2)}) collective-permute-start(bf16[80,2560]{1,0:T(8,128)(2,1)S(1)} %get-tuple-element.79), channel_id=1, source_target_pairs={{0,2},{1,3},{2,0},{3,1},{4,6},{5,7},{6,4},{7,5},{8,10},{9,11},{10,... | collective-permute-start | bytes 1228808 | tf_op jit(solution)/shard_map/out/ppermute | solution.py:41
